TPU v7x, 128 devices: a whole 4x4x4 slice. The times are simulated.
128 devices in a mesh: batch: 32 (over x, z, core), pass: 4 (over y).
Axes of the slice: x: 4, y: 4, z: 4, core: 2. Of those that a mesh axis runs over, the one named last changes fastest.
Arguments:
- embedded: bfloat16 [64, 128, 768], P('batch'), may hold values from -6 to 6
- cotangent: bfloat16 [4, 64, 128, 768], P('pass', 'batch'), may hold values from -6 to 6
- lengths: int32 [64], P('batch'), may hold values from 64 to 128, as said below
- starts: int32 [64], P('batch'), may hold values from 1 to 32, as said below
- ln1_gain: float32 [768], replicated, may hold values from 0.5 to 1.5
- ln1_shift: float32 [768], replicated, may hold values from -3 to 3
- w_qkv: bfloat16 [768, 2304], replicated, may hold values from -0.21875 to 0.21875
- b_qv: float32 [1536], replicated, may hold values from -3 to 3
- w_out: bfloat16 [768, 768], replicated, may hold values from -1.75 to 1.75
- b_out: float32 [768], replicated, may hold values from -3 to 3
- ln2_gain: float32 [768], replicated, may hold values from 0.5 to 1.5
- ln2_shift: float32 [768], replicated, may hold values from -3 to 3
- w_up: bfloat16 [768, 3072], replicated, may hold values from -0.21875 to 0.21875
- b_up: float32 [3072], replicated, may hold values from -3 to 3
- w_down: bfloat16 [3072, 768], replicated, may hold values from -0.109375 to 0.109375
- b_down: float32 [768], replicated, may hold values from -3 to 3
Outputs:
- activations: bfloat16 [4, 64, 128, 768], P('pass', 'batch')
- input_grad: bfloat16 [64, 128, 768], P('batch')
- grad_ln1_gain: float32 [768], replicated
- grad_ln1_shift: float32 [768], replicated
- grad_w_qkv: float32 [768, 2304], replicated
- grad_b_qv: float32 [1536], replicated
- grad_w_out: float32 [768, 768], replicated
- grad_b_out: float32 [768], replicated
- grad_ln2_gain: float32 [768], replicated
- grad_ln2_shift: float32 [768], replicated
- grad_w_up: float32 [768, 3072], replicated
- grad_b_up: float32 [3072], replicated
- grad_w_down: float32 [3072, 768], replicated
- grad_b_down: float32 [768], replicated
Inputs may be any that keep to these rules, and one draw needn't show every extreme that they name: `lengths`: each question has at least 64 true tokens; in every draw some question has exactly 128. The thought slots of a question are the 6 positions from its start on, all within its true length; in every draw some question starts at 32.
All inputs are finite; a program needn't handle non-finite values.
Results may differ from a plain program's by a relative error of at most 0.017.
Values may be sent and summed in bfloat16 or wider, within the bound.
A program may use at most 192 MiB of HBM per device.

v0:
```python
import jax
import jax.numpy as jnp
from jax import lax
from jax.sharding import PartitionSpec as P

HEADS = 12
THOUGHT_SLOTS = 6


epsilon = 1e-05


def from_behind(value, axis, by):
    length = lax.axis_size(axis)
    pairs = [(i, i + by) for i in range(length) if 0 <= i + by < length]
    return lax.ppermute(value, axis, pairs)


def layer_norm(field, gain, shift):
    row_mean = jnp.mean(field, -1, keepdims=True)
    centered = field - row_mean
    variance = jnp.mean(centered * centered, -1, keepdims=True)
    return centered * lax.rsqrt(variance + epsilon) * gain + shift


def gelu_tanh(field):
    return jax.nn.gelu(field, approximate=True)


def allowed_mask(lengths, row_count):
    token_position = jnp.arange(row_count, dtype=jnp.int32)
    causal = (token_position[:, None] >= token_position[None, :])[None, None]
    return causal & (token_position[None, None, None, :] < lengths[:, None, None, None])


def select_rows(field, first_row, slot_count):
    return jax.vmap(lambda single, begin: lax.dynamic_slice_in_dim(single, begin, slot_count, 0))(
        field, first_row
    )


def put_rows(field, new_rows, first_row):
    return jax.vmap(
        lambda single, block_rows, begin: lax.dynamic_update_slice_in_dim(
            single, block_rows, begin, 0
        )
    )(field, new_rows, first_row)


def forward_sweep(sent_rows):
    return from_behind(sent_rows, "pass", 1)


def backward_sweep(sent_rows):
    return from_behind(sent_rows, "pass", -1)


def forward(field, lengths, params):
    (
        ln1_gain,
        ln1_shift,
        w_qkv,
        b_qv,
        w_out,
        b_out,
        ln2_gain,
        ln2_shift,
        w_up,
        b_up,
        w_down,
        b_down,
    ) = params
    batch_size, row_count, embedding_width = field.shape
    head_size = embedding_width // HEADS
    scale_factor = head_size ** (-0.5)
    split_shape = (batch_size, row_count, HEADS, head_size)
    normed = layer_norm(field, ln1_gain, ln1_shift).astype(jnp.bfloat16)
    projected = jnp.einsum("bld,de->ble", normed, w_qkv, preferred_element_type=jnp.float32)
    queries = (
        (projected[..., :embedding_width] + b_qv[:embedding_width])
        .astype(jnp.bfloat16)
        .reshape(split_shape)
    )
    key_rows = (
        projected[..., embedding_width : 2 * embedding_width]
        .astype(jnp.bfloat16)
        .reshape(split_shape)
    )
    value_rows = (
        (projected[..., 2 * embedding_width :] + b_qv[embedding_width:])
        .astype(jnp.bfloat16)
        .reshape(split_shape)
    )
    scores = (
        jnp.einsum("bqhe,bkhe->bhqk", queries, key_rows, preferred_element_type=jnp.float32)
        * scale_factor
    )
    scores = jnp.where(allowed_mask(lengths, row_count), scores, -1e30)
    top_score = jnp.max(scores, -1, keepdims=True)
    log_total = top_score + jnp.log(jnp.sum(jnp.exp(scores - top_score), -1, keepdims=True))
    attn_probs = jnp.exp(scores - log_total).astype(jnp.bfloat16)
    mixed_heads = jnp.einsum(
        "bhqk,bkhe->bqhe", attn_probs, value_rows, preferred_element_type=jnp.float32
    )
    mixed_heads = mixed_heads.reshape(batch_size, row_count, embedding_width).astype(jnp.bfloat16)
    attn_out = (
        jnp.einsum("bld,de->ble", mixed_heads, w_out, preferred_element_type=jnp.float32) + b_out
    )
    residual = field + attn_out
    normed_two = layer_norm(residual, ln2_gain, ln2_shift).astype(jnp.bfloat16)
    hidden = jnp.einsum("bld,di->bli", normed_two, w_up, preferred_element_type=jnp.float32) + b_up
    active = gelu_tanh(hidden).astype(jnp.bfloat16)
    block_result = (
        residual
        + jnp.einsum("bli,id->bld", active, w_down, preferred_element_type=jnp.float32)
        + b_down
    )
    kept = (
        field,
        normed,
        queries,
        key_rows,
        value_rows,
        log_total,
        mixed_heads,
        residual,
        normed_two,
        hidden,
        active,
    )
    return (block_result, kept)


def backward(kept, grad_out, lengths, params):
    (
        ln1_gain,
        ln1_shift,
        w_qkv,
        b_qv,
        w_out,
        b_out,
        ln2_gain,
        ln2_shift,
        w_up,
        b_up,
        w_down,
        b_down,
    ) = params
    (
        field,
        normed,
        queries,
        key_rows,
        value_rows,
        log_total,
        mixed_heads,
        residual,
        normed_two,
        hidden,
        active,
    ) = kept
    batch_size, row_count, embedding_width = field.shape
    head_size = embedding_width // HEADS
    scale_factor = head_size ** (-0.5)
    split_shape = (batch_size, row_count, HEADS, head_size)
    grad_branch = grad_out.astype(jnp.bfloat16)
    grad_w_down = jnp.einsum("bli,bld->id", active, grad_branch, preferred_element_type=jnp.float32)
    grad_b_down = jnp.sum(grad_branch.astype(jnp.float32), (0, 1))
    grad_active = jnp.einsum("bld,id->bli", grad_branch, w_down, preferred_element_type=jnp.float32)
    gelu_value, gelu_pull = jax.vjp(gelu_tanh, hidden)
    grad_hidden = gelu_pull(grad_active)[0].astype(jnp.bfloat16)
    grad_w_up = jnp.einsum(
        "bld,bli->di", normed_two, grad_hidden, preferred_element_type=jnp.float32
    )
    grad_b_up = jnp.sum(grad_hidden.astype(jnp.float32), (0, 1))
    grad_normed_two = jnp.einsum(
        "bli,di->bld", grad_hidden, w_up, preferred_element_type=jnp.float32
    )
    norm_value, norm_pull = jax.vjp(layer_norm, residual, ln2_gain, ln2_shift)
    grad_res_part, grad_ln2_gain, grad_ln2_shift = norm_pull(grad_normed_two)
    grad_residual = grad_out + grad_res_part
    grad_attn = grad_residual.astype(jnp.bfloat16)
    grad_w_out = jnp.einsum(
        "bld,ble->de", mixed_heads, grad_attn, preferred_element_type=jnp.float32
    )
    grad_b_out = jnp.sum(grad_attn.astype(jnp.float32), (0, 1))
    grad_mixed = jnp.einsum("ble,de->bld", grad_attn, w_out, preferred_element_type=jnp.float32)
    grad_mixed = grad_mixed.astype(jnp.bfloat16).reshape(split_shape)
    scores = (
        jnp.einsum("bqhe,bkhe->bhqk", queries, key_rows, preferred_element_type=jnp.float32)
        * scale_factor
    )
    scores = jnp.where(allowed_mask(lengths, row_count), scores, -1e30)
    probs_full = jnp.exp(scores - log_total)
    probs_low = probs_full.astype(jnp.bfloat16)
    grad_values = jnp.einsum(
        "bhqk,bqhe->bkhe", probs_low, grad_mixed, preferred_element_type=jnp.float32
    )
    grad_probs = jnp.einsum(
        "bqhe,bkhe->bhqk", grad_mixed, value_rows, preferred_element_type=jnp.float32
    )
    grad_scores = probs_full * (grad_probs - jnp.sum(probs_full * grad_probs, -1, keepdims=True))
    grad_scores = grad_scores.astype(jnp.bfloat16)
    grad_queries = (
        jnp.einsum("bhqk,bkhe->bqhe", grad_scores, key_rows, preferred_element_type=jnp.float32)
        * scale_factor
    )
    grad_keys = (
        jnp.einsum("bhqk,bqhe->bkhe", grad_scores, queries, preferred_element_type=jnp.float32)
        * scale_factor
    )
    flat_shape = (batch_size, row_count, embedding_width)
    grad_qkv = jnp.concatenate(
        [
            grad_queries.reshape(flat_shape),
            grad_keys.reshape(flat_shape),
            grad_values.reshape(flat_shape),
        ],
        -1,
    ).astype(jnp.bfloat16)
    grad_w_qkv = jnp.einsum("bld,ble->de", normed, grad_qkv, preferred_element_type=jnp.float32)
    grad_bias_sums = jnp.sum(grad_qkv.astype(jnp.float32), (0, 1))
    grad_b_qv = jnp.concatenate(
        [grad_bias_sums[:embedding_width], grad_bias_sums[2 * embedding_width :]]
    )
    grad_normed = jnp.einsum("ble,de->bld", grad_qkv, w_qkv, preferred_element_type=jnp.float32)
    first_value, first_pull = jax.vjp(layer_norm, field, ln1_gain, ln1_shift)
    grad_field_part, grad_ln1_gain, grad_ln1_shift = first_pull(grad_normed)
    field_gradient = grad_residual + grad_field_part
    grads = (
        grad_ln1_gain,
        grad_ln1_shift,
        grad_w_qkv,
        grad_b_qv,
        grad_w_out,
        grad_b_out,
        grad_ln2_gain,
        grad_ln2_shift,
        grad_w_up,
        grad_b_up,
        grad_w_down,
        grad_b_down,
    )
    return (field_gradient, grads)


def kept_zeros(microbatch_count, row_count, embedding_width, hidden_width):
    head_size = embedding_width // HEADS
    flat_shape = (microbatch_count, row_count, embedding_width)
    split_shape = (microbatch_count, row_count, HEADS, head_size)
    return (
        jnp.zeros(flat_shape, jnp.float32),
        jnp.zeros(flat_shape, jnp.bfloat16),
        jnp.zeros(split_shape, jnp.bfloat16),
        jnp.zeros(split_shape, jnp.bfloat16),
        jnp.zeros(split_shape, jnp.bfloat16),
        jnp.zeros((microbatch_count, HEADS, row_count, 1), jnp.float32),
        jnp.zeros(flat_shape, jnp.bfloat16),
        jnp.zeros(flat_shape, jnp.float32),
        jnp.zeros(flat_shape, jnp.bfloat16),
        jnp.zeros((microbatch_count, row_count, hidden_width), jnp.float32),
        jnp.zeros((microbatch_count, row_count, hidden_width), jnp.bfloat16),
    )


def on_device(
    embedded,
    cotangent,
    lengths,
    starts,
    ln1_gain,
    ln1_shift,
    w_qkv,
    b_qv,
    w_out,
    b_out,
    ln2_gain,
    ln2_shift,
    w_up,
    b_up,
    w_down,
    b_down,
):
    params = (
        ln1_gain,
        ln1_shift,
        w_qkv,
        b_qv,
        w_out,
        b_out,
        ln2_gain,
        ln2_shift,
        w_up,
        b_up,
        w_down,
        b_down,
    )
    section_index = lax.axis_index("pass")
    sections = lax.axis_size("pass")
    not_first = section_index > 0
    base_field = embedded.astype(jnp.float32)
    base_cot = cotangent[0].astype(jnp.float32)
    microbatch_count, row_count, embedding_width = base_field.shape
    hidden_width = w_up.shape[1]
    round_count = sections + microbatch_count - 1

    def forward_turn(turn, loop_state):
        arriving_rows, pass_outs, kept_all = loop_state
        offset = turn - section_index
        in_range = (offset >= 0) & (offset < microbatch_count)
        item_index = jnp.clip(offset, 0, microbatch_count - 1)
        field_item = lax.dynamic_slice_in_dim(base_field, item_index, 1, 0)
        starting_entry = lax.dynamic_slice_in_dim(starts, item_index, 1, 0)
        length_item = lax.dynamic_slice_in_dim(lengths, item_index, 1, 0)
        slot_rows = lax.dynamic_slice_in_dim(arriving_rows, item_index, 1, 0).astype(jnp.float32)
        current = jnp.where(not_first, put_rows(field_item, slot_rows, starting_entry), field_item)
        block_result, kept = forward(current, length_item, params)
        pass_outs = jnp.where(
            in_range,
            lax.dynamic_update_slice_in_dim(pass_outs, block_result, item_index, 0),
            pass_outs,
        )
        kept_all = jax.tree.map(
            lambda whole_buf, piece: jnp.where(
                in_range,
                lax.dynamic_update_slice_in_dim(whole_buf, piece, item_index, 0),
                whole_buf,
            ),
            kept_all,
            kept,
        )
        gathered_rows = forward_sweep(
            select_rows(block_result, starting_entry - 1, THOUGHT_SLOTS).astype(jnp.bfloat16)
        )
        target = turn + 1 - section_index
        target_ok = (target >= 0) & (target < microbatch_count)
        target_index = jnp.clip(target, 0, microbatch_count - 1)
        arriving_rows = jnp.where(
            target_ok,
            lax.dynamic_update_slice_in_dim(arriving_rows, gathered_rows, target_index, 0),
            arriving_rows,
        )
        return (arriving_rows, pass_outs, kept_all)

    arriving_rows = jnp.zeros((microbatch_count, THOUGHT_SLOTS, embedding_width), jnp.bfloat16)
    state = (
        arriving_rows,
        jnp.zeros_like(base_field),
        kept_zeros(microbatch_count, row_count, embedding_width, hidden_width),
    )
    arriving_rows, activations, kept_all = lax.fori_loop(0, round_count, forward_turn, state)

    def backward_turn(turn, loop_state):
        returned, grad_fields, grad_totals = loop_state
        offset = turn - (sections - 1 - section_index)
        in_range = (offset >= 0) & (offset < microbatch_count)
        item_index = jnp.clip(offset, 0, microbatch_count - 1)
        kept = jax.tree.map(
            lambda whole_buf: lax.dynamic_slice_in_dim(whole_buf, item_index, 1, 0), kept_all
        )
        cot_item = lax.dynamic_slice_in_dim(base_cot, item_index, 1, 0)
        starting_entry = lax.dynamic_slice_in_dim(starts, item_index, 1, 0)
        length_item = lax.dynamic_slice_in_dim(lengths, item_index, 1, 0)
        back_rows = lax.dynamic_slice_in_dim(returned, item_index, 1, 0).astype(jnp.float32)
        grad_out = cot_item + put_rows(jnp.zeros_like(cot_item), back_rows, starting_entry - 1)
        field_gradient, grads = backward(kept, grad_out, length_item, params)
        grad_fields = jnp.where(
            in_range,
            lax.dynamic_update_slice_in_dim(grad_fields, field_gradient, item_index, 0),
            grad_fields,
        )
        grad_totals = jax.tree.map(
            lambda running, fresh: running + jnp.where(in_range, fresh, 0.0), grad_totals, grads
        )
        gathered_rows = backward_sweep(
            select_rows(field_gradient, starting_entry, THOUGHT_SLOTS).astype(jnp.bfloat16)
        )
        target = offset + 1
        target_ok = (target >= 0) & (target < microbatch_count)
        target_index = jnp.clip(target, 0, microbatch_count - 1)
        returned = jnp.where(
            target_ok,
            lax.dynamic_update_slice_in_dim(returned, gathered_rows, target_index, 0),
            returned,
        )
        return (returned, grad_fields, grad_totals)

    zero_grads = tuple((jnp.zeros(param.shape, jnp.float32) for param in params))
    state = (
        jnp.zeros((microbatch_count, THOUGHT_SLOTS, embedding_width), jnp.bfloat16),
        jnp.zeros_like(base_field),
        zero_grads,
    )
    returned, field_gradient, grads = lax.fori_loop(0, round_count, backward_turn, state)
    token_position = jnp.arange(row_count, dtype=jnp.int32)
    thought_mask = (
        (token_position[None, :] >= starts[:, None])
        & (token_position[None, :] < starts[:, None] + THOUGHT_SLOTS)
    )[:, :, None]
    own_grad = jnp.where(not_first & thought_mask, 0.0, field_gradient)
    input_grad = lax.psum(own_grad.astype(jnp.bfloat16), "pass")
    summed = lax.psum(grads, ("batch", "pass"))
    return (activations.astype(jnp.bfloat16)[None], input_grad) + tuple(summed)


def solution(mesh):
    in_specs = (
        P("batch", None, None),
        P("pass", "batch", None, None),
        P("batch"),
        P("batch"),
        P(),
        P(),
        P(),
        P(),
        P(),
        P(),
        P(),
        P(),
        P(),
        P(),
        P(),
        P(),
    )
    out_specs = (
        P("pass", "batch", None, None),
        P("batch", None, None),
        P(),
        P(),
        P(),
        P(),
        P(),
        P(),
        P(),
        P(),
        P(),
        P(),
        P(),
        P(),
    )
    return jax.shard_map(
        on_device, mesh=mesh, in_specs=in_specs, out_specs=out_specs, check_vma=False
    )
```

profile of v0, /device:TPU:1, one launch (start us, length us, event | category | flops | bytes accessed | tf_op | source)
XLA Modules:
  0.0 870.9 jit_solution(541642286619244721)
XLA Ops:
  22.0 193.0 %while.91 = (s32[]{:T(128)}, bf16[2,6,768]{2,1,0:T(8,128)(2,1)S(1)}, bf16[2,128,768]{2,1,0:T(8,128)(2,1)}, f32[2,128,768]{2,1,0:T(8,128)}, bf16[2,128,768]{2,1,0...) while((s32[]{:T(128)}, ...), condition=%wide.region_8.9_spmd, body=%wide.region_0.8_spmd.sunk | while | flops 1876576640 | bytes 113436816 | solution.py:351
  44.9 3.6 fusion.177
  50.7 4.6 collective-permute-start
  57.2 2.8 fusion.178
  85.1 3.6 fusion.177
  91.0 3.2 collective-permute-start
  96.1 2.8 fusion.178
  124.0 3.6 fusion.177
  129.9 2.9 collective-permute-start
  134.6 2.8 fusion.178
  162.6 3.6 fusion.177
  172.2 2.8 fusion.178
  192.6 2.7 convolution_bitcast_fusion.4
  200.2 3.6 fusion.177
  209.8 2.8 fusion.178
  215.0 328.5 %while.92 = (s32[]{:T(128)}, bf16[2,6,768]{2,1,0:T(8,128)(2,1)S(1)}, bf16[2,128,768]{2,1,0:T(8,128)(2,1)}, f32[768]{0:T(1024)}, f32[768]{0:T(1024)}, /*index=5*/...) while((s32[]{:T(128)}, ...), condition=%wide.region_28.29_spmd.clone, body=%wide.region_9.28_spmd.clone.sunk | while | flops 3792934144 | bytes 205010544 | solution.py:394
  230.2 4.9 convert_reduce_fusion.7
  243.6 3.5 fusion.208
  256.0 3.0 select_add_fusion.28
  259.0 4.1 select_add_fusion.27
  265.9 5.6 select_add_fusion.34
  283.9 2.7 and_reduce_fusion.5
  288.1 4.9 convert_reduce_fusion.7
  301.5 3.5 fusion.208
  313.8 3.8 select_add_fusion.28
  317.7 7.2 select_add_fusion.27
  327.7 12.3 %select_add_fusion.34 = f32[3072,768]{1,0:T(8,128)} fusion(f32[3072,768]{1,0:T(8,128)} %get-tuple-element.3318, pred[]{:T(512)S(6)} %compare.81, pred[]{:T(512)S(6)} %and.204, bf16[2,128,3072]{2,1,0:T(8,128)(2,1)S(1)} %copy-done.3, s32[]{:T(128)S(6)} %min.74, f32[1,128,768]{2,1,0:T(8,128)S(1)} %add.1179), kind=kOutput, calls=%fused_computation.63.clone.1 | convolution fusion | flops 611155968 | bytes 20054022 | tf_op jit(solution)/shard_map/while/body/eval_jaxpr/bli,bld->id/dot_general | solution.py:167
  351.5 2.7 and_reduce_fusion.5
  355.7 5.0 convert_reduce_fusion.7
  369.1 3.5 fusion.208
  381.4 3.8 select_add_fusion.28
  385.3 7.2 select_add_fusion.27
  395.3 12.3 %select_add_fusion.34 = f32[3072,768]{1,0:T(8,128)} fusion(f32[3072,768]{1,0:T(8,128)} %get-tuple-element.3318, pred[]{:T(512)S(6)} %compare.81, pred[]{:T(512)S(6)} %and.204, bf16[2,128,3072]{2,1,0:T(8,128)(2,1)S(1)} %copy-done.3, s32[]{:T(128)S(6)} %min.74, f32[1,128,768]{2,1,0:T(8,128)S(1)} %add.1179), kind=kOutput, calls=%fused_computation.63.clone.1 | convolution fusion | flops 611155968 | bytes 20054022 | tf_op jit(solution)/shard_map/while/body/eval_jaxpr/bli,bld->id/dot_general | solution.py:167
  423.3 5.0 convert_reduce_fusion.7
  436.7 3.5 fusion.208
  449.0 3.8 select_add_fusion.28
  452.9 7.2 select_add_fusion.27
  462.9 12.3 %select_add_fusion.34 = f32[3072,768]{1,0:T(8,128)} fusion(f32[3072,768]{1,0:T(8,128)} %get-tuple-element.3318, pred[]{:T(512)S(6)} %compare.81, pred[]{:T(512)S(6)} %and.204, bf16[2,128,3072]{2,1,0:T(8,128)(2,1)S(1)} %copy-done.3, s32[]{:T(128)S(6)} %min.74, f32[1,128,768]{2,1,0:T(8,128)S(1)} %add.1179), kind=kOutput, calls=%fused_computation.63.clone.1 | convolution fusion | flops 611155968 | bytes 20054022 | tf_op jit(solution)/shard_map/while/body/eval_jaxpr/bli,bld->id/dot_general | solution.py:167
  490.9 5.0 convert_reduce_fusion.7
  504.3 3.5 fusion.208
  516.7 3.8 select_add_fusion.28
  520.6 7.3 select_add_fusion.27
  530.6 12.3 %select_add_fusion.34 = f32[3072,768]{1,0:T(8,128)} fusion(f32[3072,768]{1,0:T(8,128)} %get-tuple-element.3318, pred[]{:T(512)S(6)} %compare.81, pred[]{:T(512)S(6)} %and.204, bf16[2,128,3072]{2,1,0:T(8,128)(2,1)S(1)} %copy-done.3, s32[]{:T(128)S(6)} %min.74, f32[1,128,768]{2,1,0:T(8,128)S(1)} %add.1179), kind=kOutput, calls=%fused_computation.63.clone.1 | convolution fusion | flops 611155968 | bytes 20054022 | tf_op jit(solution)/shard_map/while/body/eval_jaxpr/bli,bld->id/dot_general | solution.py:167
  546.3 73.1 %all-reduce = (f32[768]{0:T(1024)}, f32[768]{0:T(1024)}, f32[1536]{0:T(1024)}, f32[768]{0:T(1024)}, f32[768]{0:T(1024)}, /*index=5*/f32[768]{0:T(1024)}, f32[3072]{0:T(1024)}, f32[768]{0:T(1024)}) all-reduce(f32[768]{0:T(1024)S(1)} %copy-done.70, f32[768]{0:T(1024)S(1)} %copy-done.67, ...), channel_id=1, replica_groups=mesh['batch'=32,'pass'=4] {'batch','pass'}, use_global_device_ids=true, to_apply=%region_30.31 | all-reduce | flops 9216 | bytes 73728 | tf_op jit(solution)/shard_map/psum | solution.py:402
  619.4 224.3 %all-reduce.7.cloned.1.call-done = (f32[768,2304]{1,0:T(8,128)}, f32[768,768]{1,0:T(8,128)}, f32[768,3072]{1,0:T(8,128)}, f32[3072,768]{1,0:T(8,128)}) async-done(((f32[768,2304]{1,0:T(8,128)}, f32[768,768]{1,0:T(8,128)}, f32[768,3072]{1,0:T(8,128)}, f32[3072,768]{1,0:T(8,128)}), (f32[768,2304]{1,0:T(8,128)}, f32[768,768]{1,0:T(8,128)}, f32[768,3072]{1,0:T(8,128)}, ...) | async-done | bytes 28311568 | tf_op jit(solution)/shard_map/psum | solution.py:402
  845.6 6.7 copy.181
  853.7 4.8 copy.183
  860.3 3.7 copy.184
  (1279 shorter events, 299.3 us)
Async XLA Ops:
  7.2 612.2 %all-reduce.5.cloned.1.call-start = ((), (), s32[]{:S(2)}) async-start(), calls=%async_computation | async-start | bytes 786432 | tf_op jit(solution)/shard_map/psum | solution.py:401
  22.0 15.2 %copy-start.34 = (f32[2,128,768]{2,1,0:T(8,128)}, f32[2,128,768]{2,1,0:T(8,128)S(1)}, u32[]{:S(2)}) copy-start(f32[2,128,768]{2,1,0:T(8,128)S(1)} %get-tuple-element.3229) | copy-start | bytes 2359300 | tf_op jit(solution)/shard_map/while
  22.1 17.9 %copy-start.39 = (bf16[2,6,768]{2,1,0:T(8,128)(2,1)}, bf16[2,6,768]{2,1,0:T(8,128)(2,1)S(1)}, u32[]{:S(2)}) copy-start(bf16[2,6,768]{2,1,0:T(8,128)(2,1)S(1)} %get-tuple-element.3172) | copy-start | bytes 55300 | tf_op jit(solution)/shard_map/while
  50.7 10.8 %collective-permute-start = (bf16[1,6,768]{2,1,0:T(8,128)(2,1)}, bf16[1,6,768]{2,1,0:T(8,128)(2,1)}, u32[]{:S(2)}, u32[]{:S(2)}) collective-permute-start(bf16[1,6,768]{2,1,0:T(8,128)(2,1)} %dynamic-slice_convert_fusion.4), channel_id=1, source_target_pairs={{0,1},{1,2},{2,3},{4,5},{5,6},{6,7},{8,9},{9,10},{10,11},{12,13},{... | collective-permute-start | bytes 27656 | tf_op jit(solution)/shard_map/while/body/eval_jaxpr/ppermute | solution.py:16
  62.3 15.2 %copy-start.34 = (f32[2,128,768]{2,1,0:T(8,128)}, f32[2,128,768]{2,1,0:T(8,128)S(1)}, u32[]{:S(2)}) copy-start(f32[2,128,768]{2,1,0:T(8,128)S(1)} %get-tuple-element.3229) | copy-start | bytes 2359300 | tf_op jit(solution)/shard_map/while
  62.3 17.9 %copy-start.39 = (bf16[2,6,768]{2,1,0:T(8,128)(2,1)}, bf16[2,6,768]{2,1,0:T(8,128)(2,1)S(1)}, u32[]{:S(2)}) copy-start(bf16[2,6,768]{2,1,0:T(8,128)(2,1)S(1)} %get-tuple-element.3172) | copy-start | bytes 55300 | tf_op jit(solution)/shard_map/while
  91.0 9.4 %collective-permute-start = (bf16[1,6,768]{2,1,0:T(8,128)(2,1)}, bf16[1,6,768]{2,1,0:T(8,128)(2,1)}, u32[]{:S(2)}, u32[]{:S(2)}) collective-permute-start(bf16[1,6,768]{2,1,0:T(8,128)(2,1)} %dynamic-slice_convert_fusion.4), channel_id=1, source_target_pairs={{0,1},{1,2},{2,3},{4,5},{5,6},{6,7},{8,9},{9,10},{10,11},{12,13},{... | collective-permute-start | bytes 27656 | tf_op jit(solution)/shard_map/while/body/eval_jaxpr/ppermute | solution.py:16
  101.2 15.2 %copy-start.34 = (f32[2,128,768]{2,1,0:T(8,128)}, f32[2,128,768]{2,1,0:T(8,128)S(1)}, u32[]{:S(2)}) copy-start(f32[2,128,768]{2,1,0:T(8,128)S(1)} %get-tuple-element.3229) | copy-start | bytes 2359300 | tf_op jit(solution)/shard_map/while
  101.2 17.9 %copy-start.39 = (bf16[2,6,768]{2,1,0:T(8,128)(2,1)}, bf16[2,6,768]{2,1,0:T(8,128)(2,1)S(1)}, u32[]{:S(2)}) copy-start(bf16[2,6,768]{2,1,0:T(8,128)(2,1)S(1)} %get-tuple-element.3172) | copy-start | bytes 55300 | tf_op jit(solution)/shard_map/while
  129.9 9.1 %collective-permute-start = (bf16[1,6,768]{2,1,0:T(8,128)(2,1)}, bf16[1,6,768]{2,1,0:T(8,128)(2,1)}, u32[]{:S(2)}, u32[]{:S(2)}) collective-permute-start(bf16[1,6,768]{2,1,0:T(8,128)(2,1)} %dynamic-slice_convert_fusion.4), channel_id=1, source_target_pairs={{0,1},{1,2},{2,3},{4,5},{5,6},{6,7},{8,9},{9,10},{10,11},{12,13},{... | collective-permute-start | bytes 27656 | tf_op jit(solution)/shard_map/while/body/eval_jaxpr/ppermute | solution.py:16
  139.8 15.2 %copy-start.34 = (f32[2,128,768]{2,1,0:T(8,128)}, f32[2,128,768]{2,1,0:T(8,128)S(1)}, u32[]{:S(2)}) copy-start(f32[2,128,768]{2,1,0:T(8,128)S(1)} %get-tuple-element.3229) | copy-start | bytes 2359300 | tf_op jit(solution)/shard_map/while
  139.8 17.9 %copy-start.39 = (bf16[2,6,768]{2,1,0:T(8,128)(2,1)}, bf16[2,6,768]{2,1,0:T(8,128)(2,1)S(1)}, u32[]{:S(2)}) copy-start(bf16[2,6,768]{2,1,0:T(8,128)(2,1)S(1)} %get-tuple-element.3172) | copy-start | bytes 55300 | tf_op jit(solution)/shard_map/while
  168.4 8.1 collective-permute-start
  177.4 15.2 %copy-start.34 = (f32[2,128,768]{2,1,0:T(8,128)}, f32[2,128,768]{2,1,0:T(8,128)S(1)}, u32[]{:S(2)}) copy-start(f32[2,128,768]{2,1,0:T(8,128)S(1)} %get-tuple-element.3229) | copy-start | bytes 2359300 | tf_op jit(solution)/shard_map/while
  177.4 17.9 %copy-start.39 = (bf16[2,6,768]{2,1,0:T(8,128)(2,1)}, bf16[2,6,768]{2,1,0:T(8,128)(2,1)S(1)}, u32[]{:S(2)}) copy-start(bf16[2,6,768]{2,1,0:T(8,128)(2,1)S(1)} %get-tuple-element.3172) | copy-start | bytes 55300 | tf_op jit(solution)/shard_map/while
  206.1 8.1 collective-permute-start
  215.2 10.1 %copy-start.33 = (f32[2,128,768]{2,1,0:T(8,128)S(1)}, f32[2,128,768]{2,1,0:T(8,128)}, u32[]{:S(2)}) copy-start(f32[2,128,768]{2,1,0:T(8,128)} %get-tuple-element.3369) | copy-start | bytes 2359300 | tf_op jit(solution)/shard_map/while
  250.0 13.2 %slice-start.2 = ((s8[9437184]{0:T(1024)(128)(4,1)}), s8[1048576]{0:T(1024)(128)(4,1)S(1)}, s32[]{:S(2)}) async-start(s8[9437184]{0:T(1024)(128)(4,1)} %bitcast.313), calls=%async_computation.4 | async-start | bytes 2097152 | tf_op jit(solution)/shard_map/while
  252.0 20.5 %collective-permute-start.1 = (bf16[1,6,768]{2,1,0:T(8,128)(2,1)S(1)}, bf16[1,6,768]{2,1,0:T(8,128)(2,1)S(1)}, u32[]{:S(2)}, u32[]{:S(2)}) collective-permute-start(bf16[1,6,768]{2,1,0:T(8,128)(2,1)S(1)} %dynamic-slice_convert_fusion.5), channel_id=1, source_target_pairs={{1,0},{2,1},{3,2},{5,4},{6,5},{7,6},{9,8},{10,9},{11,10},{13,12},{... | collective-permute-start | bytes 27656 | tf_op jit(solution)/shard_map/while/body/eval_jaxpr/ppermute | solution.py:16
  273.1 10.1 %copy-start.33 = (f32[2,128,768]{2,1,0:T(8,128)S(1)}, f32[2,128,768]{2,1,0:T(8,128)}, u32[]{:S(2)}) copy-start(f32[2,128,768]{2,1,0:T(8,128)} %get-tuple-element.3369) | copy-start | bytes 2359300 | tf_op jit(solution)/shard_map/while
  307.8 17.2 %slice-start.2 = ((s8[9437184]{0:T(1024)(128)(4,1)}), s8[1048576]{0:T(1024)(128)(4,1)S(1)}, s32[]{:S(2)}) async-start(s8[9437184]{0:T(1024)(128)(4,1)} %bitcast.313), calls=%async_computation.4 | async-start | bytes 2097152 | tf_op jit(solution)/shard_map/while
  309.9 30.2 %collective-permute-start.1 = (bf16[1,6,768]{2,1,0:T(8,128)(2,1)S(1)}, bf16[1,6,768]{2,1,0:T(8,128)(2,1)S(1)}, u32[]{:S(2)}, u32[]{:S(2)}) collective-permute-start(bf16[1,6,768]{2,1,0:T(8,128)(2,1)S(1)} %dynamic-slice_convert_fusion.5), channel_id=1, source_target_pairs={{1,0},{2,1},{3,2},{5,4},{6,5},{7,6},{9,8},{10,9},{11,10},{13,12},{... | collective-permute-start | bytes 27656 | tf_op jit(solution)/shard_map/while/body/eval_jaxpr/ppermute | solution.py:16
  313.8 11.2 %slice-start.3 = ((s8[9437184]{0:T(1024)(128)(4,1)}), s8[4194304]{0:T(1024)(128)(4,1)S(1)}, s32[]{:S(2)}) async-start(s8[9437184]{0:T(1024)(128)(4,1)} %bitcast.313), calls=%async_computation.5 | async-start | bytes 8388608 | tf_op jit(solution)/shard_map/while
  327.7 12.3 %copy-start = (f32[768,3072]{1,0:T(8,128)}, f32[768,3072]{1,0:T(8,128)S(1)}, u32[]{:S(2)}) copy-start(f32[768,3072]{1,0:T(8,128)S(1)} %select_add_fusion.32) | copy-start | bytes 28311556 | tf_op jit(solution)/shard_map/while
  327.7 12.3 %copy-start.50 = (f32[1536]{0:T(1024)S(1)}, f32[1536]{0:T(1024)}, u32[]{:S(2)}) copy-start(f32[1536]{0:T(1024)} %get-tuple-element.3311) | copy-start | bytes 18436 | tf_op jit(solution)/shard_map/while
  327.7 12.3 %copy-start.65 = (f32[768]{0:T(1024)S(1)}, f32[768]{0:T(1024)}, u32[]{:S(2)}) copy-start(f32[768]{0:T(1024)} %get-tuple-element.3309) | copy-start | bytes 9220 | tf_op jit(solution)/shard_map/while
  340.7 10.1 %copy-start.33 = (f32[2,128,768]{2,1,0:T(8,128)S(1)}, f32[2,128,768]{2,1,0:T(8,128)}, u32[]{:S(2)}) copy-start(f32[2,128,768]{2,1,0:T(8,128)} %get-tuple-element.3369) | copy-start | bytes 2359300 | tf_op jit(solution)/shard_map/while
  375.4 17.2 %slice-start.2 = ((s8[9437184]{0:T(1024)(128)(4,1)}), s8[1048576]{0:T(1024)(128)(4,1)S(1)}, s32[]{:S(2)}) async-start(s8[9437184]{0:T(1024)(128)(4,1)} %bitcast.313), calls=%async_computation.4 | async-start | bytes 2097152 | tf_op jit(solution)/shard_map/while
  377.5 30.2 %collective-permute-start.1 = (bf16[1,6,768]{2,1,0:T(8,128)(2,1)S(1)}, bf16[1,6,768]{2,1,0:T(8,128)(2,1)S(1)}, u32[]{:S(2)}, u32[]{:S(2)}) collective-permute-start(bf16[1,6,768]{2,1,0:T(8,128)(2,1)S(1)} %dynamic-slice_convert_fusion.5), channel_id=1, source_target_pairs={{1,0},{2,1},{3,2},{5,4},{6,5},{7,6},{9,8},{10,9},{11,10},{13,12},{... | collective-permute-start | bytes 27656 | tf_op jit(solution)/shard_map/while/body/eval_jaxpr/ppermute | solution.py:16
  381.4 11.2 %slice-start.3 = ((s8[9437184]{0:T(1024)(128)(4,1)}), s8[4194304]{0:T(1024)(128)(4,1)S(1)}, s32[]{:S(2)}) async-start(s8[9437184]{0:T(1024)(128)(4,1)} %bitcast.313), calls=%async_computation.5 | async-start | bytes 8388608 | tf_op jit(solution)/shard_map/while
  395.3 12.3 %copy-start = (f32[768,3072]{1,0:T(8,128)}, f32[768,3072]{1,0:T(8,128)S(1)}, u32[]{:S(2)}) copy-start(f32[768,3072]{1,0:T(8,128)S(1)} %select_add_fusion.32) | copy-start | bytes 28311556 | tf_op jit(solution)/shard_map/while
  395.3 12.3 %copy-start.50 = (f32[1536]{0:T(1024)S(1)}, f32[1536]{0:T(1024)}, u32[]{:S(2)}) copy-start(f32[1536]{0:T(1024)} %get-tuple-element.3311) | copy-start | bytes 18436 | tf_op jit(solution)/shard_map/while
  395.3 12.3 %copy-start.65 = (f32[768]{0:T(1024)S(1)}, f32[768]{0:T(1024)}, u32[]{:S(2)}) copy-start(f32[768]{0:T(1024)} %get-tuple-element.3309) | copy-start | bytes 9220 | tf_op jit(solution)/shard_map/while
  408.3 10.1 %copy-start.33 = (f32[2,128,768]{2,1,0:T(8,128)S(1)}, f32[2,128,768]{2,1,0:T(8,128)}, u32[]{:S(2)}) copy-start(f32[2,128,768]{2,1,0:T(8,128)} %get-tuple-element.3369) | copy-start | bytes 2359300 | tf_op jit(solution)/shard_map/while
  443.0 17.2 %slice-start.2 = ((s8[9437184]{0:T(1024)(128)(4,1)}), s8[1048576]{0:T(1024)(128)(4,1)S(1)}, s32[]{:S(2)}) async-start(s8[9437184]{0:T(1024)(128)(4,1)} %bitcast.313), calls=%async_computation.4 | async-start | bytes 2097152 | tf_op jit(solution)/shard_map/while
  445.1 30.2 %collective-permute-start.1 = (bf16[1,6,768]{2,1,0:T(8,128)(2,1)S(1)}, bf16[1,6,768]{2,1,0:T(8,128)(2,1)S(1)}, u32[]{:S(2)}, u32[]{:S(2)}) collective-permute-start(bf16[1,6,768]{2,1,0:T(8,128)(2,1)S(1)} %dynamic-slice_convert_fusion.5), channel_id=1, source_target_pairs={{1,0},{2,1},{3,2},{5,4},{6,5},{7,6},{9,8},{10,9},{11,10},{13,12},{... | collective-permute-start | bytes 27656 | tf_op jit(solution)/shard_map/while/body/eval_jaxpr/ppermute | solution.py:16
  449.0 11.2 %slice-start.3 = ((s8[9437184]{0:T(1024)(128)(4,1)}), s8[4194304]{0:T(1024)(128)(4,1)S(1)}, s32[]{:S(2)}) async-start(s8[9437184]{0:T(1024)(128)(4,1)} %bitcast.313), calls=%async_computation.5 | async-start | bytes 8388608 | tf_op jit(solution)/shard_map/while
  462.9 12.3 %copy-start = (f32[768,3072]{1,0:T(8,128)}, f32[768,3072]{1,0:T(8,128)S(1)}, u32[]{:S(2)}) copy-start(f32[768,3072]{1,0:T(8,128)S(1)} %select_add_fusion.32) | copy-start | bytes 28311556 | tf_op jit(solution)/shard_map/while
  462.9 12.3 %copy-start.50 = (f32[1536]{0:T(1024)S(1)}, f32[1536]{0:T(1024)}, u32[]{:S(2)}) copy-start(f32[1536]{0:T(1024)} %get-tuple-element.3311) | copy-start | bytes 18436 | tf_op jit(solution)/shard_map/while
  462.9 12.3 %copy-start.65 = (f32[768]{0:T(1024)S(1)}, f32[768]{0:T(1024)}, u32[]{:S(2)}) copy-start(f32[768]{0:T(1024)} %get-tuple-element.3309) | copy-start | bytes 9220 | tf_op jit(solution)/shard_map/while
  475.9 10.1 %copy-start.33 = (f32[2,128,768]{2,1,0:T(8,128)S(1)}, f32[2,128,768]{2,1,0:T(8,128)}, u32[]{:S(2)}) copy-start(f32[2,128,768]{2,1,0:T(8,128)} %get-tuple-element.3369) | copy-start | bytes 2359300 | tf_op jit(solution)/shard_map/while
  510.6 17.2 %slice-start.2 = ((s8[9437184]{0:T(1024)(128)(4,1)}), s8[1048576]{0:T(1024)(128)(4,1)S(1)}, s32[]{:S(2)}) async-start(s8[9437184]{0:T(1024)(128)(4,1)} %bitcast.313), calls=%async_computation.4 | async-start | bytes 2097152 | tf_op jit(solution)/shard_map/while
  512.7 30.2 %collective-permute-start.1 = (bf16[1,6,768]{2,1,0:T(8,128)(2,1)S(1)}, bf16[1,6,768]{2,1,0:T(8,128)(2,1)S(1)}, u32[]{:S(2)}, u32[]{:S(2)}) collective-permute-start(bf16[1,6,768]{2,1,0:T(8,128)(2,1)S(1)} %dynamic-slice_convert_fusion.5), channel_id=1, source_target_pairs={{1,0},{2,1},{3,2},{5,4},{6,5},{7,6},{9,8},{10,9},{11,10},{13,12},{... | collective-permute-start | bytes 27656 | tf_op jit(solution)/shard_map/while/body/eval_jaxpr/ppermute | solution.py:16
  516.6 11.2 %slice-start.3 = ((s8[9437184]{0:T(1024)(128)(4,1)}), s8[4194304]{0:T(1024)(128)(4,1)S(1)}, s32[]{:S(2)}) async-start(s8[9437184]{0:T(1024)(128)(4,1)} %bitcast.313), calls=%async_computation.5 | async-start | bytes 8388608 | tf_op jit(solution)/shard_map/while
  530.5 12.3 %copy-start = (f32[768,3072]{1,0:T(8,128)}, f32[768,3072]{1,0:T(8,128)S(1)}, u32[]{:S(2)}) copy-start(f32[768,3072]{1,0:T(8,128)S(1)} %select_add_fusion.32) | copy-start | bytes 28311556 | tf_op jit(solution)/shard_map/while
  530.6 12.3 %copy-start.50 = (f32[1536]{0:T(1024)S(1)}, f32[1536]{0:T(1024)}, u32[]{:S(2)}) copy-start(f32[1536]{0:T(1024)} %get-tuple-element.3311) | copy-start | bytes 18436 | tf_op jit(solution)/shard_map/while
  530.6 12.3 %copy-start.65 = (f32[768]{0:T(1024)S(1)}, f32[768]{0:T(1024)}, u32[]{:S(2)}) copy-start(f32[768]{0:T(1024)} %get-tuple-element.3309) | copy-start | bytes 9220 | tf_op jit(solution)/shard_map/while
  545.4 298.3 %all-reduce.7.cloned.1.call-start = ((), (), s32[]{:S(2)}) async-start(), calls=%async_computation.1 | async-start | bytes 56623104 | tf_op jit(solution)/shard_map/psum | solution.py:402
  (351 other events, 1210.7 us)
Sparse Core Ops, SparseCore 0:
  545.5 47.9 all-reduce.4
  602.1 241.5 all-reduce.6
where the time goes:
time: 876 us; the launch traced here: 871 us
  matrix products  242 us (28%)
  waiting for transfers between devices  225 us (26%)
  other arithmetic  136 us (16%)
  local copies, waits for them, and re-layouts  113 us (13%)
  blocking collectives  73.1 us (8%)
  loops' own time  45.9 us (5%)
  starting transfers between devices  21.8 us (2%)
  between operations  14.3 us (2%)
    psum x1, waiting for transfers between devices, on_device(): summed = lax.psum(grads, ('batch', 'pass'))  224 us
    psum x1, blocking collectives, on_device(): summed = lax.psum(grads, ('batch', 'pass'))  73.1 us
    dot_general x5, matrix products, backward(): jnp.einsum('bli,bld->id', active, grad_branch, preferred_element_type=jnp...  54.8 us
    select_n x40, other arithmetic, forward_turn(): jnp.where(in_range, lax.dynamic_update_slice_in_dim(whole_buf, piece, ite...  33.6 us
    dot_general x5, matrix products, backward(): jnp.einsum('bld,ble->de', normed, grad_qkv, preferred_element_type=jnp.fl...  33.1 us
    another operation x10, other arithmetic  26.5 us
    dot_general x5, matrix products, backward(): jnp.einsum('bld,id->bli', grad_branch, w_down, preferred_element_type=jnp...  24.7 us
    another operation x1, loops' own time, on_device(): lax.fori_loop(0, round_count, backward_turn, state)  24.6 us
  transfers between devices with their start and end apart: 12, of which 1 were waited for; matrix products, arithmetic and copies ran while one was open for 17% of the time, Pallas kernels for 0%

commit v1 on v0

--- a/solution.py
+++ b/solution.py
@@ -1,6 +1,8 @@
 import jax
 import jax.numpy as jnp
 from jax import lax
+from jax.experimental import pallas as pl
+from jax.experimental.pallas import tpu as pltpu
 from jax.sharding import PartitionSpec as P
 
 HEADS = 12
@@ -263,6 +265,250 @@
     )
 
 
+MESH = pl.DeviceIdType.MESH
+BF, F32 = jnp.bfloat16, jnp.float32
+ORDERS = ((0, 1, 2), (1, 2, 0), (2, 0, 1))
+NMSG = 31
+
+def coords():
+    b = lax.axis_index("batch"); y = lax.axis_index("pass")
+    core = b % 2
+    z = (b // 2) % 4
+    x = b // 8
+    return (x, y, z), core
+
+def device(pos, core):
+    x, y, z = pos
+    return ((x * 4 + z) * 2 + core, y)
+
+def along(pos, axis, by):
+    return tuple((c + by) % 4 if i == axis else c for i, c in enumerate(pos))
+
+def comm_kernel(w_ref, out_ref, w_buf, relay1, in1, w2, relay2, in2, w3, in3, fin, lsem, ssem, rsem):
+    pos, core = coords()
+    barrier = pltpu.get_barrier_semaphore()
+    for axis in range(3):
+        for by in (1, 2, 3):
+            pl.semaphore_signal(barrier, inc=1, device_id=device(along(pos, axis, by), core), device_id_type=MESH)
+    pl.semaphore_signal(barrier, inc=1, device_id=device(pos, 1 - core), device_id_type=MESH)
+    ld = pltpu.make_async_copy(w_ref, w_buf, lsem)
+    ld.start()
+    pl.semaphore_wait(barrier, 10)
+    ld.wait()
+
+    def msg(p, m, src, dst, to):
+        return pltpu.make_async_remote_copy(src_ref=src, dst_ref=dst, send_sem=ssem.at[p, m], recv_sem=rsem.at[p, m], device_id=to, device_id_type=MESH)
+
+    sent = []
+    def send(p, m, src, dst, to):
+        c = msg(p, m, src, dst, to)
+        c.start()
+        sent.append(c)
+    def arrived(p, m, dst):
+        msg(p, m, dst, dst, device(pos, 1 - core)).wait_recv()
+
+    A = pl.ds(0, 768); B = pl.ds(768, 768)
+
+    def rs_a(p, phase):
+        axis = ORDERS[p][phase]; r = pos[axis]
+        w, relay, inn = ((w_buf, relay1, in1), (w2, relay2, in2))[phase]
+        b = 6 * phase
+        up = device(along(pos, axis, 1), core); dn = device(along(pos, axis, 3), core)
+        far = (r + 2) % 4; nx = (r + 1) % 4; pv = (r + 3) % 4
+        send(p, b + 0, w.at[p, far, :, A], relay.at[p, 0], up)
+        send(p, b + 1, w.at[p, far, :, B], relay.at[p, 1], dn)
+        send(p, b + 2, w.at[p, nx, :, B], inn.at[p, 0, :, B], up)
+        send(p, b + 3, w.at[p, pv, :, A], inn.at[p, 1, :, A], dn)
+
+    def rs_b(p, phase):
+        axis = ORDERS[p][phase]; r = pos[axis]
+        w, relay, inn = ((w_buf, relay1, in1), (w2, relay2, in2))[phase]
+        b = 6 * phase
+        up = device(along(pos, axis, 1), core); dn = device(along(pos, axis, 3), core)
+        nx = (r + 1) % 4; pv = (r + 3) % 4
+        rows = w.shape[2]
+        arrived(p, b + 0, relay.at[p, 0])
+        def add(i, _):
+            s = pl.ds(pl.multiple_of(i * 16, 16), 16)
+            relay[p, 0, s, :] = (relay[p, 0, s, :].astype(F32) + w[p, nx, s, A].astype(F32)).astype(BF)
+            return 0
+        lax.fori_loop(0, rows // 16, add, 0)
+        send(p, b + 4, relay.at[p, 0], inn.at[p, 0, :, A], up)
+        arrived(p, b + 1, relay.at[p, 1])
+        def add(i, _):
+            s = pl.ds(pl.multiple_of(i * 16, 16), 16)
+            relay[p, 1, s, :] = (relay[p, 1, s, :].astype(F32) + w[p, pv, s, B].astype(F32)).astype(BF)
+            return 0
+        lax.fori_loop(0, rows // 16, add, 0)
+        send(p, b + 5, relay.at[p, 1], inn.at[p, 1, :, B], dn)
+
+    def rs_c(p, phase):
+        axis = ORDERS[p][phase]; r = pos[axis]
+        w, relay, inn = ((w_buf, relay1, in1), (w2, relay2, in2))[phase]
+        b = 6 * phase
+        arrived(p, b + 2, inn.at[p, 0, :, B])
+        arrived(p, b + 3, inn.at[p, 1, :, A])
+        arrived(p, b + 4, inn.at[p, 0, :, A])
+        arrived(p, b + 5, inn.at[p, 1, :, B])
+        if phase == 0:
+            for k in range(4):
+                def add(i, _):
+                    s = pl.ds(pl.multiple_of(k * 48 + i * 16, 16), 16)
+                    t = pl.ds(pl.multiple_of(i * 16, 16), 16)
+                    w2[p, k, t, :] = (w[p, r, s, :].astype(F32) + inn[p, 0, s, :].astype(F32) + inn[p, 1, s, :].astype(F32)).astype(BF)
+                    return 0
+                lax.fori_loop(0, 3, add, 0)
+        else:
+            for k in range(4):
+                c = pl.ds(384 * k, 384)
+                w3[p, k] = (w[p, r, :, c].astype(F32) + inn[p, 0, :, c].astype(F32) + inn[p, 1, :, c].astype(F32)).astype(BF)
+
+    def rs3_a(p):
+        axis = ORDERS[p][2]; r = pos[axis]
+        for d in (1, 2, 3):
+            send(p, 11 + d, w3.at[p, (r + d) % 4], in3.at[p, d - 1], device(along(pos, axis, d), core))
+
+    def spot(p, c1, c2=None, c3=None, cols=None):
+        o = out_ref.at[core, p]
+        if c2 is None:
+            rows = pl.ds(pl.multiple_of(192 * c1, 16), 192)
+        else:
+            rows = pl.ds(pl.multiple_of(192 * c1 + 48 * c2, 16), 48)
+        if c3 is not None:
+            cols = pl.ds(pl.multiple_of(384 * c3, 128), 384)
+        if cols is None:
+            return o.at[rows]
+        return o.at[rows, cols]
+
+    def rs3_b(p):
+        axis = ORDERS[p][2]; r = pos[axis]
+        for d in (1, 2, 3):
+            arrived(p, 11 + d, in3.at[p, d - 1])
+        fin[p] = (w3[p, r].astype(F32) + in3[p, 0].astype(F32) + in3[p, 1].astype(F32) + in3[p, 2].astype(F32)).astype(BF)
+        c1, c2, c3 = (pos[a] for a in ORDERS[p])
+        own = pltpu.make_async_copy(fin.at[p], spot(p, c1, c2, c3), lsem)
+        own.start()
+        for d in (1, 2, 3):
+            send(p, 14 + d, fin.at[p], spot(p, c1, c2, c3), device(along(pos, axis, d), core))
+        own.wait()
+
+    def ag3(p):
+        axis = ORDERS[p][2]
+        c1, c2, c3 = (pos[a] for a in ORDERS[p])
+        for d in (1, 2, 3):
+            arrived(p, 14 + d, spot(p, c1, c2, (c3 + 4 - d) % 4))
+
+    def ag_a(p, phase):
+        axis = ORDERS[p][phase]
+        c1, c2, _ = (pos[a] for a in ORDERS[p])
+        b = 18 if phase == 1 else 22
+        mine = spot(p, c1, c2) if phase == 1 else spot(p, c1)
+        up = device(along(pos, axis, 1), core); dn = device(along(pos, axis, 3), core)
+        send(p, b, mine, mine, up)
+        send(p, b + 1, mine, mine, dn)
+        if phase == 0:
+            send(p, 26, mine, mine, device(pos, 1 - core))
+
+    def ag_b(p, phase):
+        axis = ORDERS[p][phase]
+        c1, c2, _ = (pos[a] for a in ORDERS[p])
+        b = 18 if phase == 1 else 22
+        def sp(d, cols=None):
+            return spot(p, c1, (c2 + d) % 4, cols=cols) if phase == 1 else spot(p, (c1 + d) % 4, cols=cols)
+        up = device(along(pos, axis, 1), core); dn = device(along(pos, axis, 3), core)
+        arrived(p, b, sp(3))
+        send(p, b + 2, sp(3, A), sp(3, A), up)
+        if phase == 0:
+            send(p, 27, sp(3), sp(3), device(pos, 1 - core))
+        arrived(p, b + 1, sp(1))
+        send(p, b + 3, sp(1, B), sp(1, B), dn)
+        if phase == 0:
+            send(p, 28, sp(1), sp(1), device(pos, 1 - core))
+
+    def ag_c(p, phase):
+        axis = ORDERS[p][phase]
+        c1, c2, _ = (pos[a] for a in ORDERS[p])
+        b = 18 if phase == 1 else 22
+        def sp(d, cols=None):
+            return spot(p, c1, (c2 + d) % 4, cols=cols) if phase == 1 else spot(p, (c1 + d) % 4, cols=cols)
+        arrived(p, b + 2, sp(2, A))
+        if phase == 0:
+            send(p, 29, sp(2, A), sp(2, A), device(pos, 1 - core))
+        arrived(p, b + 3, sp(2, B))
+        if phase == 0:
+            send(p, 30, sp(2, B), sp(2, B), device(pos, 1 - core))
+
+    def sib(p):
+        c1 = pos[ORDERS[p][0]]
+        def sp(d, cols=None):
+            o = out_ref.at[1 - core, p]
+            rows = pl.ds(pl.multiple_of(192 * ((c1 + d) % 4), 16), 192)
+            return o.at[rows] if cols is None else o.at[rows, cols]
+        arrived(p, 26, sp(0)); arrived(p, 27, sp(3)); arrived(p, 28, sp(1))
+        arrived(p, 29, sp(2, A)); arrived(p, 30, sp(2, B))
+
+    T = range(3)
+    for p in T: rs_a(p, 0)
+    for p in T: rs_b(p, 0)
+    for p in T:
+        rs_c(p, 0)
+        rs_a(p, 1)
+    for p in T: rs_b(p, 1)
+    for p in T:
+        rs_c(p, 1)
+        rs3_a(p)
+    for p in T: rs3_b(p)
+    for p in T:
+        ag3(p); ag_a(p, 1)
+    for p in T: ag_b(p, 1)
+    for p in T:
+        ag_c(p, 1); ag_a(p, 0)
+    for p in T: ag_b(p, 0)
+    for p in T: ag_c(p, 0)
+    for p in T: sib(p)
+    for c in sent: c.wait_send()
+
+def allreduce(w):
+    return pl.pallas_call(
+        comm_kernel,
+        out_shape=jax.ShapeDtypeStruct((2, 3, 768, 1536), BF),
+        in_specs=[pl.BlockSpec(memory_space=pl.ANY)],
+        out_specs=pl.BlockSpec(memory_space=pl.ANY),
+        scratch_shapes=[
+            pltpu.VMEM((3, 4, 192, 1536), BF),
+            pltpu.VMEM((3, 2, 192, 768), BF), pltpu.VMEM((3, 2, 192, 1536), BF),
+            pltpu.VMEM((3, 4, 48, 1536), BF), pltpu.VMEM((3, 2, 48, 768), BF), pltpu.VMEM((3, 2, 48, 1536), BF),
+            pltpu.VMEM((3, 4, 48, 384), BF), pltpu.VMEM((3, 3, 48, 384), BF), pltpu.VMEM((3, 48, 384), BF),
+            pltpu.SemaphoreType.DMA, pltpu.SemaphoreType.DMA((3, NMSG)), pltpu.SemaphoreType.DMA((3, NMSG)),
+        ],
+        compiler_params=pltpu.CompilerParams(collective_id=0, has_side_effects=True, vmem_limit_bytes=50 * 2**20),
+        name="comm",
+    )(w)
+
+
+def sum_gradients(grads):
+    gq, go, gu, gd = [g.astype(BF) for g in grads]
+    def half(c):
+        return jnp.stack([
+            jnp.concatenate([gq[:, c * 1152:(c + 1) * 1152], go[:, c * 384:(c + 1) * 384]], 1),
+            gu[:, c * 1536:(c + 1) * 1536],
+            jnp.concatenate([gd[c * 1536:c * 1536 + 768], gd[c * 1536 + 768:(c + 1) * 1536]], 1),
+        ])
+    halves = jnp.stack([half(0), half(1)])
+    core = lax.axis_index("batch") % 2
+    keep = lax.dynamic_index_in_dim(halves, core, 0, keepdims=False)
+    give = lax.dynamic_index_in_dim(halves, 1 - core, 0, keepdims=False)
+    got = lax.ppermute(give, "batch", [(i, i ^ 1) for i in range(lax.axis_size("batch"))])
+    mine = (keep.astype(F32) + got.astype(F32)).astype(BF)
+    out = allreduce(mine.reshape(3, 4, 192, 1536)).astype(F32)
+    return (
+        jnp.concatenate([out[0, 0, :, :1152], out[1, 0, :, :1152]], 1),
+        jnp.concatenate([out[0, 0, :, 1152:], out[1, 0, :, 1152:]], 1),
+        jnp.concatenate([out[0, 1], out[1, 1]], 1),
+        jnp.concatenate([out[0, 2, :, :768], out[0, 2, :, 768:], out[1, 2, :, :768], out[1, 2, :, 768:]], 0),
+    )
+
+
 def on_device(
     embedded,
     cotangent,
@@ -399,7 +645,9 @@
     )[:, :, None]
     own_grad = jnp.where(not_first & thought_mask, 0.0, field_gradient)
     input_grad = lax.psum(own_grad.astype(jnp.bfloat16), "pass")
-    summed = lax.psum(grads, ("batch", "pass"))
+    big = sum_gradients([grads[2], grads[4], grads[8], grads[10]])
+    small = list(lax.psum([g for i, g in enumerate(grads) if i not in (2, 4, 8, 10)], ("batch", "pass")))
+    summed = small[:2] + [big[0], small[2], big[1]] + small[3:6] + [big[2], small[6], big[3], small[7]]
     return (activations.astype(jnp.bfloat16)[None], input_grad) + tuple(summed)
 
 

time: 876 us -> 821 us (0.937)
  waiting for transfers between devices: 225 us -> 0.05 us
  Pallas kernels: 0 us -> 77.6 us
  other arithmetic: 136 us -> 201 us
  matrix products: 242 us -> 258 us
    psum x1 -> x0, waiting for transfers between devices: 224 us -> none  [on_device(): summed = lax.psum(grads, ('batch', 'pass'))]
    pallas_call x0 -> x1, Pallas kernels: none -> 77.6 us  [allreduce(): pl.pallas_call(comm_kernel, out_shape=jax.ShapeDtypeStruct((2, 3, 768, 15...]
    convert_element_type x0 -> x6, other arithmetic: none -> 36.6 us  [the longest x1 16 us: sum_gradients(): out = allreduce(mine.reshape(3, 4, 192, 1536)).astype(F32)]
    dot_general x5, matrix products: 13.2 us -> 41.1 us  [backward(): jnp.einsum('bld,bli->di', normed_two, grad_hidden, preferred_element_type...]
    concatenate x0 -> x4, other arithmetic: none -> 17.9 us  [the longest x1 8.26 us: sum_gradients(): jnp.concatenate([out[0, 2, :, :768], out[0, 2, :, 768:], out[1, 2, :, :76...]
    squeeze x0 -> x4, local copies, waits for them, and re-layouts: none -> 17.5 us  [the longest x1 7.58 us: sum_gradients(): out[0, 2, :, :768]]
    unnamed x50 -> x54, local copies, waits for them, and re-layouts: 21.3 us -> 4.89 us
    dot_general x5, matrix products: 54.8 us -> 40.7 us  [backward(): jnp.einsum('bli,bld->id', active, grad_branch, preferred_element_type=jnp...]
  transfers between devices with their start and end apart: 12 -> 12, of which waited for: 1 -> 0; matrix products, arithmetic and copies ran while one was open for 17% -> 28% of each run, Pallas kernels for 0% -> 10%
where the time goes in v1:
time: 821 us; the launch traced here: 816 us
  matrix products  258 us (31%)
  other arithmetic  201 us (24%)
  local copies, waits for them, and re-layouts  120 us (15%)
  Pallas kernels  77.6 us (9%)
  blocking collectives  74.9 us (9%)
  loops' own time  47.7 us (6%)
  starting transfers between devices  22.7 us (3%)
  between operations  14.5 us (2%)
    pallas_call x1, Pallas kernels, allreduce(): pl.pallas_call(comm_kernel, out_shape=jax.ShapeDtypeStruct((2, 3, 768, 15...  77.6 us
    psum x1, blocking collectives, on_device(): lax.psum([g for i, g in enumerate(grads) if i not in (2, 4, 8, 10)], ('ba...  74.9 us
    dot_general x5, matrix products, backward(): jnp.einsum('bld,bli->di', normed_two, grad_hidden, preferred_element_type...  41.1 us
    dot_general x5, matrix products, backward(): jnp.einsum('bli,bld->id', active, grad_branch, preferred_element_type=jnp...  40.7 us
    select_n x40, other arithmetic, forward_turn(): jnp.where(in_range, lax.dynamic_update_slice_in_dim(whole_buf, piece, ite...  35.8 us
    dot_general x5, matrix products, backward(): jnp.einsum('bld,ble->de', normed, grad_qkv, preferred_element_type=jnp.fl...  34.1 us
    dot_general x5, matrix products, backward(): jnp.einsum('bld,id->bli', grad_branch, w_down, preferred_element_type=jnp...  27.7 us
    another operation x1, loops' own time, on_device(): lax.fori_loop(0, round_count, backward_turn, state)  24.2 us
  transfers between devices with their start and end apart: 12, of which 0 were waited for; matrix products, arithmetic and copies ran while one was open for 28% of the time, Pallas kernels for 10%

profile of v1, /device:TPU:1, one launch (start us, length us, event | category | flops | bytes accessed | tf_op | source)
XLA Modules:
  0.0 816.0 jit_solution(9838773370765795632)
XLA Ops:
  21.0 201.9 %while.91 = (s32[]{:T(128)}, bf16[2,6,768]{2,1,0:T(8,128)(2,1)}, bf16[2,128,768]{2,1,0:T(8,128)(2,1)}, f32[2,128,768]{2,1,0:T(8,128)}, bf16[2,128,768]{2,1,0:T(8...) while((s32[]{:T(128)}, bf16[2,6,768]{2,1,0:T(8,128)(2,1)}, ...), condition=%wide.region_8.9_spmd, body=%wide.region_0.8_spmd.sunk | while | flops 1876576640 | bytes 100807720 | solution.py:597
  43.5 3.5 fusion.185
  49.2 4.6 collective-permute-start
  85.5 3.5 fusion.185
  126.2 3.5 fusion.185
  166.6 3.5 fusion.185
  206.0 3.5 fusion.185
  223.0 329.8 %while.92 = (s32[]{:T(128)}, bf16[2,6,768]{2,1,0:T(8,128)(2,1)S(1)}, bf16[2,128,768]{2,1,0:T(8,128)(2,1)}, f32[768]{0:T(1024)}, f32[768]{0:T(1024)}, /*index=5*/...) while((s32[]{:T(128)}, ...), condition=%wide.region_28.29_spmd.clone, body=%wide.region_9.28_spmd.clone.sunk | while | flops 3792934144 | bytes 134381392 | solution.py:640
  235.5 5.5 convert_reduce_fusion.7
  261.5 5.1 select_add_fusion.27
  268.7 5.2 select_add_fusion.32
  274.0 5.2 select_add_fusion.34
  292.3 5.5 convert_reduce_fusion.7
  307.8 3.5 fusion.216
  318.3 7.3 select_add_fusion.27
  325.6 3.7 select_add_fusion.28
  329.4 9.0 %select_add_fusion.32 = f32[768,3072]{1,0:T(8,128)} fusion(f32[768,3072]{1,0:T(8,128)} %get-tuple-element.3336, pred[]{:T(512)S(6)} %compare.82, pred[]{:T(512)S(6)} %and.211, bf16[1,128,3072]{2,1,0:T(8,128)(2,1)S(1)} %copy-done.1, bf16[2,128,768]{2,1,0:T(8,128)(2,1)S(1)} %copy-done.20, s32[]{:T(128)S(6)} %min.74), kind=kOutput, calls=%fused_computation.64.clone.1 | convolution fusion | flops 611057664 | bytes 19857414 | tf_op jit(solution)/shard_map/while/body/eval_jaxpr/bld,bli->di/dot_general | solution.py:174
  338.5 8.9 %select_add_fusion.34 = f32[3072,768]{1,0:T(8,128)} fusion(f32[3072,768]{1,0:T(8,128)} %get-tuple-element.3338, pred[]{:T(512)S(6)} %compare.82, pred[]{:T(512)S(6)} %and.211, bf16[2,128,3072]{2,1,0:T(8,128)(2,1)S(1)} %copy-done.2, s32[]{:T(128)S(6)} %min.74, f32[1,128,768]{2,1,0:T(8,128)S(1)} %add.1193), kind=kOutput, calls=%fused_computation.63.clone.1 | convolution fusion | flops 611155968 | bytes 20054022 | tf_op jit(solution)/shard_map/while/body/eval_jaxpr/bli,bld->id/dot_general | solution.py:169
  360.4 5.5 convert_reduce_fusion.7
  375.9 3.5 fusion.216
  386.4 7.3 select_add_fusion.27
  393.8 3.7 select_add_fusion.28
  397.6 9.0 %select_add_fusion.32 = f32[768,3072]{1,0:T(8,128)} fusion(f32[768,3072]{1,0:T(8,128)} %get-tuple-element.3336, pred[]{:T(512)S(6)} %compare.82, pred[]{:T(512)S(6)} %and.211, bf16[1,128,3072]{2,1,0:T(8,128)(2,1)S(1)} %copy-done.1, bf16[2,128,768]{2,1,0:T(8,128)(2,1)S(1)} %copy-done.20, s32[]{:T(128)S(6)} %min.74), kind=kOutput, calls=%fused_computation.64.clone.1 | convolution fusion | flops 611057664 | bytes 19857414 | tf_op jit(solution)/shard_map/while/body/eval_jaxpr/bld,bli->di/dot_general | solution.py:174
  406.7 8.9 %select_add_fusion.34 = f32[3072,768]{1,0:T(8,128)} fusion(f32[3072,768]{1,0:T(8,128)} %get-tuple-element.3338, pred[]{:T(512)S(6)} %compare.82, pred[]{:T(512)S(6)} %and.211, bf16[2,128,3072]{2,1,0:T(8,128)(2,1)S(1)} %copy-done.2, s32[]{:T(128)S(6)} %min.74, f32[1,128,768]{2,1,0:T(8,128)S(1)} %add.1193), kind=kOutput, calls=%fused_computation.63.clone.1 | convolution fusion | flops 611155968 | bytes 20054022 | tf_op jit(solution)/shard_map/while/body/eval_jaxpr/bli,bld->id/dot_general | solution.py:169
  428.6 5.5 convert_reduce_fusion.7
  444.1 3.5 fusion.216
  454.6 7.3 select_add_fusion.27
  461.9 3.7 select_add_fusion.28
  465.7 9.0 %select_add_fusion.32 = f32[768,3072]{1,0:T(8,128)} fusion(f32[768,3072]{1,0:T(8,128)} %get-tuple-element.3336, pred[]{:T(512)S(6)} %compare.82, pred[]{:T(512)S(6)} %and.211, bf16[1,128,3072]{2,1,0:T(8,128)(2,1)S(1)} %copy-done.1, bf16[2,128,768]{2,1,0:T(8,128)(2,1)S(1)} %copy-done.20, s32[]{:T(128)S(6)} %min.74), kind=kOutput, calls=%fused_computation.64.clone.1 | convolution fusion | flops 611057664 | bytes 19857414 | tf_op jit(solution)/shard_map/while/body/eval_jaxpr/bld,bli->di/dot_general | solution.py:174
  474.8 8.9 %select_add_fusion.34 = f32[3072,768]{1,0:T(8,128)} fusion(f32[3072,768]{1,0:T(8,128)} %get-tuple-element.3338, pred[]{:T(512)S(6)} %compare.82, pred[]{:T(512)S(6)} %and.211, bf16[2,128,3072]{2,1,0:T(8,128)(2,1)S(1)} %copy-done.2, s32[]{:T(128)S(6)} %min.74, f32[1,128,768]{2,1,0:T(8,128)S(1)} %add.1193), kind=kOutput, calls=%fused_computation.63.clone.1 | convolution fusion | flops 611155968 | bytes 20054022 | tf_op jit(solution)/shard_map/while/body/eval_jaxpr/bli,bld->id/dot_general | solution.py:169
  496.7 5.5 convert_reduce_fusion.7
  522.8 7.3 select_add_fusion.27
  530.1 3.7 select_add_fusion.28
  533.9 9.0 %select_add_fusion.32 = f32[768,3072]{1,0:T(8,128)} fusion(f32[768,3072]{1,0:T(8,128)} %get-tuple-element.3336, pred[]{:T(512)S(6)} %compare.82, pred[]{:T(512)S(6)} %and.211, bf16[1,128,3072]{2,1,0:T(8,128)(2,1)S(1)} %copy-done.1, bf16[2,128,768]{2,1,0:T(8,128)(2,1)S(1)} %copy-done.20, s32[]{:T(128)S(6)} %min.74), kind=kOutput, calls=%fused_computation.64.clone.1 | convolution fusion | flops 611057664 | bytes 19857414 | tf_op jit(solution)/shard_map/while/body/eval_jaxpr/bld,bli->di/dot_general | solution.py:174
  543.0 8.9 %select_add_fusion.34 = f32[3072,768]{1,0:T(8,128)} fusion(f32[3072,768]{1,0:T(8,128)} %get-tuple-element.3338, pred[]{:T(512)S(6)} %compare.82, pred[]{:T(512)S(6)} %and.211, bf16[2,128,3072]{2,1,0:T(8,128)(2,1)S(1)} %copy-done.2, s32[]{:T(128)S(6)} %min.74, f32[1,128,768]{2,1,0:T(8,128)S(1)} %add.1193), kind=kOutput, calls=%fused_computation.63.clone.1 | convolution fusion | flops 611155968 | bytes 20054022 | tf_op jit(solution)/shard_map/while/body/eval_jaxpr/bli,bld->id/dot_general | solution.py:169
  552.8 4.1 convert_element_type.454
  558.8 4.5 convert_element_type.453
  582.7 8.6 %fusion.86 = bf16[3,768,1536]{2,1,0:T(8,128)(2,1)} fusion(s32[]{:T(128)S(6)} %select_n.641, bf16[1,3,768,1536]{3,2,1,0:T(8,128)(2,1)} %maximum_bitcast_fusion, bf16[1,3,768,1536]{3,2,1,0:T(8,128)(2,1)} %maximum_bitcast_fusion.1), kind=kLoop, calls=%fused_computation.192 | loop fusion | flops 3538944 | bytes 21233668 | tf_op jit(solution)/shard_map/jit(dynamic_index_in_dim)/squeeze | solution.py:500
  593.9 74.9 %all-reduce = (f32[768]{0:T(1024)}, f32[768]{0:T(1024)}, f32[1536]{0:T(1024)}, f32[768]{0:T(1024)}, f32[768]{0:T(1024)}, /*index=5*/f32[768]{0:T(1024)}, f32[3072]{0:T(1024)}, f32[768]{0:T(1024)}) all-reduce(f32[768]{0:T(1024)S(1)} %copy-done.52, f32[768]{0:T(1024)S(1)} %copy-done.55, ...), channel_id=1, replica_groups=mesh['batch'=32,'pass'=4] {'batch','pass'}, use_global_device_ids=true, to_apply=%region_30.31 | all-reduce | flops 9216 | bytes 73728 | tf_op jit(solution)/shard_map/psum | solution.py:649
  668.8 9.4 %fusion.84 = bf16[3,768,1536]{2,1,0:T(8,128)(2,1)} fusion(bf16[3,768,1536]{2,1,0:T(8,128)(2,1)} %collective-permute-done.2, s32[]{:T(128)S(6)} %select_n.640, bf16[1,3,768,1536]{3,2,1,0:T(8,128)(2,1)} %maximum_bitcast_fusion, bf16[1,3,768,1536]{3,2,1,0:T(8,128)(2,1)} %maximum_bitcast_fusion.1), kind=kLoop, calls=%fused_computation.188 | loop fusion | flops 17694720 | bytes 28311556 | tf_op jit(solution)/shard_map/convert_element_type | solution.py:502
  678.2 77.6 %comm.1 = bf16[2,3,768,1536]{3,2,1,0:T(8,128)(2,1)} custom-call(bf16[3,4,192,1536]{3,2,1,0:T(8,128)(2,1)} %bitcast.378), custom_call_target="tpu_custom_call" | custom-call | tf_op jit(solution)/shard_map/comm/pallas_call | solution.py:472
  755.8 16.0 %convert_element_type.459 = f32[2,3,768,1536]{3,2,1,0:T(8,128)} convert(bf16[2,3,768,1536]{3,2,1,0:T(8,128)(2,1)} %comm.1) | non-fusion elementwise | flops 7077888 | bytes 42467328 | tf_op jit(solution)/shard_map/convert_element_type | solution.py:503
  771.9 3.5 slice_bitcast_fusion.3
  777.2 4.6 slice_bitcast_fusion.1
  781.8 7.6 slice_bitcast_fusion.7
  789.4 3.5 pad_maximum_fusion.5
  794.5 4.6 pad_maximum_fusion.3
  799.1 8.3 %pad_maximum_fusion.4 = f32[3072,768]{1,0:T(8,128)} fusion(f32[768,768]{1,0:T(8,128)} %get-tuple-element.2621, f32[768,768]{1,0:T(8,128)} %get-tuple-element.2622, f32[768,768]{1,0:T(8,128)} %get-tuple-element.2623, f32[768,768]{1,0:T(8,128)} %get-tuple-element.2620), kind=kLoop, calls=%fused_computation.190 | loop fusion | flops 7077888 | bytes 18874368 | tf_op jit(solution)/shard_map/concatenate | solution.py:508
  (1250 shorter events, 335.7 us)
Async XLA Ops:
  7.2 800.2 %all-reduce.3.cloned.1.call-start = ((), (), s32[]{:S(2)}) async-start(), calls=%async_computation | async-start | bytes 786432 | tf_op jit(solution)/shard_map/psum | solution.py:647
  49.2 12.4 %collective-permute-start = (bf16[1,6,768]{2,1,0:T(8,128)(2,1)}, bf16[1,6,768]{2,1,0:T(8,128)(2,1)}, u32[]{:S(2)}, u32[]{:S(2)}) collective-permute-start(bf16[1,6,768]{2,1,0:T(8,128)(2,1)} %dynamic-slice_convert_fusion.4), channel_id=1, source_target_pairs={{0,1},{1,2},{2,3},{4,5},{5,6},{6,7},{8,9},{9,10},{10,11},{12,13},{... | collective-permute-start | bytes 27656 | tf_op jit(solution)/shard_map/while/body/eval_jaxpr/ppermute | solution.py:18
  91.3 11.1 %collective-permute-start = (bf16[1,6,768]{2,1,0:T(8,128)(2,1)}, bf16[1,6,768]{2,1,0:T(8,128)(2,1)}, u32[]{:S(2)}, u32[]{:S(2)}) collective-permute-start(bf16[1,6,768]{2,1,0:T(8,128)(2,1)} %dynamic-slice_convert_fusion.4), channel_id=1, source_target_pairs={{0,1},{1,2},{2,3},{4,5},{5,6},{6,7},{8,9},{9,10},{10,11},{12,13},{... | collective-permute-start | bytes 27656 | tf_op jit(solution)/shard_map/while/body/eval_jaxpr/ppermute | solution.py:18
  132.0 10.7 %collective-permute-start = (bf16[1,6,768]{2,1,0:T(8,128)(2,1)}, bf16[1,6,768]{2,1,0:T(8,128)(2,1)}, u32[]{:S(2)}, u32[]{:S(2)}) collective-permute-start(bf16[1,6,768]{2,1,0:T(8,128)(2,1)} %dynamic-slice_convert_fusion.4), channel_id=1, source_target_pairs={{0,1},{1,2},{2,3},{4,5},{5,6},{6,7},{8,9},{9,10},{10,11},{12,13},{... | collective-permute-start | bytes 27656 | tf_op jit(solution)/shard_map/while/body/eval_jaxpr/ppermute | solution.py:18
  172.3 9.8 %collective-permute-start = (bf16[1,6,768]{2,1,0:T(8,128)(2,1)}, bf16[1,6,768]{2,1,0:T(8,128)(2,1)}, u32[]{:S(2)}, u32[]{:S(2)}) collective-permute-start(bf16[1,6,768]{2,1,0:T(8,128)(2,1)} %dynamic-slice_convert_fusion.4), channel_id=1, source_target_pairs={{0,1},{1,2},{2,3},{4,5},{5,6},{6,7},{8,9},{9,10},{10,11},{12,13},{... | collective-permute-start | bytes 27656 | tf_op jit(solution)/shard_map/while/body/eval_jaxpr/ppermute | solution.py:18
  211.8 9.8 %collective-permute-start = (bf16[1,6,768]{2,1,0:T(8,128)(2,1)}, bf16[1,6,768]{2,1,0:T(8,128)(2,1)}, u32[]{:S(2)}, u32[]{:S(2)}) collective-permute-start(bf16[1,6,768]{2,1,0:T(8,128)(2,1)} %dynamic-slice_convert_fusion.4), channel_id=1, source_target_pairs={{0,1},{1,2},{2,3},{4,5},{5,6},{6,7},{8,9},{9,10},{10,11},{12,13},{... | collective-permute-start | bytes 27656 | tf_op jit(solution)/shard_map/while/body/eval_jaxpr/ppermute | solution.py:18
  223.2 12.3 %copy-start.35 = (f32[2,12,128,1]{2,1,3,0:T(8,128)}, f32[2,12,128,1]{2,1,3,0:T(8,128)S(1)}, u32[]{:S(2)}) copy-start(f32[2,12,128,1]{2,1,3,0:T(8,128)S(1)} %get-tuple-element.3399) | copy-start | bytes 36868 | tf_op jit(solution)/shard_map/while
  223.2 12.3 %copy-start.78 = (s32[3]{0:T(128)}, s32[3]{0:T(128)S(1)}, u32[]{:S(2)}) copy-start(s32[3]{0:T(128)S(1)} %get-tuple-element.3418) | copy-start | bytes 40 | tf_op jit(solution)/shard_map/while
  223.2 12.3 %copy-start.82 = (s32[1,2]{1,0:T(1,128)}, s32[1,2]{1,0:T(1,128)S(1)}, u32[]{:S(2)}) copy-start(s32[1,2]{1,0:T(1,128)S(1)} %get-tuple-element.3412) | copy-start | bytes 28 | tf_op jit(solution)/shard_map/while
  228.9 12.2 %slice-start = ((s8[4718592]{0:T(1024)(128)(4,1)}), s8[524288]{0:T(1024)(128)(4,1)S(1)}, s32[]{:S(2)}) async-start(s8[4718592]{0:T(1024)(128)(4,1)} %bitcast.355), calls=%async_computation.1 | async-start | bytes 1048576 | tf_op jit(solution)/shard_map/while
  259.8 19.5 %collective-permute-start.1 = (bf16[1,6,768]{2,1,0:T(8,128)(2,1)S(1)}, bf16[1,6,768]{2,1,0:T(8,128)(2,1)S(1)}, u32[]{:S(2)}, u32[]{:S(2)}) collective-permute-start(bf16[1,6,768]{2,1,0:T(8,128)(2,1)S(1)} %dynamic-slice_convert_fusion.5), channel_id=1, source_target_pairs={{1,0},{2,1},{3,2},{5,4},{6,5},{7,6},{9,8},{10,9},{11,10},{13,12},{... | collective-permute-start | bytes 27656 | tf_op jit(solution)/shard_map/while/body/eval_jaxpr/ppermute | solution.py:18
  279.9 12.3 %copy-start.35 = (f32[2,12,128,1]{2,1,3,0:T(8,128)}, f32[2,12,128,1]{2,1,3,0:T(8,128)S(1)}, u32[]{:S(2)}) copy-start(f32[2,12,128,1]{2,1,3,0:T(8,128)S(1)} %get-tuple-element.3399) | copy-start | bytes 36868 | tf_op jit(solution)/shard_map/while
  279.9 12.3 %copy-start.78 = (s32[3]{0:T(128)}, s32[3]{0:T(128)S(1)}, u32[]{:S(2)}) copy-start(s32[3]{0:T(128)S(1)} %get-tuple-element.3418) | copy-start | bytes 40 | tf_op jit(solution)/shard_map/while
  279.9 12.3 %copy-start.82 = (s32[1,2]{1,0:T(1,128)}, s32[1,2]{1,0:T(1,128)S(1)}, u32[]{:S(2)}) copy-start(s32[1,2]{1,0:T(1,128)S(1)} %get-tuple-element.3412) | copy-start | bytes 28 | tf_op jit(solution)/shard_map/while
  285.6 12.2 %slice-start = ((s8[4718592]{0:T(1024)(128)(4,1)}), s8[524288]{0:T(1024)(128)(4,1)S(1)}, s32[]{:S(2)}) async-start(s8[4718592]{0:T(1024)(128)(4,1)} %bitcast.355), calls=%async_computation.1 | async-start | bytes 1048576 | tf_op jit(solution)/shard_map/while
  316.6 30.9 %collective-permute-start.1 = (bf16[1,6,768]{2,1,0:T(8,128)(2,1)S(1)}, bf16[1,6,768]{2,1,0:T(8,128)(2,1)S(1)}, u32[]{:S(2)}, u32[]{:S(2)}) collective-permute-start(bf16[1,6,768]{2,1,0:T(8,128)(2,1)S(1)} %dynamic-slice_convert_fusion.5), channel_id=1, source_target_pairs={{1,0},{2,1},{3,2},{5,4},{6,5},{7,6},{9,8},{10,9},{11,10},{13,12},{... | collective-permute-start | bytes 27656 | tf_op jit(solution)/shard_map/while/body/eval_jaxpr/ppermute | solution.py:18
  338.5 9.6 %copy-start.36 = (f32[2,12,128,1]{2,1,3,0:T(8,128)S(1)}, f32[2,12,128,1]{2,1,3,0:T(8,128)}, u32[]{:S(2)}) copy-start(f32[2,12,128,1]{2,1,3,0:T(8,128)} %copy-done.35) | copy-start | bytes 36868 | tf_op jit(solution)/shard_map/while
  338.5 9.5 %copy-start.79 = (s32[3]{0:T(128)S(1)}, s32[3]{0:T(128)}, u32[]{:S(2)}) copy-start(s32[3]{0:T(128)} %copy-done.78) | copy-start | bytes 40 | tf_op jit(solution)/shard_map/while
  348.0 12.3 %copy-start.35 = (f32[2,12,128,1]{2,1,3,0:T(8,128)}, f32[2,12,128,1]{2,1,3,0:T(8,128)S(1)}, u32[]{:S(2)}) copy-start(f32[2,12,128,1]{2,1,3,0:T(8,128)S(1)} %get-tuple-element.3399) | copy-start | bytes 36868 | tf_op jit(solution)/shard_map/while
  348.1 12.3 %copy-start.78 = (s32[3]{0:T(128)}, s32[3]{0:T(128)S(1)}, u32[]{:S(2)}) copy-start(s32[3]{0:T(128)S(1)} %get-tuple-element.3418) | copy-start | bytes 40 | tf_op jit(solution)/shard_map/while
  348.1 12.3 %copy-start.82 = (s32[1,2]{1,0:T(1,128)}, s32[1,2]{1,0:T(1,128)S(1)}, u32[]{:S(2)}) copy-start(s32[1,2]{1,0:T(1,128)S(1)} %get-tuple-element.3412) | copy-start | bytes 28 | tf_op jit(solution)/shard_map/while
  353.7 12.2 %slice-start = ((s8[4718592]{0:T(1024)(128)(4,1)}), s8[524288]{0:T(1024)(128)(4,1)S(1)}, s32[]{:S(2)}) async-start(s8[4718592]{0:T(1024)(128)(4,1)} %bitcast.355), calls=%async_computation.1 | async-start | bytes 1048576 | tf_op jit(solution)/shard_map/while
  384.7 30.9 %collective-permute-start.1 = (bf16[1,6,768]{2,1,0:T(8,128)(2,1)S(1)}, bf16[1,6,768]{2,1,0:T(8,128)(2,1)S(1)}, u32[]{:S(2)}, u32[]{:S(2)}) collective-permute-start(bf16[1,6,768]{2,1,0:T(8,128)(2,1)S(1)} %dynamic-slice_convert_fusion.5), channel_id=1, source_target_pairs={{1,0},{2,1},{3,2},{5,4},{6,5},{7,6},{9,8},{10,9},{11,10},{13,12},{... | collective-permute-start | bytes 27656 | tf_op jit(solution)/shard_map/while/body/eval_jaxpr/ppermute | solution.py:18
  406.6 9.6 %copy-start.36 = (f32[2,12,128,1]{2,1,3,0:T(8,128)S(1)}, f32[2,12,128,1]{2,1,3,0:T(8,128)}, u32[]{:S(2)}) copy-start(f32[2,12,128,1]{2,1,3,0:T(8,128)} %copy-done.35) | copy-start | bytes 36868 | tf_op jit(solution)/shard_map/while
  416.2 12.3 %copy-start.35 = (f32[2,12,128,1]{2,1,3,0:T(8,128)}, f32[2,12,128,1]{2,1,3,0:T(8,128)S(1)}, u32[]{:S(2)}) copy-start(f32[2,12,128,1]{2,1,3,0:T(8,128)S(1)} %get-tuple-element.3399) | copy-start | bytes 36868 | tf_op jit(solution)/shard_map/while
  416.2 12.3 %copy-start.78 = (s32[3]{0:T(128)}, s32[3]{0:T(128)S(1)}, u32[]{:S(2)}) copy-start(s32[3]{0:T(128)S(1)} %get-tuple-element.3418) | copy-start | bytes 40 | tf_op jit(solution)/shard_map/while
  416.2 12.3 %copy-start.82 = (s32[1,2]{1,0:T(1,128)}, s32[1,2]{1,0:T(1,128)S(1)}, u32[]{:S(2)}) copy-start(s32[1,2]{1,0:T(1,128)S(1)} %get-tuple-element.3412) | copy-start | bytes 28 | tf_op jit(solution)/shard_map/while
  421.9 12.2 %slice-start = ((s8[4718592]{0:T(1024)(128)(4,1)}), s8[524288]{0:T(1024)(128)(4,1)S(1)}, s32[]{:S(2)}) async-start(s8[4718592]{0:T(1024)(128)(4,1)} %bitcast.355), calls=%async_computation.1 | async-start | bytes 1048576 | tf_op jit(solution)/shard_map/while
  452.9 30.9 %collective-permute-start.1 = (bf16[1,6,768]{2,1,0:T(8,128)(2,1)S(1)}, bf16[1,6,768]{2,1,0:T(8,128)(2,1)S(1)}, u32[]{:S(2)}, u32[]{:S(2)}) collective-permute-start(bf16[1,6,768]{2,1,0:T(8,128)(2,1)S(1)} %dynamic-slice_convert_fusion.5), channel_id=1, source_target_pairs={{1,0},{2,1},{3,2},{5,4},{6,5},{7,6},{9,8},{10,9},{11,10},{13,12},{... | collective-permute-start | bytes 27656 | tf_op jit(solution)/shard_map/while/body/eval_jaxpr/ppermute | solution.py:18
  474.8 9.6 %copy-start.36 = (f32[2,12,128,1]{2,1,3,0:T(8,128)S(1)}, f32[2,12,128,1]{2,1,3,0:T(8,128)}, u32[]{:S(2)}) copy-start(f32[2,12,128,1]{2,1,3,0:T(8,128)} %copy-done.35) | copy-start | bytes 36868 | tf_op jit(solution)/shard_map/while
  484.3 12.3 %copy-start.35 = (f32[2,12,128,1]{2,1,3,0:T(8,128)}, f32[2,12,128,1]{2,1,3,0:T(8,128)S(1)}, u32[]{:S(2)}) copy-start(f32[2,12,128,1]{2,1,3,0:T(8,128)S(1)} %get-tuple-element.3399) | copy-start | bytes 36868 | tf_op jit(solution)/shard_map/while
  484.4 12.3 %copy-start.78 = (s32[3]{0:T(128)}, s32[3]{0:T(128)S(1)}, u32[]{:S(2)}) copy-start(s32[3]{0:T(128)S(1)} %get-tuple-element.3418) | copy-start | bytes 40 | tf_op jit(solution)/shard_map/while
  484.4 12.3 %copy-start.82 = (s32[1,2]{1,0:T(1,128)}, s32[1,2]{1,0:T(1,128)S(1)}, u32[]{:S(2)}) copy-start(s32[1,2]{1,0:T(1,128)S(1)} %get-tuple-element.3412) | copy-start | bytes 28 | tf_op jit(solution)/shard_map/while
  490.1 12.2 %slice-start = ((s8[4718592]{0:T(1024)(128)(4,1)}), s8[524288]{0:T(1024)(128)(4,1)S(1)}, s32[]{:S(2)}) async-start(s8[4718592]{0:T(1024)(128)(4,1)} %bitcast.355), calls=%async_computation.1 | async-start | bytes 1048576 | tf_op jit(solution)/shard_map/while
  521.1 30.9 %collective-permute-start.1 = (bf16[1,6,768]{2,1,0:T(8,128)(2,1)S(1)}, bf16[1,6,768]{2,1,0:T(8,128)(2,1)S(1)}, u32[]{:S(2)}, u32[]{:S(2)}) collective-permute-start(bf16[1,6,768]{2,1,0:T(8,128)(2,1)S(1)} %dynamic-slice_convert_fusion.5), channel_id=1, source_target_pairs={{1,0},{2,1},{3,2},{5,4},{6,5},{7,6},{9,8},{10,9},{11,10},{13,12},{... | collective-permute-start | bytes 27656 | tf_op jit(solution)/shard_map/while/body/eval_jaxpr/ppermute | solution.py:18
  543.0 9.6 %copy-start.36 = (f32[2,12,128,1]{2,1,3,0:T(8,128)S(1)}, f32[2,12,128,1]{2,1,3,0:T(8,128)}, u32[]{:S(2)}) copy-start(f32[2,12,128,1]{2,1,3,0:T(8,128)} %copy-done.35) | copy-start | bytes 36868 | tf_op jit(solution)/shard_map/while
  558.8 9.6 %slice-start.2 = ((s8[7077888]{0:T(1024)(128)(4,1)}), s8[2883584]{0:T(1024)(128)(4,1)S(1)}, s32[]{:S(2)}) async-start(s8[7077888]{0:T(1024)(128)(4,1)} %bitcast.357), calls=%async_computation.3 | async-start | bytes 5767168
  582.6 10.2 %copy-start.85 = (s32[2]{0:T(128)S(1)}, s32[2]{0:T(128)}, u32[]{:S(2)}) copy-start(s32[2]{0:T(128)} %get-tuple-element.3581) | copy-start | bytes 28
  582.6 10.3 %copy-start.25 = (bf16[2,128,768]{2,1,0:T(8,128)(2,1)S(1)}, bf16[2,128,768]{2,1,0:T(8,128)(2,1)}, u32[]{:S(2)}) copy-start(bf16[2,128,768]{2,1,0:T(8,128)(2,1)} %get-tuple-element.2247) | copy-start | bytes 1179652
  582.6 11.2 %copy-start.39 = (f32[3072]{0:T(1024)S(1)}, f32[3072]{0:T(1024)}, u32[]{:S(2)}) copy-start(f32[3072]{0:T(1024)} %get-tuple-element.2258) | copy-start | bytes 36868
  582.6 11.2 %copy-start.49 = (f32[1536]{0:T(1024)S(1)}, f32[1536]{0:T(1024)}, u32[]{:S(2)}) copy-start(f32[1536]{0:T(1024)} %get-tuple-element.2254) | copy-start | bytes 18436
  582.6 11.2 %copy-start.52 = (f32[768]{0:T(1024)S(1)}, f32[768]{0:T(1024)}, u32[]{:S(2)}) copy-start(f32[768]{0:T(1024)} %get-tuple-element.2248) | copy-start | bytes 9220
  582.6 11.2 %copy-start.55 = (f32[768]{0:T(1024)S(1)}, f32[768]{0:T(1024)}, u32[]{:S(2)}) copy-start(f32[768]{0:T(1024)} %get-tuple-element.2249) | copy-start | bytes 9220
  582.6 11.2 %copy-start.58 = (f32[768]{0:T(1024)S(1)}, f32[768]{0:T(1024)}, u32[]{:S(2)}) copy-start(f32[768]{0:T(1024)} %get-tuple-element.2255) | copy-start | bytes 9220
  582.6 11.2 %copy-start.61 = (f32[768]{0:T(1024)S(1)}, f32[768]{0:T(1024)}, u32[]{:S(2)}) copy-start(f32[768]{0:T(1024)} %get-tuple-element.2256) | copy-start | bytes 9220
  582.7 11.2 %copy-start.64 = (f32[768]{0:T(1024)S(1)}, f32[768]{0:T(1024)}, u32[]{:S(2)}) copy-start(f32[768]{0:T(1024)} %get-tuple-element.2257) | copy-start | bytes 9220
  582.7 11.2 %copy-start.67 = (f32[768]{0:T(1024)S(1)}, f32[768]{0:T(1024)}, u32[]{:S(2)}) copy-start(f32[768]{0:T(1024)} %get-tuple-element.2259) | copy-start | bytes 9220
  591.3 77.5 %collective-permute-start.2 = (bf16[3,768,1536]{2,1,0:T(8,128)(2,1)}, bf16[3,768,1536]{2,1,0:T(8,128)(2,1)}, u32[]{:S(2)}, u32[]{:S(2)}) collective-permute-start(bf16[3,768,1536]{2,1,0:T(8,128)(2,1)} %fusion.86), channel_id=1, source_target_pairs={{0,4},{4,0},{8,12},{12,8},{16,20},{20,16},{24,28},{28,24},{32,36},... | collective-permute-start | bytes 21233672 | tf_op jit(solution)/shard_map/ppermute | solution.py:501
  (330 other events, 1523.3 us)
Sparse Core Ops, SparseCore 0:
  593.9 46.6 all-reduce.2

commit v2 on v0

v2 whole, which is shorter than its diff:
```python
import functools

import jax
import jax.numpy as jnp
from jax import lax
from jax.experimental import pallas as pl
from jax.experimental.pallas import tpu as pltpu
from jax.sharding import PartitionSpec as P

MESH = pl.DeviceIdType.MESH
BF, F32 = jnp.bfloat16, jnp.float32
HEADS = 12
D = 768
FF = 3072
ROWS = 256
TOP = 48
epsilon = 1e-05
SCALE = 0.125

LN1G, LN1S, BQV, BOUT, LN2G, LN2S, BUP, BDOWN = 0, 1, 2, 4, 5, 6, 7, 11

ORDERS = ((0, 1, 2), (1, 2, 0), (2, 0, 1))
NMSG = 31
A = pl.ds(0, 768)
B = pl.ds(768, 768)


def mm(a, b):
    return jnp.dot(a, b, preferred_element_type=F32)


def mm_nt(a, b):
    return lax.dot_general(a, b, (((1,), (1,)), ((), ())), preferred_element_type=F32)


def mm_tn(a, b):
    return lax.dot_general(a, b, (((0,), (0,)), ((), ())), preferred_element_type=F32)


def normalise(v):
    mu = jnp.sum(v, -1, keepdims=True) * (1.0 / D)
    c = v - mu
    var = jnp.sum(c * c, -1, keepdims=True) * (1.0 / D)
    rs = lax.rsqrt(var + epsilon)
    return c * rs, rs


def normalise_back(grad, gain, xhat, rs):
    gy = grad * gain
    m1 = jnp.sum(gy, -1, keepdims=True) * (1.0 / D)
    m2 = jnp.sum(gy * xhat, -1, keepdims=True) * (1.0 / D)
    return rs * (gy - m1 - xhat * m2)


def gelu_both(u):
    k = 0.7978845608028654
    u2 = u * u
    th = jnp.tanh(k * u * (1.0 + 0.044715 * u2))
    half = 0.5 * (1.0 + th)
    return u * half, half + 0.5 * u * (1.0 - th * th) * (k * (1.0 + 3 * 0.044715 * u2))


def eights(v):
    return jnp.sum(v.reshape(v.shape[0] // 8, 8, v.shape[1]), 0)


def column_sum(v):
    return jnp.sum(eights(v), 0, keepdims=True)


def coords():
    b = lax.axis_index("batch")
    y = lax.axis_index("pass")
    core = b % 2
    z = (b // 2) % 4
    x = b // 8
    return (x, y, z), core


def device(pos, core):
    x, y, z = pos
    return ((x * 4 + z) * 2 + core, y)


def along(pos, axis, by):
    return tuple((c + by) % 4 if i == axis else c for i, c in enumerate(pos))


def iota(shape, dim):
    return lax.broadcasted_iota(jnp.int32, shape, dim)


def lane_heads(v, rows):
    head = iota((rows, D), 1) // 64
    zero = jnp.zeros((rows, D), v.dtype)
    return jnp.concatenate([jnp.where(head == h, v, zero) for h in range(HEADS)], 0)


def join_heads(v, rows):
    head = iota((rows, D), 1) // 64
    total = jnp.zeros((rows, D), F32)
    for h in range(HEADS):
        total = jnp.where(head == h, v[h * rows : (h + 1) * rows], total)
    return total


def pair_rows(v):
    left = iota((128, 128), 1) < 64
    zero = jnp.zeros((128, 128), v.dtype)
    return jnp.concatenate([jnp.where(left, v, zero), jnp.where(left, zero, v)], 0)


def pair_join(v):
    left = iota((128, 128), 1) < 64
    return jnp.where(left, v[:128], v[128:])


SCRATCH = dict(
    x_v=((ROWS, D), BF),
    wq=((D, 3 * D), BF), wo=((D, D), BF), wu=((D, FF), BF), wd=((FF, D), BF),
    par=((16, D), F32),
    xh1=((ROWS, D), F32), rs1=((ROWS, 1), F32), qkv=((ROWS, 3 * D), BF),
    prob=((12, 256, 128), F32), res=((ROWS, D), F32), xh2=((ROWS, D), F32), rs2=((ROWS, 1), F32),
    gp=((ROWS, FF), F32), act=((ROWS, FF), BF),
    tmp=((ROWS, D), F32), dmix=((ROWS, D), BF),
    du=((ROWS, FF), BF), da=((ROWS, D), BF), dqkv=((ROWS, 3 * D), BF), sums=((16, D), F32),
    xm=((4, 16, D), F32), xh1m=((4, 16, D), F32), rs1m=((4, 16, 1), F32), qkvm=((4, 16, 3 * D), BF),
    kall=((3, 128, D), BF), vall=((3, 128, D), BF), pm=((3, 192, 128), F32),
    xh2m=((3, 16, D), F32), rs2m=((3, 16, 1), F32), gpm=((3, 16, FF), F32),
    slots=((4, 16, D), BF), slot_out=((16, D), BF),
    e_own=((16, D), BF), du_own=((16, FF), BF), da_own=((16, D), BF), dqkv_own=((80, 3 * D), BF),
    dx_mini=((16, D), F32), dxm_own=((16, D), BF), dxb_own=((64, D), F32),
    f_n1=((512, D), BF), f_o=((512, D), BF), f_n2=((512, D), BF), f_dh=((512, D), BF),
    f_qo=((512, 1536), BF), f_du=((512, 1536), BF), f_act=((512, 1536), BF),
    w1=((3, 768, 1536), BF), relay1=((3, 2, 192, 768), BF), in1=((3, 2, 192, 1536), BF),
    w2=((3, 192, 1536), BF), relay2=((3, 2, 48, 768), BF), in2=((3, 2, 48, 1536), BF),
    w3=((3, 4, 48, 384), BF), in3=((3, 3, 48, 384), BF), fin=((3, 48, 384), BF),
    own=((4, 64, D), BF), own_in=((3, 64, D), BF), own_sum=((64, D), BF),
    small_in=((10, 16, D), F32),
)
NAMES = list(SCRATCH)


def kernel(start_ref, length_ref, x_hbm, cot_hbm, par_hbm, wq_hbm, wo_hbm, wu_hbm, wd_hbm,
           act_out, own_out, small_out, out_ref, *scratch):
    r = dict(zip(NAMES, scratch))
    lsem, fsem, frem, ssem, rsem, xs_send, xs_recv = scratch[len(NAMES):]
    g = type("Refs", (), r)
    g.dx, g.dres, g.dn1, g.out_act = g.res, g.tmp, g.xh2, g.x_v
    g.cot_v = g.f_dh.at[pl.ds(0, 256)]
    pos, core = coords()
    me = pos[1]
    sibling = device(pos, 1 - core)

    barrier = pltpu.get_barrier_semaphore()
    for axis in range(3):
        for by in (1, 2, 3):
            pl.semaphore_signal(barrier, inc=1, device_id=device(along(pos, axis, by), core), device_id_type=MESH)
    pl.semaphore_signal(barrier, inc=1, device_id=sibling, device_id_type=MESH)

    loads = [
        pltpu.make_async_copy(src, dst, lsem.at[i])
        for i, (src, dst) in enumerate(
            ((x_hbm, g.x_v), (par_hbm, g.par), (wq_hbm, g.wq), (wo_hbm, g.wo), (wu_hbm, g.wu), (wd_hbm, g.wd), (cot_hbm, g.cot_v))
        )
    ]
    for c in loads:
        c.start()

    def row(i, n=1):
        if n == 1:
            return g.par[i : i + 1, :]
        return jnp.concatenate([g.par[i + k : i + k + 1, :] for k in range(n)], 1)

    s0, s1 = start_ref[0], start_ref[1]
    n0, n1 = length_ref[0], length_ref[1]
    r16 = iota((16, 256), 0)
    want = jnp.where(r16 < 8, s0 - 1 + r16, 128 + s1 - 1 + r16 - 8)
    pick = (iota((16, 256), 1) == want).astype(BF)
    col16 = iota((TOP, 16), 1)
    row48 = iota((TOP, 16), 0)
    place = []
    place_slots = []
    for q, s in ((0, s0), (1, s1)):
        i = col16 - 8 * q
        hit = (i >= 0) & (i < 8) & (row48 == s - 1 + i)
        place.append(hit.astype(BF))
        place_slots.append((hit & (i >= 1) & (i <= 6)).astype(BF))

    def is_slot(s, rows):
        j = iota((rows, 1), 0)
        return (j >= s) & (j < s + 6)

    loads[0].wait()
    loads[1].wait()

    def norm_one(i, _):
        rows = pl.ds(pl.multiple_of(i * 32, 32), 32)
        xhat, rs = normalise(g.x_v[rows, :].astype(F32))
        g.xh1[rows, :] = xhat
        g.rs1[rows, :] = rs
        g.f_n1[rows, :] = (xhat * row(LN1G) + row(LN1S)).astype(BF)
        return 0

    lax.fori_loop(0, 8, norm_one, 0)
    loads[2].wait()
    qkv_bias = (row(BQV), jnp.zeros((1, D), F32), row(BQV + 1))
    for k in range(3):
        c = slice(k * D, (k + 1) * D)
        g.qkv[:, c] = (mm(g.f_n1[0:256, :], g.wq[:, c]) + qkv_bias[k]).astype(BF)

    xm = mm(pick, g.x_v[...])
    g.xm[0] = xm
    xhat, rs = normalise(xm)
    g.xh1m[0] = xhat
    g.rs1m[0] = rs
    g.qkvm[0] = mm(pick, g.qkv[...]).astype(BF)
    for t in range(3):
        for buf, lane in ((g.kall, D), (g.vall, 2 * D)):
            buf[t, 0:32, :] = g.qkv[0:32, lane : lane + D]
            buf[t, 32:64, :] = g.qkv[128:160, lane : lane + D]
            buf[t, 80:128, :] = jnp.zeros((48, D), BF)
    for c in loads[3:6]:
        c.wait()

    rr = iota((192, 128), 0) % 16
    cc = iota((192, 128), 1)
    rq, ri = rr // 8, rr % 8
    base_ok = (cc < 64) & (cc // 32 == rq) & (cc % 32 < jnp.where(rq == 0, s0, s1))
    mi = cc - 64
    mini_ok = (mi >= 0) & (mi < 16) & (mi // 8 == rq) & (mi % 8 >= 1) & (mi % 8 <= ri)
    mini_allowed = base_ok | mini_ok
    mini_first = iota((16, D), 0) % 8 == 0

    def thought(t, _):
        g.kall[t, 64:80, :] = g.qkvm[t, :, D : 2 * D]
        g.vall[t, 64:80, :] = g.qkvm[t, :, 2 * D : 3 * D]
        s = mm_nt(lane_heads(g.qkvm[t, :, 0:D], 16), g.kall[t]) * SCALE
        s = jnp.where(mini_allowed, s, -1e30)
        e = jnp.exp(s - jnp.max(s, -1, keepdims=True))
        p = e / jnp.sum(e, -1, keepdims=True)
        g.pm[t] = p
        o = join_heads(mm(p.astype(BF), g.vall[t]), 16).astype(BF)
        res = g.xm[t] + mm(o, g.wo[...]) + row(BOUT)
        xhat, rs = normalise(res)
        g.xh2m[t] = xhat
        g.rs2m[t] = rs
        n2 = (xhat * row(LN2G) + row(LN2S)).astype(BF)
        parts = []
        for k in range(2):
            u = mm(n2, g.wu[:, k * 1536 : (k + 1) * 1536]) + row(BUP + 2 * k, 2)
            m, slope = gelu_both(u)
            g.gpm[t, :, k * 1536 : (k + 1) * 1536] = slope
            parts.append(m.astype(BF))
        h = res + mm(jnp.concatenate(parts, 1), g.wd[...]) + row(BDOWN)
        h = h.astype(BF).astype(F32)
        nxt = jnp.where(mini_first, g.xm[t], pltpu.roll(h, 1, 0))
        g.xm[t + 1] = nxt
        xhat, rs = normalise(nxt)
        g.xh1m[t + 1] = xhat
        g.rs1m[t + 1] = rs
        n1 = (xhat * row(LN1G) + row(LN1S)).astype(BF)
        for k in range(3):
            c = slice(k * D, (k + 1) * D)
            g.qkvm[t + 1, :, c] = (mm(n1, g.wq[:, c]) + qkv_bias[k]).astype(BF)
        return 0

    lax.fori_loop(0, 3, thought, 0)

    for q, s in ((0, s0), (1, s1)):
        rows = slice(128 * q, 128 * q + TOP)
        slot = is_slot(s, TOP)
        x = jnp.where(slot, mm(place_slots[q], g.xm[me].astype(BF)), g.x_v[rows, :].astype(F32))
        g.x_v[rows, :] = x.astype(BF)
        xhat, rs = normalise(x)
        g.xh1[rows, :] = xhat
        g.rs1[rows, :] = rs
        g.f_n1[rows, :] = (xhat * row(LN1G) + row(LN1S)).astype(BF)
        g.qkv[rows, :] = jnp.where(slot, mm(place_slots[q], g.qkvm[me]), g.qkv[rows, :].astype(F32)).astype(BF)

    qi = iota((256, 128), 0) % 128
    kj = iota((256, 128), 1)

    def attend(q, _):
        rows = pl.ds(pl.multiple_of(q * 128, 128), 128)
        ok = (kj <= qi) & (kj < jnp.where(q == 0, n0, n1))
        for hp in range(6):
            lanes = slice(128 * hp, 128 * hp + 128)
            q2 = pair_rows(g.qkv[rows, lanes])
            s = mm_nt(q2, g.qkv[rows, D + 128 * hp : D + 128 * hp + 128]) * SCALE
            s = jnp.where(ok, s, -1e30)
            e = jnp.exp(s - jnp.max(s, -1, keepdims=True))
            p = e / jnp.sum(e, -1, keepdims=True)
            g.prob[q * 6 + hp] = p
            o2 = mm(p.astype(BF), g.qkv[rows, 2 * D + 128 * hp : 2 * D + 128 * hp + 128])
            g.f_o[rows, lanes] = pair_join(o2).astype(BF)
        return 0

    lax.fori_loop(0, 2, attend, 0)

    g.tmp[...] = mm(g.f_o[0:256, :], g.wo[...])

    def norm_two(i, _):
        rows = pl.ds(pl.multiple_of(i * 32, 32), 32)
        res = g.x_v[rows, :].astype(F32) + g.tmp[rows, :] + row(BOUT)
        g.res[rows, :] = res
        xhat, rs = normalise(res)
        g.xh2[rows, :] = xhat
        g.rs2[rows, :] = rs
        g.f_n2[rows, :] = (xhat * row(LN2G) + row(LN2S)).astype(BF)
        return 0

    lax.fori_loop(0, 8, norm_two, 0)
    for k in range(4):
        c = slice(k * D, (k + 1) * D)
        m, slope = gelu_both(mm(g.f_n2[0:256, :], g.wu[:, c]) + row(BUP + k))
        g.gp[:, c] = slope
        g.act[:, c] = m.astype(BF)
    g.out_act[...] = (g.res[...] + mm(g.act[...], g.wd[...]) + row(BDOWN)).astype(BF)
    act_copy = pltpu.make_async_copy(g.out_act, act_out, lsem.at[0])
    act_copy.start()

    pl.semaphore_wait(barrier, 10)
    lo, hi = pl.ds(0, 256), pl.ds(256, 256)
    started = []

    def to_sibling(i, src, dst):
        c = pltpu.make_async_remote_copy(src_ref=src, dst_ref=dst, send_sem=fsem.at[i], recv_sem=frem.at[i],
                                         device_id=sibling, device_id_type=MESH)
        c.start()
        started.append(c)
        return c

    def local(i, src, dst):
        c = pltpu.make_async_copy(src, dst, lsem.at[i])
        c.start()
        return c

    def half(ref, which, width):
        return ref.at[:, pl.ds(pl.multiple_of(which * width, 128), width)]

    n1_go = to_sibling(0, g.f_n1.at[lo], g.f_n1.at[hi])
    o_go = to_sibling(1, g.f_o.at[lo], g.f_o.at[hi])
    n2_go = to_sibling(2, g.f_n2.at[lo], g.f_n2.at[hi])
    act_go = to_sibling(3, half(g.act, 1 - core, 1536), g.f_act.at[hi])
    act_local = local(1, half(g.act, core, 1536), g.f_act.at[lo])

    loads[6].wait()
    for k in range(4):
        c = slice(k * D, (k + 1) * D)
        du = (mm_nt(g.cot_v[...], g.wd[c, :]) * g.gp[:, c]).astype(BF)
        g.du[:, c] = du
        g.sums[BUP + k : BUP + k + 1, :] = column_sum(du.astype(F32))
    g.sums[BDOWN : BDOWN + 1, :] = column_sum(g.cot_v[...].astype(F32))
    g.tmp[...] = mm_nt(g.du[...], g.wu[...])
    zero8 = jnp.zeros((8, D), F32)

    def back_two(i, acc):
        rows = pl.ds(pl.multiple_of(i * 32, 32), 32)
        dn = g.tmp[rows, :]
        xhat = g.xh2[rows, :]
        dres = g.cot_v[rows, :].astype(F32) + normalise_back(dn, row(LN2G), xhat, g.rs2[rows, :])
        g.dres[rows, :] = dres
        da = dres.astype(BF)
        g.da[rows, :] = da
        return acc[0] + eights(dn * xhat), acc[1] + eights(dn), acc[2] + eights(da.astype(F32))

    acc = lax.fori_loop(0, 8, back_two, (zero8, zero8, zero8))
    for i, a in zip((LN2G, LN2S, BOUT), acc):
        g.sums[i : i + 1, :] = jnp.sum(a, 0, keepdims=True)
    g.dmix[...] = mm_nt(g.da[...], g.wo[...]).astype(BF)

    def attend_back(q, _):
        rows = pl.ds(pl.multiple_of(q * 128, 128), 128)
        for hp in range(6):
            lanes = slice(128 * hp, 128 * hp + 128)
            klanes = slice(D + 128 * hp, D + 128 * hp + 128)
            vlanes = slice(2 * D + 128 * hp, 2 * D + 128 * hp + 128)
            do2 = pair_rows(g.dmix[rows, lanes])
            p = g.prob[q * 6 + hp]
            dp = mm_nt(do2, g.qkv[rows, vlanes])
            ds = (p * (dp - jnp.sum(p * dp, -1, keepdims=True))).astype(BF)
            g.dqkv[rows, lanes] = (pair_join(mm(ds, g.qkv[rows, klanes])) * SCALE).astype(BF)
            g.dqkv[rows, klanes] = (mm_tn(ds, pair_rows(g.qkv[rows, lanes])) * SCALE).astype(BF)
            g.dqkv[rows, vlanes] = mm_tn(p.astype(BF), do2).astype(BF)
        return 0

    lax.fori_loop(0, 2, attend_back, 0)
    g.dn1[...] = mm_nt(g.dqkv[...], g.wq[...])

    def back_one(i, acc):
        rows = pl.ds(pl.multiple_of(i * 32, 32), 32)
        dn = g.dn1[rows, :]
        xhat = g.xh1[rows, :]
        g.dx[rows, :] = g.dres[rows, :] + normalise_back(dn, row(LN1G), xhat, g.rs1[rows, :])
        dq = eights(g.dqkv[rows, 0:D].astype(F32))
        dv = eights(g.dqkv[rows, 2 * D : 3 * D].astype(F32))
        return acc[0] + eights(dn * xhat), acc[1] + eights(dn), acc[2] + dq, acc[3] + dv

    acc = lax.fori_loop(0, 8, back_one, (zero8, zero8, zero8, zero8))
    for i, a in zip((LN1G, LN1S, BQV, BQV + 1), acc):
        g.sums[i : i + 1, :] = jnp.sum(a, 0, keepdims=True)

    g.slot_out[...] = mm(pick, g.dx[...].astype(BF)).astype(BF)
    for by in (1, 2, 3):
        c = pltpu.make_async_remote_copy(
            src_ref=g.slot_out, dst_ref=g.slots.at[me], send_sem=xs_send.at[by - 1], recv_sem=xs_recv.at[by - 1],
            device_id=device(along(pos, 1, by), core), device_id_type=MESH)
        c.start()
        started.append(c)
    g.dx_mini[...] = jnp.zeros((16, D), F32)
    g.e_own[...] = jnp.zeros((16, D), BF)
    g.du_own[...] = jnp.zeros((16, FF), BF)
    g.da_own[...] = jnp.zeros((16, D), BF)
    g.dqkv_own[...] = jnp.zeros((80, 3 * D), BF)
    g.dxm_own[...] = jnp.zeros((16, D), BF)
    g.dxb_own[...] = jnp.zeros((64, D), F32)
    for by in (1, 2, 3):
        src = (me + 4 - by) % 4
        pltpu.make_async_remote_copy(
            src_ref=g.slot_out, dst_ref=g.slots.at[src], send_sem=xs_send.at[by - 1], recv_sem=xs_recv.at[by - 1],
            device_id=device(along(pos, 1, by), core), device_id_type=MESH).wait_recv()
    keep = iota((16, D), 0) % 8 <= 5

    def thought_back(i, _):
        t = 2 - i

        @pl.when(t >= me)
        def _():
            e = (g.slots[t + 1].astype(F32) + g.dx_mini[...]).astype(BF).astype(F32)
            e = jnp.where(keep, pltpu.roll(e, 15, 0), 0.0)
            eb = e.astype(BF)
            parts = []
            for k in range(2):
                dm = mm_nt(eb, g.wd[k * 1536 : (k + 1) * 1536, :])
                parts.append((dm * g.gpm[t, :, k * 1536 : (k + 1) * 1536]).astype(BF))
            du = jnp.concatenate(parts, 1)
            dn2 = mm_nt(du, g.wu[...])
            xhat2 = g.xh2m[t]
            dres = e + normalise_back(dn2, row(LN2G), xhat2, g.rs2m[t])
            da = dres.astype(BF)
            dmix = mm_nt(da, g.wo[...]).astype(BF)
            do_s = lane_heads(dmix, 16)
            q_s = lane_heads(g.qkvm[t, :, 0:D], 16)
            p = g.pm[t]
            dp = mm_nt(do_s, g.vall[t])
            ds = (p * (dp - jnp.sum(p * dp, -1, keepdims=True))).astype(BF)
            dq = (join_heads(mm(ds, g.kall[t]), 16) * SCALE).astype(BF)
            dk = (mm_tn(ds, q_s)[0:80] * SCALE).astype(BF)
            dv = mm_tn(p.astype(BF), do_s)[0:80].astype(BF)
            dq = jnp.concatenate([jnp.zeros((64, D), BF), dq], 0)
            dqkv = jnp.concatenate([dq, dk, dv], 1)
            dn1 = mm_nt(dqkv, g.wq[...])
            gain = row(LN1G)
            xhat1 = g.xh1m[t]
            dxm = dres + normalise_back(dn1[64:80], gain, xhat1, g.rs1m[t])
            g.dx_mini[...] = dxm

            @pl.when(t == me)
            def _():
                g.e_own[...] = eb
                g.du_own[...] = du
                g.da_own[...] = da
                g.dqkv_own[...] = dqkv
                g.dxm_own[...] = dxm.astype(BF)
                total = {}
                b0, b1 = g.xh1[0:32, :], g.xh1[128:160, :]
                g.dxb_own[0:32, :] = normalise_back(dn1[0:32], gain, b0, g.rs1[0:32, :])
                g.dxb_own[32:64, :] = normalise_back(dn1[32:64], gain, b1, g.rs1[128:160, :])
                total[LN1G] = column_sum(dn1[0:32] * b0) + column_sum(dn1[32:64] * b1) + column_sum(dn1[64:80] * xhat1)
                total[LN1S] = column_sum(dn1)
                total[BQV] = column_sum(dq.astype(F32))
                total[BQV + 1] = column_sum(dv.astype(F32))
                total[BOUT] = column_sum(da.astype(F32))
                total[LN2G] = column_sum(dn2 * xhat2)
                total[LN2S] = column_sum(dn2)
                total[BDOWN] = column_sum(e)
                for i, v in total.items():
                    g.sums[i : i + 1, :] += v
                for k in range(4):
                    g.sums[BUP + k : BUP + k + 1, :] += column_sum(du[:, k * D : (k + 1) * D].astype(F32))

        return 0

    lax.fori_loop(0, 3, thought_back, 0)

    top = [slice(128 * q, 128 * q + TOP) for q in range(2)]

    def merge(into, own, q):
        into[top[q], :] = (into[top[q], :].astype(F32) + mm(place[q], own[...])).astype(BF)

    for q in range(2):
        merge(g.cot_v, g.e_own, q)
    dh_go = to_sibling(4, g.cot_v, g.f_dh.at[hi])
    for q in range(2):
        merge(g.du, g.du_own, q)
    du_go = to_sibling(5, half(g.du, 1 - core, 1536), g.f_du.at[hi])
    du_local = local(3, half(g.du, core, 1536), g.f_du.at[lo])
    for q in range(2):
        merge(g.da, g.da_own, q)
        base = jnp.concatenate([g.dqkv_own[32 * q : 32 * q + 32, :].astype(F32), jnp.zeros((16, 3 * D), F32)], 0)
        g.dqkv[top[q], :] = (g.dqkv[top[q], :].astype(F32) + mm(place[q], g.dqkv_own[64:80, :]) + base).astype(BF)
    dq_go = to_sibling(6, half(g.dqkv, 1 - core, 1152), g.f_qo.at[hi, pl.ds(0, 1152)])
    dq_local = local(4, half(g.dqkv, core, 1152), g.f_qo.at[lo, pl.ds(0, 1152)])
    da_go = to_sibling(7, half(g.da, 1 - core, 384), g.f_qo.at[hi, pl.ds(1152, 384)])
    da_local = local(5, half(g.da, core, 384), g.f_qo.at[lo, pl.ds(1152, 384)])
    later = (me > 0).astype(F32)
    for q, s in ((0, s0), (1, s1)):
        dx = g.dx[top[q], :] + mm(place[q], g.dxm_own[...])
        dx = dx + jnp.concatenate([g.dxb_own[32 * q : 32 * q + 32, :], jnp.zeros((16, D), F32)], 0)
        dx = dx * (1.0 - later * is_slot(s, TOP).astype(F32))
        g.dx[top[q], :] = dx
    for k in range(4):
        g.own[k] = g.dx[64 * k : 64 * k + 64, :].astype(BF)

    def msg(p, m, src, dst, to):
        return pltpu.make_async_remote_copy(src_ref=src, dst_ref=dst, send_sem=ssem.at[p, m], recv_sem=rsem.at[p, m],
                                            device_id=to, device_id_type=MESH)

    def send(p, m, src, dst, to):
        c = msg(p, m, src, dst, to)
        c.start()
        started.append(c)

    def arrived(p, m, dst):
        msg(p, m, dst, dst, sibling).wait_recv()

    stages = ((g.w1, g.relay1, g.in1, 192), (g.w2, g.relay2, g.in2, 48))

    def ring(p, phase):
        axis = ORDERS[p][phase]
        i = pos[axis]
        return i, device(along(pos, axis, 1), core), device(along(pos, axis, 3), core)

    def rs_a(p, phase):
        i, up, dn = ring(p, phase)
        w, relay, inn, n = stages[phase]
        b = 6 * phase

        def blk(k):
            return pl.ds(pl.multiple_of(((i + k) % 4) * n, 16), n)

        send(p, b + 0, w.at[p, blk(2), A], relay.at[p, 0], up)
        send(p, b + 1, w.at[p, blk(2), B], relay.at[p, 1], dn)
        send(p, b + 2, w.at[p, blk(1), B], inn.at[p, 0, :, B], up)
        send(p, b + 3, w.at[p, blk(3), A], inn.at[p, 1, :, A], dn)

    def rs_b(p, phase):
        i, up, dn = ring(p, phase)
        w, relay, inn, n = stages[phase]
        b = 6 * phase
        for side, by, cols, to in ((0, 1, A, up), (1, 3, B, dn)):
            first = ((i + by) % 4) * n
            arrived(p, b + side, relay.at[p, side])

            def add(j, _):
                s = pl.ds(pl.multiple_of(j * 16, 16), 16)
                t = pl.ds(pl.multiple_of(first + j * 16, 16), 16)
                relay[p, side, s, :] = (relay[p, side, s, :].astype(F32) + w[p, t, cols].astype(F32)).astype(BF)
                return 0

            lax.fori_loop(0, n // 16, add, 0)
            send(p, b + 4 + side, relay.at[p, side], inn.at[p, side, :, cols], to)

    def rs_c(p, phase):
        i, up, dn = ring(p, phase)
        w, relay, inn, n = stages[phase]
        b = 6 * phase
        arrived(p, b + 2, inn.at[p, 0, :, B])
        arrived(p, b + 3, inn.at[p, 1, :, A])
        arrived(p, b + 4, inn.at[p, 0, :, A])
        arrived(p, b + 5, inn.at[p, 1, :, B])

        def add(j, _):
            s = pl.ds(pl.multiple_of(j * 16, 16), 16)
            t = pl.ds(pl.multiple_of(i * n + j * 16, 16), 16)
            v = (w[p, t, :].astype(F32) + inn[p, 0, s, :].astype(F32) + inn[p, 1, s, :].astype(F32)).astype(BF)
            if phase == 0:
                g.w2[p, s, :] = v
            else:
                for k in range(4):
                    g.w3[p, k, s, :] = v[:, 384 * k : 384 * k + 384]
            return 0

        lax.fori_loop(0, n // 16, add, 0)

    def spot(p, c1, c2=None, c3=None, cols=None, c=None):
        o = out_ref.at[core if c is None else c, p]
        if c2 is None:
            rows = pl.ds(pl.multiple_of(192 * c1, 16), 192)
        else:
            rows = pl.ds(pl.multiple_of(192 * c1 + 48 * c2, 16), 48)
        if c3 is not None:
            cols = pl.ds(pl.multiple_of(384 * c3, 128), 384)
        return o.at[rows] if cols is None else o.at[rows, cols]

    def where(p):
        return tuple(pos[a] for a in ORDERS[p])

    def rs3_a(p):
        axis = ORDERS[p][2]
        for d in (1, 2, 3):
            send(p, 11 + d, g.w3.at[p, (pos[axis] + d) % 4], g.in3.at[p, d - 1], device(along(pos, axis, d), core))

    def rs3_b(p):
        axis = ORDERS[p][2]
        for d in (1, 2, 3):
            arrived(p, 11 + d, g.in3.at[p, d - 1])
        total = g.w3[p, pos[axis]].astype(F32)
        for d in range(3):
            total = total + g.in3[p, d].astype(F32)
        g.fin[p] = total.astype(BF)
        mine = spot(p, *where(p))
        own = pltpu.make_async_copy(g.fin.at[p], mine, lsem.at[7])
        own.start()
        for d in (1, 2, 3):
            send(p, 14 + d, g.fin.at[p], mine, device(along(pos, axis, d), core))
        own.wait()

    def ag3(p):
        c1, c2, c3 = where(p)
        for d in (1, 2, 3):
            arrived(p, 14 + d, spot(p, c1, c2, (c3 + 4 - d) % 4))

    def ag_a(p, phase):
        i, up, dn = ring(p, phase)
        c1, c2, _ = where(p)
        b = 18 if phase == 1 else 22
        mine = spot(p, c1, c2) if phase == 1 else spot(p, c1)
        send(p, b, mine, mine, up)
        send(p, b + 1, mine, mine, dn)
        if phase == 0:
            send(p, 26, mine, mine, sibling)

    def turned(p, phase):
        c1, c2, _ = where(p)

        def sp(d, cols=None):
            return spot(p, c1, (c2 + d) % 4, cols=cols) if phase == 1 else spot(p, (c1 + d) % 4, cols=cols)

        return sp

    def ag_b(p, phase):
        i, up, dn = ring(p, phase)
        b = 18 if phase == 1 else 22
        sp = turned(p, phase)
        arrived(p, b, sp(3))
        send(p, b + 2, sp(3, A), sp(3, A), up)
        if phase == 0:
            send(p, 27, sp(3), sp(3), sibling)
        arrived(p, b + 1, sp(1))
        send(p, b + 3, sp(1, B), sp(1, B), dn)
        if phase == 0:
            send(p, 28, sp(1), sp(1), sibling)

    def ag_c(p, phase):
        b = 18 if phase == 1 else 22
        sp = turned(p, phase)
        arrived(p, b + 2, sp(2, A))
        if phase == 0:
            send(p, 29, sp(2, A), sp(2, A), sibling)
        arrived(p, b + 3, sp(2, B))
        if phase == 0:
            send(p, 30, sp(2, B), sp(2, B), sibling)

    def sib(p):
        c1 = where(p)[0]

        def sp(d, cols=None):
            return spot(p, (c1 + d) % 4, cols=cols, c=1 - core)

        arrived(p, 26, sp(0))
        arrived(p, 27, sp(3))
        arrived(p, 28, sp(1))
        arrived(p, 29, sp(2, A))
        arrived(p, 30, sp(2, B))

    def own_a():
        for by in (1, 2, 3):
            c = pltpu.make_async_remote_copy(
                src_ref=g.own.at[(me + by) % 4], dst_ref=g.own_in.at[by - 1], send_sem=xs_send.at[2 + by],
                recv_sem=xs_recv.at[2 + by], device_id=device(along(pos, 1, by), core), device_id_type=MESH)
            c.start()
            started.append(c)

    def own_b():
        total = g.own[me].astype(F32)
        for by in (1, 2, 3):
            pltpu.make_async_remote_copy(
                src_ref=g.own_in.at[by - 1], dst_ref=g.own_in.at[by - 1], send_sem=xs_send.at[2 + by],
                recv_sem=xs_recv.at[2 + by], device_id=sibling, device_id_type=MESH).wait_recv()
            total = total + g.own_in[by - 1].astype(F32)
        g.own_sum[...] = total.astype(BF)
        mine = own_out.at[pl.ds(pl.multiple_of(64 * me, 16), 64)]
        here = pltpu.make_async_copy(g.own_sum, mine, lsem.at[6])
        here.start()
        for by in (1, 2, 3):
            c = pltpu.make_async_remote_copy(
                src_ref=g.own_sum, dst_ref=mine, send_sem=xs_send.at[5 + by],
                recv_sem=xs_recv.at[5 + by], device_id=device(along(pos, 1, by), core), device_id_type=MESH)
            c.start()
            started.append(c)
        return here

    def own_c(here):
        here.wait()
        for by in (1, 2, 3):
            src = own_out.at[pl.ds(pl.multiple_of(64 * ((me + 4 - by) % 4), 16), 64)]
            pltpu.make_async_remote_copy(
                src_ref=src, dst_ref=src, send_sem=xs_send.at[5 + by],
                recv_sem=xs_recv.at[5 + by], device_id=sibling, device_id_type=MESH).wait_recv()

    def small_send(stage):
        n = 1 if stage == 0 else 3
        first = 0 if stage == 0 else 3 * stage - 2
        for k in range(n):
            to = sibling if stage == 0 else device(along(pos, stage - 1, k + 1), core)
            c = pltpu.make_async_remote_copy(
                src_ref=g.small_out_v.at[stage], dst_ref=g.small_in.at[first + k], send_sem=xs_send.at[9 + first + k],
                recv_sem=xs_recv.at[9 + first + k], device_id=to, device_id_type=MESH)
            c.start()
            started.append(c)

    def small_take(stage):
        n = 1 if stage == 0 else 3
        first = 0 if stage == 0 else 3 * stage - 2
        total = g.small_out_v[stage]
        for k in range(n):
            ref = g.small_in.at[first + k]
            pltpu.make_async_remote_copy(
                src_ref=ref, dst_ref=ref, send_sem=xs_send.at[9 + first + k],
                recv_sem=xs_recv.at[9 + first + k], device_id=sibling, device_id_type=MESH).wait_recv()
            total = total + g.small_in[first + k]
        g.small_out_v[stage + 1] = total

    g.small_out_v[0] = g.sums[...]
    small_send(0)
    act_local.wait()
    act_go.wait_recv()
    dh_go.wait_recv()
    for k in range(2):
        g.w1[2, :, 768 * k : 768 * k + 768] = mm_tn(g.f_act[:, 768 * k : 768 * k + 768], g.f_dh[...]).astype(BF)
    rs_a(2, 0)
    du_local.wait()
    du_go.wait_recv()
    n2_go.wait_recv()
    for k in range(2):
        g.w1[1, :, 768 * k : 768 * k + 768] = mm_tn(g.f_n2[...], g.f_du[:, 768 * k : 768 * k + 768]).astype(BF)
    rs_a(1, 0)
    for c in (dq_local, da_local):
        c.wait()
    for c in (dq_go, da_go, n1_go, o_go):
        c.wait_recv()
    g.w1[0, :, 1152:1536] = mm_tn(g.f_o[...], g.f_qo[:, 1152:1536]).astype(BF)
    g.w1[0, :, 0:768] = mm_tn(g.f_n1[...], g.f_qo[:, 0:768]).astype(BF)
    g.w1[0, :, 768:1152] = mm_tn(g.f_n1[...], g.f_qo[:, 768:1152]).astype(BF)
    rs_a(0, 0)
    own_a()
    small_take(0)
    small_send(1)
    T = (2, 1, 0)
    for p in T:
        rs_b(p, 0)
    small_take(1)
    small_send(2)
    for p in T:
        rs_c(p, 0)
        rs_a(p, 1)
    small_take(2)
    small_send(3)
    here = own_b()
    for p in T:
        rs_b(p, 1)
    for p in T:
        rs_c(p, 1)
        rs3_a(p)
    small_take(3)
    small_copy = pltpu.make_async_copy(g.small_out_v.at[4], small_out, lsem.at[8])
    small_copy.start()
    for p in T:
        rs3_b(p)
    own_c(here)
    for p in T:
        ag3(p)
        ag_a(p, 1)
    for p in T:
        ag_b(p, 1)
    for p in T:
        ag_c(p, 1)
        ag_a(p, 0)
    for p in T:
        ag_b(p, 0)
    for p in T:
        ag_c(p, 0)
    for p in T:
        sib(p)
    act_copy.wait()
    small_copy.wait()
    for c in started:
        c.wait_send()


SCRATCH["small_out_v"] = ((5, 16, D), F32)
NAMES.append("small_out_v")


def passes(starts, lengths, x, cot, par, wq, wo, wu, wd):
    smem = pl.BlockSpec(memory_space=pltpu.SMEM)
    hbm = pl.BlockSpec(memory_space=pl.ANY)
    dma = pltpu.SemaphoreType.DMA
    return pl.pallas_call(
        kernel,
        out_shape=[
            jax.ShapeDtypeStruct((ROWS, D), BF),
            jax.ShapeDtypeStruct((ROWS, D), BF),
            jax.ShapeDtypeStruct((16, D), F32),
            jax.ShapeDtypeStruct((2, 3, 768, 1536), BF),
        ],
        in_specs=[smem, smem] + [hbm] * 7,
        out_specs=[hbm] * 4,
        scratch_shapes=[pltpu.VMEM(s, t) for s, t in SCRATCH.values()]
        + [dma((9,)), dma((8,)), dma((8,)), dma((3, NMSG)), dma((3, NMSG)), dma((19,)), dma((19,))],
        compiler_params=pltpu.CompilerParams(
            collective_id=0, has_side_effects=True, vmem_limit_bytes=60 * 2**20
        ),
        name="passes",
    )(starts, lengths, x, cot, par, wq, wo, wu, wd)


def widen_kernel(all_ref, gq, go, gu, gd):
    for c in range(2):
        gq[:, 1152 * c : 1152 * c + 1152] = all_ref[c, 0, :, 0:1152].astype(F32)
        go[:, 384 * c : 384 * c + 384] = all_ref[c, 0, :, 1152:1536].astype(F32)
        gu[:, 1536 * c : 1536 * c + 1536] = all_ref[c, 1].astype(F32)
        for k in range(2):
            gd[2 * c + k] = all_ref[c, 2, :, 768 * k : 768 * k + 768].astype(F32)


def widen(gathered):
    n = 96
    return pl.pallas_call(
        widen_kernel,
        grid=(768 // n,),
        in_specs=[pl.BlockSpec((2, 3, n, 1536), lambda i: (0, 0, i, 0))],
        out_specs=[
            pl.BlockSpec((n, 2304), lambda i: (i, 0)),
            pl.BlockSpec((n, 768), lambda i: (i, 0)),
            pl.BlockSpec((n, 3072), lambda i: (i, 0)),
            pl.BlockSpec((4, n, 768), lambda i: (0, i, 0)),
        ],
        out_shape=[
            jax.ShapeDtypeStruct((768, 2304), F32),
            jax.ShapeDtypeStruct((768, 768), F32),
            jax.ShapeDtypeStruct((768, 3072), F32),
            jax.ShapeDtypeStruct((4, 768, 768), F32),
        ],
        compiler_params=pltpu.CompilerParams(vmem_limit_bytes=40 * 2**20),
        name="widen",
    )(gathered)


def on_device(embedded, cotangent, lengths, starts, ln1_gain, ln1_shift, w_qkv, b_qv, w_out, b_out,
              ln2_gain, ln2_shift, w_up, b_up, w_down, b_down):
    par = jnp.concatenate(
        [ln1_gain, ln1_shift, b_qv, b_out, ln2_gain, ln2_shift, b_up, b_down, jnp.zeros((4 * D,), F32)]
    ).reshape(16, D)
    act, own, small, gathered = passes(
        starts, lengths, embedded.reshape(ROWS, D), cotangent.reshape(ROWS, D), par, w_qkv, w_out, w_up, w_down
    )
    gq, go, gu, gd = widen(gathered)
    return (
        act.reshape(1, 2, 128, D),
        own.reshape(2, 128, D),
        small[LN1G],
        small[LN1S],
        gq,
        small[BQV : BQV + 2].reshape(2 * D),
        go,
        small[BOUT],
        small[LN2G],
        small[LN2S],
        gu,
        small[BUP : BUP + 4].reshape(FF),
        gd.reshape(FF, D),
        small[BDOWN],
    )


def solution(mesh):
    rows = P("batch", None, None)
    passes_rows = P("pass", "batch", None, None)
    return jax.shard_map(
        on_device,
        mesh=mesh,
        in_specs=(rows, passes_rows, P("batch"), P("batch")) + (P(),) * 12,
        out_specs=(passes_rows, rows) + (P(),) * 12,
        check_vma=False,
    )
```

time: 876 us -> 176 us (0.20)
  matrix products: 242 us -> 0 us
  waiting for transfers between devices: 225 us -> 0 us
  Pallas kernels: 0 us -> 158 us
  other arithmetic: 136 us -> 0.01 us
  local copies, waits for them, and re-layouts: 113 us -> 17.1 us
  blocking collectives: 73.1 us -> 0 us
  loops' own time: 45.9 us -> 0 us
  starting transfers between devices: 21.8 us -> 0 us
  between operations: 14.3 us -> 0.67 us
    dot_general x95 -> x0, matrix products: 242 us -> none  [the longest x5 54.8 us: backward(): jnp.einsum('bli,bld->id', active, grad_branch, preferred_element_type=jnp...]
    psum x2 -> x0, waiting for transfers between devices: 224 us -> none  [the longest x1 224 us: on_device(): summed = lax.psum(grads, ('batch', 'pass'))]
    pallas_call x0 -> x2, Pallas kernels: none -> 158 us  [the longest x1 148 us: passes(): pl.pallas_call(kernel, out_shape=[jax.ShapeDtypeStruct((ROWS, D), BF), ja...]
    psum x1 -> x0, blocking collectives: 73.1 us -> none  [on_device(): summed = lax.psum(grads, ('batch', 'pass'))]
    select_n x60 -> x0, other arithmetic: 47.8 us -> none  [the longest x40 33.6 us: forward_turn(): jnp.where(in_range, lax.dynamic_update_slice_in_dim(whole_buf, piece, ite...]
    another operation x2 -> x0, loops' own time: 45.9 us -> none  [the longest x1 24.6 us: on_device(): lax.fori_loop(0, round_count, backward_turn, state)]
    reduce_sum x55 -> x0, other arithmetic: 36.5 us -> none  [the longest x10 11.3 us: layer_norm(): centered = field - row_mean]
    dynamic_slice x30 -> x0, local copies, waits for them, and re-layouts: 26.7 us -> none  [the longest x5 6.96 us: backward_turn(): starting_entry = lax.dynamic_slice_in_dim(starts, item_index, 1, 0)]
  transfers between devices with their start and end apart: 12 -> 0, of which waited for: 1 -> 0; matrix products, arithmetic and copies ran while one was open for 17% -> 0% of each run, Pallas kernels for 0% -> 0%
where the time goes in v2:
time: 176 us
  Pallas kernels  158 us (90%)
  local copies, waits for them, and re-layouts  17.1 us (10%)
    pallas_call x1, Pallas kernels, passes(): pl.pallas_call(kernel, out_shape=[jax.ShapeDtypeStruct((ROWS, D), BF), ja...  148 us
    unnamed x16, local copies, waits for them, and re-layouts  12.1 us
    pallas_call x1, Pallas kernels, widen(): pl.pallas_call(widen_kernel, grid=(768 // n,), in_specs=[pl.BlockSpec((2,...  9.66 us

profile of v2, /device:TPU:1, one launch (start us, length us, event | category | flops | bytes accessed | tf_op | source)
XLA Modules:
  0.0 175.7 jit_solution(9611275791372772693)
XLA Ops:
  0.7 0.7 constant_dynamic-update-slice_fusion.7
  1.3 0.7 constant_dynamic-update-slice_fusion.6
  2.0 0.7 constant_dynamic-update-slice_fusion.5
  2.7 0.7 constant_dynamic-update-slice_fusion.4
  3.4 0.7 constant_dynamic-update-slice_fusion.3
  4.1 0.7 constant_dynamic-update-slice_fusion.2
  4.8 0.7 constant_dynamic-update-slice_fusion.1
  5.5 0.7 constant_dynamic-update-slice_fusion
  6.2 0.6 reshape.54.par_hbm
  6.9 148.3 %passes.1 = (bf16[256,768]{1,0:T(8,128)(2,1)}, bf16[256,768]{1,0:T(8,128)(2,1)}, f32[16,768]{1,0:T(8,128)}, bf16[2,3,768,1536]{3,2,1,0:T(8,128)(2,1)}) custom-call(s32[2]{0:T(128)} %start_ref.1, s32[2]{0:T(128)} %length_ref.1, bf16[256,768]{1,0:T(8,128)(2,1)} %bitcast.7, bf16[256,768]{1,0:T(8,128)(2,1)} %bitcast.8, f32[16,768]{1,0:T(8,128)} %reshape.54.par_hbm, ...), custom_call_target="tpu_custom_call" | custom-call | tf_op jit(solution)/shard_map/passes/pallas_call | solution.py:811
  155.2 0.7 slice.26
  155.9 0.6 reshape.57
  156.5 0.8 slice.30
  157.3 1.6 slice_reduce_fusion
  158.9 0.6 reshape.58
  159.5 0.0 copy-start
  159.5 5.0 %copy-done = bf16[2,3,768,1536]{3,2,1,0:T(8,128)(2,1)S(1)} copy-done((bf16[2,3,768,1536]{3,2,1,0:T(8,128)(2,1)S(1)}, bf16[2,3,768,1536]{3,2,1,0:T(8,128)(2,1)}, u32[]{:S(2)}) %copy-start) | copy-done | bytes 14155800
  164.5 0.0 copy-start.2
  164.5 0.0 copy-start.1
  164.5 9.7 %widen.1 = (f32[768,2304]{1,0:T(8,128)}, f32[768,768]{1,0:T(8,128)}, f32[768,3072]{1,0:T(8,128)}, f32[4,768,768]{2,1,0:T(8,128)}) custom-call(bf16[2,3,768,1536]{3,2,1,0:T(8,128)(2,1)S(1)} %copy-done), custom_call_target="tpu_custom_call" | custom-call | tf_op jit(solution)/shard_map/widen/pallas_call | solution.py:841
  174.2 0.0 copy-done.2
  174.2 0.7 copy.41
  175.0 0.0 copy-done.1
  175.0 0.7 copy.42
  (2 shorter events, 0.0 us)
Async XLA Ops:
  159.5 5.0 %copy-start = (bf16[2,3,768,1536]{3,2,1,0:T(8,128)(2,1)S(1)}, bf16[2,3,768,1536]{3,2,1,0:T(8,128)(2,1)}, u32[]{:S(2)}) copy-start(bf16[2,3,768,1536]{3,2,1,0:T(8,128)(2,1)} %get-tuple-element.25.all_ref) | copy-start | bytes 42467332
  164.5 9.7 %copy-start.2 = (bf16[256,768]{1,0:T(8,128)(2,1)S(1)}, bf16[256,768]{1,0:T(8,128)(2,1)}, u32[]{:S(2)}) copy-start(bf16[256,768]{1,0:T(8,128)(2,1)} %get-tuple-element.22) | copy-start | bytes 1179652
  164.5 10.4 %copy-start.1 = (bf16[256,768]{1,0:T(8,128)(2,1)S(1)}, bf16[256,768]{1,0:T(8,128)(2,1)}, u32[]{:S(2)}) copy-start(bf16[256,768]{1,0:T(8,128)(2,1)} %get-tuple-element.23) | copy-start | bytes 1179652

commit v3 on v2

--- a/solution.py
+++ b/solution.py
@@ -20,9 +20,10 @@
 LN1G, LN1S, BQV, BOUT, LN2G, LN2S, BUP, BDOWN = 0, 1, 2, 4, 5, 6, 7, 11
 
 ORDERS = ((0, 1, 2), (1, 2, 0), (2, 0, 1))
-NMSG = 31
-A = pl.ds(0, 768)
-B = pl.ds(768, 768)
+NMSG = 30
+WAVES = 3
+SHAPES = ((512, 768), (768, 512), (768, 512))
+SUBS = ((16, 384), (48, 128), (48, 128))
 
 
 def mm(a, b):
@@ -116,14 +117,12 @@
 
 
 SCRATCH = dict(
-    x_v=((ROWS, D), BF),
-    wq=((D, 3 * D), BF), wo=((D, D), BF), wu=((D, FF), BF), wd=((FF, D), BF),
-    par=((16, D), F32),
+        par=((16, D), F32),
     xh1=((ROWS, D), F32), rs1=((ROWS, 1), F32), qkv=((ROWS, 3 * D), BF),
     prob=((12, 256, 128), F32), res=((ROWS, D), F32), xh2=((ROWS, D), F32), rs2=((ROWS, 1), F32),
     gp=((ROWS, FF), F32), act=((ROWS, FF), BF),
     tmp=((ROWS, D), F32), dmix=((ROWS, D), BF),
-    du=((ROWS, FF), BF), da=((ROWS, D), BF), dqkv=((ROWS, 3 * D), BF), sums=((16, D), F32),
+    du=((ROWS, FF), BF), dqo=((ROWS, FF), BF), sums=((16, D), F32),
     xm=((4, 16, D), F32), xh1m=((4, 16, D), F32), rs1m=((4, 16, 1), F32), qkvm=((4, 16, 3 * D), BF),
     kall=((3, 128, D), BF), vall=((3, 128, D), BF), pm=((3, 192, 128), F32),
     xh2m=((3, 16, D), F32), rs2m=((3, 16, 1), F32), gpm=((3, 16, FF), F32),
@@ -132,20 +131,27 @@
     dx_mini=((16, D), F32), dxm_own=((16, D), BF), dxb_own=((64, D), F32),
     f_n1=((512, D), BF), f_o=((512, D), BF), f_n2=((512, D), BF), f_dh=((512, D), BF),
     f_qo=((512, 1536), BF), f_du=((512, 1536), BF), f_act=((512, 1536), BF),
-    w1=((3, 768, 1536), BF), relay1=((3, 2, 192, 768), BF), in1=((3, 2, 192, 1536), BF),
-    w2=((3, 192, 1536), BF), relay2=((3, 2, 48, 768), BF), in2=((3, 2, 48, 1536), BF),
-    w3=((3, 4, 48, 384), BF), in3=((3, 3, 48, 384), BF), fin=((3, 48, 384), BF),
-    own=((4, 64, D), BF), own_in=((3, 64, D), BF), own_sum=((64, D), BF),
+    w1_0=((3, 512, 768), BF), w1_1=((3, 768, 512), BF), w1_2=((3, 768, 512), BF),
+    relay_0=((3, 2, 128, 384), BF), relay_1=((3, 2, 192, 256), BF), relay_2=((3, 2, 192, 256), BF),
+    in1_0=((3, 2, 128, 768), BF), in1_1=((3, 2, 192, 512), BF), in1_2=((3, 2, 192, 512), BF),
+    w2_0=((3, 128, 768), BF), w2_1=((3, 192, 512), BF), w2_2=((3, 192, 512), BF),
+    in2_0=((3, 3, 32, 768), BF), in2_1=((3, 3, 48, 512), BF), in2_2=((3, 3, 48, 512), BF),
+    w3_0=((3, 32, 768), BF), w3_1=((3, 48, 512), BF), w3_2=((3, 48, 512), BF),
+    in3_0=((3, 3, 16, 384), BF), in3_1=((3, 3, 48, 128), BF), in3_2=((3, 3, 48, 128), BF),
+    own=((4, 64, D), BF), own_in=((3, 64, D), BF),
     small_in=((10, 16, D), F32),
 )
 NAMES = list(SCRATCH)
 
 
-def kernel(start_ref, length_ref, x_hbm, cot_hbm, par_hbm, wq_hbm, wo_hbm, wu_hbm, wd_hbm,
-           act_out, own_out, small_out, out_ref, *scratch):
+def kernel(start_ref, length_ref, x_hbm, cot_hbm, ln1g_hbm, ln1s_hbm, wq_hbm, bqv_hbm, wo_hbm, bout_hbm, ln2g_hbm, ln2s_hbm,
+           wu_hbm, bup_hbm, wd_hbm, bdown_hbm, x_v, own_out, small_out, w_qo, w_u, w_d, *scratch):
     r = dict(zip(NAMES, scratch))
     lsem, fsem, frem, ssem, rsem, xs_send, xs_recv = scratch[len(NAMES):]
     g = type("Refs", (), r)
+    g.x_v, g.wu, g.wd = x_v, w_u, w_d
+    g.wq, g.wo = w_qo.at[:, pl.ds(0, 3 * D)], w_qo.at[:, pl.ds(3 * D, D)]
+    g.dqkv, g.da = g.dqo.at[:, pl.ds(0, 3 * D)], g.dqo.at[:, pl.ds(3 * D, D)]
     g.dx, g.dres, g.dn1, g.out_act = g.res, g.tmp, g.xh2, g.x_v
     g.cot_v = g.f_dh.at[pl.ds(0, 256)]
     pos, core = coords()
@@ -158,14 +164,19 @@
             pl.semaphore_signal(barrier, inc=1, device_id=device(along(pos, axis, by), core), device_id_type=MESH)
     pl.semaphore_signal(barrier, inc=1, device_id=sibling, device_id_type=MESH)
 
-    loads = [
-        pltpu.make_async_copy(src, dst, lsem.at[i])
-        for i, (src, dst) in enumerate(
-            ((x_hbm, g.x_v), (par_hbm, g.par), (wq_hbm, g.wq), (wo_hbm, g.wo), (wu_hbm, g.wu), (wd_hbm, g.wd), (cot_hbm, g.cot_v))
-        )
-    ]
-    for c in loads:
+    def load(i, src, dst):
+        c = pltpu.make_async_copy(src, dst, lsem.at[i])
         c.start()
+        return c
+
+    vectors = ((ln1g_hbm, LN1G), (ln1s_hbm, LN1S), (bqv_hbm, BQV), (bout_hbm, BOUT), (ln2g_hbm, LN2G), (ln2s_hbm, LN2S),
+               (bup_hbm, BUP), (bdown_hbm, BDOWN))
+    x_load = load(0, x_hbm, g.x_v)
+    par_loads = []
+    for src, first in vectors:
+        for k in range(src.shape[0] // D):
+            par_loads.append(load(9 + first + k, src.at[pl.ds(k * D, D)], g.par.at[first + k]))
+    wq_load = load(2, wq_hbm, g.wq)
 
     def row(i, n=1):
         if n == 1:
@@ -191,8 +202,9 @@
         j = iota((rows, 1), 0)
         return (j >= s) & (j < s + 6)
 
-    loads[0].wait()
-    loads[1].wait()
+    x_load.wait()
+    for c in par_loads:
+        c.wait()
 
     def norm_one(i, _):
         rows = pl.ds(pl.multiple_of(i * 32, 32), 32)
@@ -202,8 +214,10 @@
         g.f_n1[rows, :] = (xhat * row(LN1G) + row(LN1S)).astype(BF)
         return 0
 
+    w_loads = [load(3, wo_hbm, g.wo), load(4, wu_hbm, g.wu), load(5, wd_hbm, g.wd)]
+    cot_load = load(6, cot_hbm, g.cot_v)
     lax.fori_loop(0, 8, norm_one, 0)
-    loads[2].wait()
+    wq_load.wait()
     qkv_bias = (row(BQV), jnp.zeros((1, D), F32), row(BQV + 1))
     for k in range(3):
         c = slice(k * D, (k + 1) * D)
@@ -220,7 +234,7 @@
             buf[t, 0:32, :] = g.qkv[0:32, lane : lane + D]
             buf[t, 32:64, :] = g.qkv[128:160, lane : lane + D]
             buf[t, 80:128, :] = jnp.zeros((48, D), BF)
-    for c in loads[3:6]:
+    for c in w_loads:
         c.wait()
 
     rr = iota((192, 128), 0) % 16
@@ -317,8 +331,6 @@
         g.gp[:, c] = slope
         g.act[:, c] = m.astype(BF)
     g.out_act[...] = (g.res[...] + mm(g.act[...], g.wd[...]) + row(BDOWN)).astype(BF)
-    act_copy = pltpu.make_async_copy(g.out_act, act_out, lsem.at[0])
-    act_copy.start()
 
     pl.semaphore_wait(barrier, 10)
     lo, hi = pl.ds(0, 256), pl.ds(256, 256)
@@ -345,7 +357,7 @@
     act_go = to_sibling(3, half(g.act, 1 - core, 1536), g.f_act.at[hi])
     act_local = local(1, half(g.act, core, 1536), g.f_act.at[lo])
 
-    loads[6].wait()
+    cot_load.wait()
     for k in range(4):
         c = slice(k * D, (k + 1) * D)
         du = (mm_nt(g.cot_v[...], g.wd[c, :]) * g.gp[:, c]).astype(BF)
@@ -500,10 +512,8 @@
         merge(g.da, g.da_own, q)
         base = jnp.concatenate([g.dqkv_own[32 * q : 32 * q + 32, :].astype(F32), jnp.zeros((16, 3 * D), F32)], 0)
         g.dqkv[top[q], :] = (g.dqkv[top[q], :].astype(F32) + mm(place[q], g.dqkv_own[64:80, :]) + base).astype(BF)
-    dq_go = to_sibling(6, half(g.dqkv, 1 - core, 1152), g.f_qo.at[hi, pl.ds(0, 1152)])
-    dq_local = local(4, half(g.dqkv, core, 1152), g.f_qo.at[lo, pl.ds(0, 1152)])
-    da_go = to_sibling(7, half(g.da, 1 - core, 384), g.f_qo.at[hi, pl.ds(1152, 384)])
-    da_local = local(5, half(g.da, core, 384), g.f_qo.at[lo, pl.ds(1152, 384)])
+    dq_go = to_sibling(6, half(g.dqo, 1 - core, 1536), g.f_qo.at[hi])
+    dq_local = local(4, half(g.dqo, core, 1536), g.f_qo.at[lo])
     later = (me > 0).astype(F32)
     for q, s in ((0, s0), (1, s1)):
         dx = g.dx[top[q], :] + mm(place[q], g.dxm_own[...])
@@ -513,167 +523,209 @@
     for k in range(4):
         g.own[k] = g.dx[64 * k : 64 * k + 64, :].astype(BF)
 
-    def msg(p, m, src, dst, to):
-        return pltpu.make_async_remote_copy(src_ref=src, dst_ref=dst, send_sem=ssem.at[p, m], recv_sem=rsem.at[p, m],
+    def msg(w, k, m, src, dst, to):
+        i = 3 * w + k
+        return pltpu.make_async_remote_copy(src_ref=src, dst_ref=dst, send_sem=ssem.at[i, m], recv_sem=rsem.at[i, m],
                                             device_id=to, device_id_type=MESH)
 
-    def send(p, m, src, dst, to):
-        c = msg(p, m, src, dst, to)
+    def send(w, k, m, src, dst, to):
+        c = msg(w, k, m, src, dst, to)
         c.start()
         started.append(c)
 
-    def arrived(p, m, dst):
-        msg(p, m, dst, dst, sibling).wait_recv()
-
-    stages = ((g.w1, g.relay1, g.in1, 192), (g.w2, g.relay2, g.in2, 48))
-
-    def ring(p, phase):
-        axis = ORDERS[p][phase]
-        i = pos[axis]
-        return i, device(along(pos, axis, 1), core), device(along(pos, axis, 3), core)
-
-    def rs_a(p, phase):
-        i, up, dn = ring(p, phase)
-        w, relay, inn, n = stages[phase]
-        b = 6 * phase
-
-        def blk(k):
-            return pl.ds(pl.multiple_of(((i + k) % 4) * n, 16), n)
-
-        send(p, b + 0, w.at[p, blk(2), A], relay.at[p, 0], up)
-        send(p, b + 1, w.at[p, blk(2), B], relay.at[p, 1], dn)
-        send(p, b + 2, w.at[p, blk(1), B], inn.at[p, 0, :, B], up)
-        send(p, b + 3, w.at[p, blk(3), A], inn.at[p, 1, :, A], dn)
-
-    def rs_b(p, phase):
-        i, up, dn = ring(p, phase)
-        w, relay, inn, n = stages[phase]
-        b = 6 * phase
-        for side, by, cols, to in ((0, 1, A, up), (1, 3, B, dn)):
+    def arrived(w, k, m, dst):
+        msg(w, k, m, dst, dst, sibling).wait_recv()
+
+    w1s, relays, in1s = (g.w1_0, g.w1_1, g.w1_2), (g.relay_0, g.relay_1, g.relay_2), (g.in1_0, g.in1_1, g.in1_2)
+    w2s, in2s = (g.w2_0, g.w2_1, g.w2_2), (g.in2_0, g.in2_1, g.in2_2)
+    w3s, in3s = (g.w3_0, g.w3_1, g.w3_2), (g.in3_0, g.in3_1, g.in3_2)
+    outs = (w_d, w_u, w_qo)
+
+    def ds(i, n, m):
+        return pl.ds(pl.multiple_of(i, m), n)
+
+    def place_of(k, phase):
+        axis = ORDERS[k][phase]
+        return pos[axis], lambda by: device(along(pos, axis, by), core)
+
+    def dims(w):
+        n, c = SHAPES[w]
+        return n // 4, n // 16, c, ds(0, c // 2, 128), ds(c // 2, c // 2, 128)
+
+    def rs1a(w, k):
+        i, to = place_of(k, 0)
+        n, _, _, A, B = dims(w)
+        w1, relay, inn = w1s[w].at[k], relays[w].at[k], in1s[w].at[k]
+
+        def blk(by):
+            return ds(((i + by) % 4) * n, n, 16)
+
+        send(w, k, 0, w1.at[blk(2), A], relay.at[0], to(1))
+        send(w, k, 1, w1.at[blk(2), B], relay.at[1], to(3))
+        send(w, k, 2, w1.at[blk(1), B], inn.at[0, :, B], to(1))
+        send(w, k, 3, w1.at[blk(3), A], inn.at[1, :, A], to(3))
+
+    def rs1b(w, k):
+        i, to = place_of(k, 0)
+        n, _, _, A, B = dims(w)
+        w1, relay, inn = w1s[w], relays[w], in1s[w]
+        for side, by, cols in ((0, 1, A), (1, 3, B)):
             first = ((i + by) % 4) * n
-            arrived(p, b + side, relay.at[p, side])
+            arrived(w, k, side, relay.at[k, side])
 
             def add(j, _):
-                s = pl.ds(pl.multiple_of(j * 16, 16), 16)
-                t = pl.ds(pl.multiple_of(first + j * 16, 16), 16)
-                relay[p, side, s, :] = (relay[p, side, s, :].astype(F32) + w[p, t, cols].astype(F32)).astype(BF)
+                s = ds(j * 16, 16, 16)
+                t = ds(first + j * 16, 16, 16)
+                relay[k, side, s, :] = (relay[k, side, s, :].astype(F32) + w1[k, t, cols].astype(F32)).astype(BF)
                 return 0
 
             lax.fori_loop(0, n // 16, add, 0)
-            send(p, b + 4 + side, relay.at[p, side], inn.at[p, side, :, cols], to)
-
-    def rs_c(p, phase):
-        i, up, dn = ring(p, phase)
-        w, relay, inn, n = stages[phase]
-        b = 6 * phase
-        arrived(p, b + 2, inn.at[p, 0, :, B])
-        arrived(p, b + 3, inn.at[p, 1, :, A])
-        arrived(p, b + 4, inn.at[p, 0, :, A])
-        arrived(p, b + 5, inn.at[p, 1, :, B])
+            send(w, k, 4 + side, relay.at[k, side], inn.at[k, side, :, cols], to(by))
+
+    def rs1c(w, k):
+        i, _ = place_of(k, 0)
+        n, _, _, A, B = dims(w)
+        w1, inn, w2 = w1s[w], in1s[w], w2s[w]
+        arrived(w, k, 2, inn.at[k, 0, :, B])
+        arrived(w, k, 3, inn.at[k, 1, :, A])
+        arrived(w, k, 4, inn.at[k, 0, :, A])
+        arrived(w, k, 5, inn.at[k, 1, :, B])
 
         def add(j, _):
-            s = pl.ds(pl.multiple_of(j * 16, 16), 16)
-            t = pl.ds(pl.multiple_of(i * n + j * 16, 16), 16)
-            v = (w[p, t, :].astype(F32) + inn[p, 0, s, :].astype(F32) + inn[p, 1, s, :].astype(F32)).astype(BF)
-            if phase == 0:
-                g.w2[p, s, :] = v
+            s = ds(j * 16, 16, 16)
+            t = ds(i * n + j * 16, 16, 16)
+            w2[k, s, :] = (w1[k, t, :].astype(F32) + inn[k, 0, s, :].astype(F32) + inn[k, 1, s, :].astype(F32)).astype(BF)
+            return 0
+
+        lax.fori_loop(0, n // 16, add, 0)
+
+    def rs2a(w, k):
+        i, to = place_of(k, 1)
+        _, n, _, _, _ = dims(w)
+        for d in (1, 2, 3):
+            send(w, k, 5 + d, w2s[w].at[k, ds(((i + d) % 4) * n, n, 16)], in2s[w].at[k, d - 1], to(d))
+
+    def rs2b(w, k):
+        i, _ = place_of(k, 1)
+        _, n, _, _, _ = dims(w)
+        for d in (1, 2, 3):
+            arrived(w, k, 5 + d, in2s[w].at[k, d - 1])
+        total = w2s[w][k, ds(i * n, n, 16), :].astype(F32)
+        for d in range(3):
+            total = total + in2s[w][k, d].astype(F32)
+        w3s[w][k] = total.astype(BF)
+
+    def sub(w, j):
+        n, c = SUBS[w]
+        if w == 0:
+            return ds((j // 2) * n, n, 16), ds((j % 2) * c, c, 128)
+        return slice(None), ds(j * c, c, 128)
+
+    def rs3a(w, k):
+        i, to = place_of(k, 2)
+        for d in (1, 2, 3):
+            rows, cols = sub(w, (i + d) % 4)
+            send(w, k, 8 + d, w3s[w].at[k, rows, cols], in3s[w].at[k, d - 1], to(d))
+
+    def spot(w, k, c1, c2=None, c3=None, cols=None, c=None):
+        c = core if c is None else c
+        n1, n2, width, _, _ = dims(w)
+        r0, l0 = (c * 1536 + 512 * k, 0) if w == 0 else (0, c * 1536 + 512 * k)
+        r0 = r0 + n1 * c1
+        n = n1
+        if c2 is not None:
+            r0 = r0 + n2 * c2
+            n = n2
+        if c3 is not None:
+            n, width = SUBS[w]
+            if w == 0:
+                r0, l0 = r0 + n * (c3 // 2), l0 + width * (c3 % 2)
             else:
-                for k in range(4):
-                    g.w3[p, k, s, :] = v[:, 384 * k : 384 * k + 384]
-            return 0
-
-        lax.fori_loop(0, n // 16, add, 0)
-
-    def spot(p, c1, c2=None, c3=None, cols=None, c=None):
-        o = out_ref.at[core if c is None else c, p]
-        if c2 is None:
-            rows = pl.ds(pl.multiple_of(192 * c1, 16), 192)
-        else:
-            rows = pl.ds(pl.multiple_of(192 * c1 + 48 * c2, 16), 48)
-        if c3 is not None:
-            cols = pl.ds(pl.multiple_of(384 * c3, 128), 384)
-        return o.at[rows] if cols is None else o.at[rows, cols]
-
-    def where(p):
-        return tuple(pos[a] for a in ORDERS[p])
-
-    def rs3_a(p):
-        axis = ORDERS[p][2]
+                l0 = l0 + width * c3
+        elif cols is not None:
+            width = width // 2
+            l0 = l0 + width * cols
+        return outs[w].at[ds(r0, n, 16), ds(l0, width, 128)]
+
+    def at(k):
+        return tuple(pos[a] for a in ORDERS[k])
+
+    def rs3b(w, k):
+        i, to = place_of(k, 2)
         for d in (1, 2, 3):
-            send(p, 11 + d, g.w3.at[p, (pos[axis] + d) % 4], g.in3.at[p, d - 1], device(along(pos, axis, d), core))
-
-    def rs3_b(p):
-        axis = ORDERS[p][2]
+            arrived(w, k, 8 + d, in3s[w].at[k, d - 1])
+        rows, cols = sub(w, i)
+        total = w3s[w][k, rows, cols].astype(F32)
+        for d in range(3):
+            total = total + in3s[w][k, d].astype(F32)
+        mine = spot(w, k, *at(k))
+        mine[...] = total.astype(BF)
         for d in (1, 2, 3):
-            arrived(p, 11 + d, g.in3.at[p, d - 1])
-        total = g.w3[p, pos[axis]].astype(F32)
-        for d in range(3):
-            total = total + g.in3[p, d].astype(F32)
-        g.fin[p] = total.astype(BF)
-        mine = spot(p, *where(p))
-        own = pltpu.make_async_copy(g.fin.at[p], mine, lsem.at[7])
-        own.start()
+            send(w, k, 11 + d, mine, mine, to(d))
+
+    def ag3b(w, k):
+        c1, c2, c3 = at(k)
         for d in (1, 2, 3):
-            send(p, 14 + d, g.fin.at[p], mine, device(along(pos, axis, d), core))
-        own.wait()
-
-    def ag3(p):
-        c1, c2, c3 = where(p)
+            arrived(w, k, 11 + d, spot(w, k, c1, c2, (c3 + 4 - d) % 4))
+
+    def ag2a(w, k):
+        c1, c2, _ = at(k)
+        _, to = place_of(k, 1)
+        mine = spot(w, k, c1, c2)
         for d in (1, 2, 3):
-            arrived(p, 14 + d, spot(p, c1, c2, (c3 + 4 - d) % 4))
-
-    def ag_a(p, phase):
-        i, up, dn = ring(p, phase)
-        c1, c2, _ = where(p)
-        b = 18 if phase == 1 else 22
-        mine = spot(p, c1, c2) if phase == 1 else spot(p, c1)
-        send(p, b, mine, mine, up)
-        send(p, b + 1, mine, mine, dn)
-        if phase == 0:
-            send(p, 26, mine, mine, sibling)
-
-    def turned(p, phase):
-        c1, c2, _ = where(p)
-
-        def sp(d, cols=None):
-            return spot(p, c1, (c2 + d) % 4, cols=cols) if phase == 1 else spot(p, (c1 + d) % 4, cols=cols)
-
-        return sp
-
-    def ag_b(p, phase):
-        i, up, dn = ring(p, phase)
-        b = 18 if phase == 1 else 22
-        sp = turned(p, phase)
-        arrived(p, b, sp(3))
-        send(p, b + 2, sp(3, A), sp(3, A), up)
-        if phase == 0:
-            send(p, 27, sp(3), sp(3), sibling)
-        arrived(p, b + 1, sp(1))
-        send(p, b + 3, sp(1, B), sp(1, B), dn)
-        if phase == 0:
-            send(p, 28, sp(1), sp(1), sibling)
-
-    def ag_c(p, phase):
-        b = 18 if phase == 1 else 22
-        sp = turned(p, phase)
-        arrived(p, b + 2, sp(2, A))
-        if phase == 0:
-            send(p, 29, sp(2, A), sp(2, A), sibling)
-        arrived(p, b + 3, sp(2, B))
-        if phase == 0:
-            send(p, 30, sp(2, B), sp(2, B), sibling)
-
-    def sib(p):
-        c1 = where(p)[0]
-
-        def sp(d, cols=None):
-            return spot(p, (c1 + d) % 4, cols=cols, c=1 - core)
-
-        arrived(p, 26, sp(0))
-        arrived(p, 27, sp(3))
-        arrived(p, 28, sp(1))
-        arrived(p, 29, sp(2, A))
-        arrived(p, 30, sp(2, B))
+            send(w, k, 14 + d, mine, mine, to(d))
+
+    def ag2b(w, k):
+        c1, c2, _ = at(k)
+        for d in (1, 2, 3):
+            arrived(w, k, 14 + d, spot(w, k, c1, (c2 + 4 - d) % 4))
+
+    def ag1a(w, k):
+        c1, _, _ = at(k)
+        _, to = place_of(k, 0)
+        for cols, m in ((0, 18), (1, 20)):
+            up = spot(w, k, c1, cols=cols)
+            send(w, k, m, up, up, to(1))
+            dn = spot(w, k, c1, cols=1 - cols)
+            send(w, k, m + 1, dn, dn, to(3))
+        mine = spot(w, k, c1)
+        send(w, k, 24, mine, mine, sibling)
+
+    def ag1b(w, k):
+        c1, _, _ = at(k)
+        _, to = place_of(k, 0)
+        left, right = (c1 + 3) % 4, (c1 + 1) % 4
+        a = spot(w, k, left, cols=0)
+        arrived(w, k, 18, a)
+        send(w, k, 22, a, a, to(1))
+        b = spot(w, k, right, cols=1)
+        arrived(w, k, 19, b)
+        send(w, k, 23, b, b, to(3))
+        arrived(w, k, 20, spot(w, k, left, cols=1))
+        send(w, k, 25, spot(w, k, left), spot(w, k, left), sibling)
+        arrived(w, k, 21, spot(w, k, right, cols=0))
+        send(w, k, 26, spot(w, k, right), spot(w, k, right), sibling)
+
+    def ag1c(w, k):
+        c1, _, _ = at(k)
+        for cols in range(2):
+            far = spot(w, k, (c1 + 2) % 4, cols=cols)
+            arrived(w, k, 22 + cols, far)
+            send(w, k, 27 + cols, far, far, sibling)
+
+    def sib(w, k):
+        c1, _, _ = at(k)
+        for by, m in ((0, 24), (3, 25), (1, 26)):
+            arrived(w, k, m, spot(w, k, (c1 + by) % 4, c=1 - core))
+        for cols in range(2):
+            arrived(w, k, 27 + cols, spot(w, k, (c1 + 2) % 4, cols=cols, c=1 - core))
+
+    STEPS = ((rs1a,), (rs1b,), (rs1c, rs2a), (rs2b, rs3a), (rs3b,), (ag3b, ag2a), (ag2b, ag1a), (ag1b,), (ag1c,), (sib,))
+
+    def step(w, n):
+        for k in range(3):
+            for f in STEPS[n]:
+                f(w, k)
 
     def own_a():
         for by in (1, 2, 3):
@@ -690,20 +742,16 @@
                 src_ref=g.own_in.at[by - 1], dst_ref=g.own_in.at[by - 1], send_sem=xs_send.at[2 + by],
                 recv_sem=xs_recv.at[2 + by], device_id=sibling, device_id_type=MESH).wait_recv()
             total = total + g.own_in[by - 1].astype(F32)
-        g.own_sum[...] = total.astype(BF)
         mine = own_out.at[pl.ds(pl.multiple_of(64 * me, 16), 64)]
-        here = pltpu.make_async_copy(g.own_sum, mine, lsem.at[6])
-        here.start()
+        mine[...] = total.astype(BF)
         for by in (1, 2, 3):
             c = pltpu.make_async_remote_copy(
-                src_ref=g.own_sum, dst_ref=mine, send_sem=xs_send.at[5 + by],
+                src_ref=mine, dst_ref=mine, send_sem=xs_send.at[5 + by],
                 recv_sem=xs_recv.at[5 + by], device_id=device(along(pos, 1, by), core), device_id_type=MESH)
             c.start()
             started.append(c)
-        return here
-
-    def own_c(here):
-        here.wait()
+
+    def own_c():
         for by in (1, 2, 3):
             src = own_out.at[pl.ds(pl.multiple_of(64 * ((me + 4 - by) % 4), 16), 64)]
             pltpu.make_async_remote_copy(
@@ -738,64 +786,73 @@
     act_local.wait()
     act_go.wait_recv()
     dh_go.wait_recv()
-    for k in range(2):
-        g.w1[2, :, 768 * k : 768 * k + 768] = mm_tn(g.f_act[:, 768 * k : 768 * k + 768], g.f_dh[...]).astype(BF)
-    rs_a(2, 0)
+    for k in range(3):
+        g.w1_0[k] = mm_tn(g.f_act[:, 512 * k : 512 * k + 512], g.f_dh[...]).astype(BF)
+    step(0, 0)
     du_local.wait()
     du_go.wait_recv()
     n2_go.wait_recv()
-    for k in range(2):
-        g.w1[1, :, 768 * k : 768 * k + 768] = mm_tn(g.f_n2[...], g.f_du[:, 768 * k : 768 * k + 768]).astype(BF)
-    rs_a(1, 0)
-    for c in (dq_local, da_local):
-        c.wait()
-    for c in (dq_go, da_go, n1_go, o_go):
+    for k in range(3):
+        g.w1_1[k] = mm_tn(g.f_n2[...], g.f_du[:, 512 * k : 512 * k + 512]).astype(BF)
+    dq_local.wait()
+    for c in (dq_go, n1_go, o_go):
         c.wait_recv()
-    g.w1[0, :, 1152:1536] = mm_tn(g.f_o[...], g.f_qo[:, 1152:1536]).astype(BF)
-    g.w1[0, :, 0:768] = mm_tn(g.f_n1[...], g.f_qo[:, 0:768]).astype(BF)
-    g.w1[0, :, 768:1152] = mm_tn(g.f_n1[...], g.f_qo[:, 768:1152]).astype(BF)
-    rs_a(0, 0)
+    left = mm_tn(g.f_n1[...], g.f_qo[:, 0:768]).astype(BF)
+    g.w1_2[0] = left[:, 0:512]
+    g.w1_2[1, :, 0:256] = left[:, 512:768]
+    step(0, 1)
+    step(1, 0)
+
+    def right(factor):
+        v = mm_tn(factor[...], g.f_qo[:, 768:1536]).astype(BF)
+        g.w1_2[1, :, 256:512] = v[:, 0:256]
+        g.w1_2[2] = v[:, 256:768]
+
+    @pl.when(core == 0)
+    def _():
+        right(g.f_n1)
+
+    @pl.when(core == 1)
+    def _():
+        right(g.f_o)
+
+    step(0, 2)
+    step(1, 1)
+    step(2, 0)
     own_a()
     small_take(0)
     small_send(1)
-    T = (2, 1, 0)
-    for p in T:
-        rs_b(p, 0)
+    step(0, 3)
+    step(1, 2)
+    step(2, 1)
     small_take(1)
     small_send(2)
-    for p in T:
-        rs_c(p, 0)
-        rs_a(p, 1)
+    step(0, 4)
+    step(1, 3)
+    step(2, 2)
+    own_b()
     small_take(2)
     small_send(3)
-    here = own_b()
-    for p in T:
-        rs_b(p, 1)
-    for p in T:
-        rs_c(p, 1)
-        rs3_a(p)
+    step(0, 5)
+    step(1, 4)
+    step(2, 3)
     small_take(3)
-    small_copy = pltpu.make_async_copy(g.small_out_v.at[4], small_out, lsem.at[8])
-    small_copy.start()
-    for p in T:
-        rs3_b(p)
-    own_c(here)
-    for p in T:
-        ag3(p)
-        ag_a(p, 1)
-    for p in T:
-        ag_b(p, 1)
-    for p in T:
-        ag_c(p, 1)
-        ag_a(p, 0)
-    for p in T:
-        ag_b(p, 0)
-    for p in T:
-        ag_c(p, 0)
-    for p in T:
-        sib(p)
-    act_copy.wait()
-    small_copy.wait()
+    small_out[...] = g.small_out_v[4]
+    step(0, 6)
+    step(1, 5)
+    step(2, 4)
+    own_c()
+    step(0, 7)
+    step(1, 6)
+    step(2, 5)
+    step(0, 8)
+    step(1, 7)
+    step(2, 6)
+    step(1, 8)
+    step(2, 7)
+    step(2, 8)
+    for w in range(3):
+        step(w, 9)
     for c in started:
         c.wait_send()
 
@@ -804,86 +861,93 @@
 NAMES.append("small_out_v")
 
 
-def passes(starts, lengths, x, cot, par, wq, wo, wu, wd):
+def passes(*args):
     smem = pl.BlockSpec(memory_space=pltpu.SMEM)
     hbm = pl.BlockSpec(memory_space=pl.ANY)
+    vmem = pl.BlockSpec(memory_space=pltpu.VMEM)
     dma = pltpu.SemaphoreType.DMA
     return pl.pallas_call(
         kernel,
         out_shape=[
-            jax.ShapeDtypeStruct((ROWS, D), BF),
-            jax.ShapeDtypeStruct((ROWS, D), BF),
-            jax.ShapeDtypeStruct((16, D), F32),
-            jax.ShapeDtypeStruct((2, 3, 768, 1536), BF),
+            pltpu.VMEM((ROWS, D), BF),
+            pltpu.VMEM((ROWS, D), BF),
+            pltpu.VMEM((16, D), F32),
+            pltpu.VMEM((D, FF), BF),
+            pltpu.VMEM((D, FF), BF),
+            pltpu.VMEM((FF, D), BF),
         ],
-        in_specs=[smem, smem] + [hbm] * 7,
-        out_specs=[hbm] * 4,
+        in_specs=[smem, smem] + [hbm] * (len(args) - 2),
+        out_specs=[vmem] * 6,
         scratch_shapes=[pltpu.VMEM(s, t) for s, t in SCRATCH.values()]
-        + [dma((9,)), dma((8,)), dma((8,)), dma((3, NMSG)), dma((3, NMSG)), dma((19,)), dma((19,))],
+        + [dma((21,)), dma((8,)), dma((8,)), dma((9, NMSG)), dma((9, NMSG)), dma((19,)), dma((19,))],
         compiler_params=pltpu.CompilerParams(
-            collective_id=0, has_side_effects=True, vmem_limit_bytes=60 * 2**20
+            collective_id=0, has_side_effects=True, vmem_limit_bytes=VMEM_LIMIT
         ),
         name="passes",
-    )(starts, lengths, x, cot, par, wq, wo, wu, wd)
-
-
-def widen_kernel(all_ref, gq, go, gu, gd):
-    for c in range(2):
-        gq[:, 1152 * c : 1152 * c + 1152] = all_ref[c, 0, :, 0:1152].astype(F32)
-        go[:, 384 * c : 384 * c + 384] = all_ref[c, 0, :, 1152:1536].astype(F32)
-        gu[:, 1536 * c : 1536 * c + 1536] = all_ref[c, 1].astype(F32)
-        for k in range(2):
-            gd[2 * c + k] = all_ref[c, 2, :, 768 * k : 768 * k + 768].astype(F32)
-
-
-def widen(gathered):
-    n = 96
+    )(*args)
+
+
+VMEM_LIMIT = 46 * 2**20
+SMALL = ((LN1G, 1), (LN1S, 1), (BQV, 2), (BOUT, 1), (LN2G, 1), (LN2S, 1), (BUP, 4), (BDOWN, 1))
+
+
+def widen_kernel(act, own, small, qo, u, d, act_out, own_out, gq, go, gu, gd, *rest):
+    small_outs, (wide, tall, sem, wide_sem, tall_sem) = rest[:8], rest[8:]
+    pending = []
+
+    def copy(src, dst, s):
+        c = pltpu.make_async_copy(src, dst, s)
+        c.start()
+        return c
+
+    pending.append(copy(act, act_out, sem.at[0]))
+    pending.append(copy(own, own_out, sem.at[1]))
+    n = 2
+    for (first, count), ref in zip(SMALL, small_outs):
+        for k in range(count):
+            pending.append(copy(small.at[first + k], ref.at[pl.ds(k * D, D)], sem.at[n]))
+            n += 1
+    slots = {}
+
+    def chunk(buf, sems, i, value, parts):
+        slot = i % buf.shape[0]
+        key = (buf is wide, slot)
+        for c in slots.get(key, ()):
+            c.wait()
+        buf[slot] = value.astype(F32)
+        slots[key] = [copy(buf.at[slot, :, pl.ds(l0, n)], dst, sems.at[slot, j]) for j, (l0, n, dst) in enumerate(parts)]
+
+    for i in range(12):
+        rows = pl.ds(64 * i, 64)
+        chunk(wide, wide_sem, 2 * i, qo[64 * i : 64 * i + 64, :], ((0, 3 * D, gq.at[rows]), (3 * D, D, go.at[rows])))
+        chunk(tall, tall_sem, i, d[256 * i : 256 * i + 256, :], ((0, D, gd.at[pl.ds(256 * i, 256)]),))
+        chunk(wide, wide_sem, 2 * i + 1, u[64 * i : 64 * i + 64, :], ((0, FF, gu.at[rows]),))
+    for cs in list(slots.values()) + [pending]:
+        for c in cs:
+            c.wait()
+
+
+def widen(*arrays):
+    hbm = pl.BlockSpec(memory_space=pl.ANY)
+    vmem = pl.BlockSpec(memory_space=pltpu.VMEM)
+    dma = pltpu.SemaphoreType.DMA
+    shape = jax.ShapeDtypeStruct
     return pl.pallas_call(
         widen_kernel,
-        grid=(768 // n,),
-        in_specs=[pl.BlockSpec((2, 3, n, 1536), lambda i: (0, 0, i, 0))],
-        out_specs=[
-            pl.BlockSpec((n, 2304), lambda i: (i, 0)),
-            pl.BlockSpec((n, 768), lambda i: (i, 0)),
-            pl.BlockSpec((n, 3072), lambda i: (i, 0)),
-            pl.BlockSpec((4, n, 768), lambda i: (0, i, 0)),
-        ],
-        out_shape=[
-            jax.ShapeDtypeStruct((768, 2304), F32),
-            jax.ShapeDtypeStruct((768, 768), F32),
-            jax.ShapeDtypeStruct((768, 3072), F32),
-            jax.ShapeDtypeStruct((4, 768, 768), F32),
-        ],
-        compiler_params=pltpu.CompilerParams(vmem_limit_bytes=40 * 2**20),
+        in_specs=[vmem] * 6,
+        out_specs=[hbm] * 14,
+        out_shape=[shape((ROWS, D), BF), shape((ROWS, D), BF), shape((D, 3 * D), F32), shape((D, D), F32), shape((D, FF), F32),
+                   shape((FF, D), F32)] + [shape((n * D,), F32) for _, n in SMALL],
+        scratch_shapes=[pltpu.VMEM((6, 64, FF), F32), pltpu.VMEM((3, 256, D), F32), dma((14,)), dma((6, 2)), dma((3, 1))],
+        compiler_params=pltpu.CompilerParams(vmem_limit_bytes=24 * 2**20),
         name="widen",
-    )(gathered)
-
-
-def on_device(embedded, cotangent, lengths, starts, ln1_gain, ln1_shift, w_qkv, b_qv, w_out, b_out,
-              ln2_gain, ln2_shift, w_up, b_up, w_down, b_down):
-    par = jnp.concatenate(
-        [ln1_gain, ln1_shift, b_qv, b_out, ln2_gain, ln2_shift, b_up, b_down, jnp.zeros((4 * D,), F32)]
-    ).reshape(16, D)
-    act, own, small, gathered = passes(
-        starts, lengths, embedded.reshape(ROWS, D), cotangent.reshape(ROWS, D), par, w_qkv, w_out, w_up, w_down
-    )
-    gq, go, gu, gd = widen(gathered)
-    return (
-        act.reshape(1, 2, 128, D),
-        own.reshape(2, 128, D),
-        small[LN1G],
-        small[LN1S],
-        gq,
-        small[BQV : BQV + 2].reshape(2 * D),
-        go,
-        small[BOUT],
-        small[LN2G],
-        small[LN2S],
-        gu,
-        small[BUP : BUP + 4].reshape(FF),
-        gd.reshape(FF, D),
-        small[BDOWN],
-    )
+    )(*arrays)
+
+
+def on_device(embedded, cotangent, lengths, starts, *params):
+    gathered = passes(starts, lengths, embedded.reshape(ROWS, D), cotangent.reshape(ROWS, D), *params)
+    act, own, gq, go, gu, gd, ln1g, ln1s, bqv, bout, ln2g, ln2s, bup, bdown = widen(*gathered)
+    return (act.reshape(1, 2, 128, D), own.reshape(2, 128, D), ln1g, ln1s, gq, bqv, go, bout, ln2g, ln2s, gu, bup, gd, bdown)
 
 
 def solution(mesh):

time: 176 us -> 157 us (0.89)
  local copies, waits for them, and re-layouts: 17.1 us -> 0 us
  Pallas kernels: 158 us -> 156 us
    unnamed x16 -> x0, local copies, waits for them, and re-layouts: 12.1 us -> none
    slice x3 -> x0, local copies, waits for them, and re-layouts: 3.13 us -> none  [the longest x1 1.58 us: on_device(): small[BDOWN]]
    reshape x3 -> x0, local copies, waits for them, and re-layouts: 1.85 us -> none  [the longest x1 0.63 us: on_device(): par = jnp.concatenate([ln1_gain, ln1_shift, b_qv, b_out, ln2_gain, ln2_sh...]
where the time goes in v3:
time: 157 us
  Pallas kernels  156 us (99%)
    pallas_call x1, Pallas kernels, passes(): pl.pallas_call(kernel, out_shape=[pltpu.VMEM((ROWS, D), BF), pltpu.VMEM((...  146 us
    pallas_call x1, Pallas kernels, widen(): pl.pallas_call(widen_kernel, in_specs=[vmem] * 6, out_specs=[hbm] * 14, o...  9.85 us

profile of v3, /device:TPU:1, one launch (start us, length us, event | category | flops | bytes accessed | tf_op | source)
XLA Modules:
  0.0 157.2 jit_solution(4628490828786601292)
XLA Ops:
  0.7 146.5 %passes.1 = (bf16[256,768]{1,0:T(8,128)(2,1)S(1)}, bf16[256,768]{1,0:T(8,128)(2,1)S(1)}, f32[16,768]{1,0:T(8,128)S(1)}, bf16[768,3072]{1,0:T(8,128)(2,1)S(1)}, b...) custom-call(s32[2]{0:T(128)} %start_ref.1, s32[2]{0:T(128)} %length_ref.1, bf16[256,768]{1,0:T(8,128)(2,1)} %bitcast.4, ...), custom_call_target="tpu_custom_call" | custom-call | tf_op jit(solution)/shard_map/passes/pallas_call | solution.py:869
  147.1 9.9 %widen.1 = (bf16[256,768]{1,0:T(8,128)(2,1)}, bf16[256,768]{1,0:T(8,128)(2,1)}, f32[768,2304]{1,0:T(8,128)}, f32[768,768]{1,0:T(8,128)}, f32[768,3072]{1,0:T(8,1...) custom-call(bf16[256,768]{1,0:T(8,128)(2,1)S(1)} %get-tuple-element., ...), custom_call_target="tpu_custom_call" | custom-call | tf_op jit(solution)/shard_map/widen/pallas_call | solution.py:935

commit v4 on v3

--- a/solution.py
+++ b/solution.py
@@ -20,10 +20,12 @@
 LN1G, LN1S, BQV, BOUT, LN2G, LN2S, BUP, BDOWN = 0, 1, 2, 4, 5, 6, 7, 11
 
 ORDERS = ((0, 1, 2), (1, 2, 0), (2, 0, 1))
-NMSG = 30
+NMSG = 32
 WAVES = 3
-SHAPES = ((512, 768), (768, 512), (768, 512))
-SUBS = ((16, 384), (48, 128), (48, 128))
+SHAPES = ((1536, 256), (768, 512), (768, 512))
+BLOCKS = ((384, 256), (768, 128), (192, 512))
+PIECES = ((96, 256), (192, 128), (48, 512))
+SUB = (48, 128)
 
 
 def mm(a, b):
@@ -72,10 +74,7 @@
 def coords():
     b = lax.axis_index("batch")
     y = lax.axis_index("pass")
-    core = b % 2
-    z = (b // 2) % 4
-    x = b // 8
-    return (x, y, z), core
+    return (lax.div(b, 8), y, lax.rem(lax.div(b, 2), 4)), lax.rem(b, 2)
 
 
 def device(pos, core):
@@ -84,7 +83,7 @@
 
 
 def along(pos, axis, by):
-    return tuple((c + by) % 4 if i == axis else c for i, c in enumerate(pos))
+    return tuple(lax.rem(c + by, 4) if i == axis else c for i, c in enumerate(pos))
 
 
 def iota(shape, dim):
@@ -131,14 +130,16 @@
     dx_mini=((16, D), F32), dxm_own=((16, D), BF), dxb_own=((64, D), F32),
     f_n1=((512, D), BF), f_o=((512, D), BF), f_n2=((512, D), BF), f_dh=((512, D), BF),
     f_qo=((512, 1536), BF), f_du=((512, 1536), BF), f_act=((512, 1536), BF),
-    w1_0=((3, 512, 768), BF), w1_1=((3, 768, 512), BF), w1_2=((3, 768, 512), BF),
-    relay_0=((3, 2, 128, 384), BF), relay_1=((3, 2, 192, 256), BF), relay_2=((3, 2, 192, 256), BF),
-    in1_0=((3, 2, 128, 768), BF), in1_1=((3, 2, 192, 512), BF), in1_2=((3, 2, 192, 512), BF),
-    w2_0=((3, 128, 768), BF), w2_1=((3, 192, 512), BF), w2_2=((3, 192, 512), BF),
-    in2_0=((3, 3, 32, 768), BF), in2_1=((3, 3, 48, 512), BF), in2_2=((3, 3, 48, 512), BF),
-    w3_0=((3, 32, 768), BF), w3_1=((3, 48, 512), BF), w3_2=((3, 48, 512), BF),
-    in3_0=((3, 3, 16, 384), BF), in3_1=((3, 3, 48, 128), BF), in3_2=((3, 3, 48, 128), BF),
-    own=((4, 64, D), BF), own_in=((3, 64, D), BF),
+    w1_0=((3, 1536, 256), BF), w1_1=((3, 768, 512), BF), w1_2=((3, 768, 512), BF),
+    relay=((3, 2, 192, 256), BF),
+    in1_0=((3, 3, 384, 256), BF), in1_1=((3, 3, 768, 128), BF), in1_2=((3, 2, 192, 512), BF),
+    w2_0=((3, 384, 256), BF), w2_1=((3, 768, 128), BF), w2_2=((3, 192, 512), BF),
+    in2_0=((3, 3, 96, 256), BF), in2_1=((3, 3, 192, 128), BF), in2_2=((3, 3, 48, 512), BF),
+    w3_0=((3, 96, 256), BF), w3_1=((3, 192, 128), BF), w3_2=((3, 48, 512), BF),
+    in3_0=((3, 3, 48, 128), BF), in3_1=((3, 3, 48, 128), BF), in3_2=((3, 3, 48, 128), BF),
+    act_mini=((16, FF), BF), c_act=((32, 1536), BF), c_n2=((32, D), BF), c_e=((32, D), BF), c_du=((32, 1536), BF),
+    ca_0=((3, 4, 32, 384), BF), cg_0=((3, 4, 32, 256), BF), ca_1=((3, 4, 32, D), BF), cg_1=((3, 4, 32, 128), BF),
+    own=((2, 4, 32, D), BF), own_in=((2, 3, 32, D), BF),
     small_in=((10, 16, D), F32),
 )
 NAMES = list(SCRATCH)
@@ -351,18 +352,27 @@
     def half(ref, which, width):
         return ref.at[:, pl.ds(pl.multiple_of(which * width, 128), width)]
 
+    cot_load.wait()
+    dh_go = to_sibling(4, g.f_dh.at[lo], g.f_dh.at[hi])
+    act_go = to_sibling(3, half(g.act, 1 - core, 1536), g.f_act.at[hi])
+    act_local = local(1, half(g.act, core, 1536), g.f_act.at[lo])
+    n2_go = to_sibling(2, g.f_n2.at[lo], g.f_n2.at[hi])
     n1_go = to_sibling(0, g.f_n1.at[lo], g.f_n1.at[hi])
     o_go = to_sibling(1, g.f_o.at[lo], g.f_o.at[hi])
-    n2_go = to_sibling(2, g.f_n2.at[lo], g.f_n2.at[hi])
-    act_go = to_sibling(3, half(g.act, 1 - core, 1536), g.f_act.at[hi])
-    act_local = local(1, half(g.act, core, 1536), g.f_act.at[lo])
-
-    cot_load.wait()
+    mini_lo, mini_hi = pl.ds(0, 16), pl.ds(16, 16)
+    g.act_mini[...] = mm(pick, g.act[...]).astype(BF)
+    g.c_act[0:16, :] = g.act_mini[:, pl.ds(pl.multiple_of(core * 1536, 128), 1536)]
+    g.c_n2[0:16, :] = mm(pick, g.f_n2[0:256, :]).astype(BF)
+    c_act_go = to_sibling(7, half(g.act_mini, 1 - core, 1536), g.c_act.at[mini_hi])
+    c_n2_go = to_sibling(8, g.c_n2.at[mini_lo], g.c_n2.at[mini_hi])
+
     for k in range(4):
         c = slice(k * D, (k + 1) * D)
         du = (mm_nt(g.cot_v[...], g.wd[c, :]) * g.gp[:, c]).astype(BF)
         g.du[:, c] = du
         g.sums[BUP + k : BUP + k + 1, :] = column_sum(du.astype(F32))
+    du_go = to_sibling(5, half(g.du, 1 - core, 1536), g.f_du.at[hi])
+    du_local = local(3, half(g.du, core, 1536), g.f_du.at[lo])
     g.sums[BDOWN : BDOWN + 1, :] = column_sum(g.cot_v[...].astype(F32))
     g.tmp[...] = mm_nt(g.du[...], g.wu[...])
     zero8 = jnp.zeros((8, D), F32)
@@ -413,6 +423,302 @@
     for i, a in zip((LN1G, LN1S, BQV, BQV + 1), acc):
         g.sums[i : i + 1, :] = jnp.sum(a, 0, keepdims=True)
 
+    def msg(w, k, m, src, dst, to):
+        i = 3 * w + k
+        return pltpu.make_async_remote_copy(src_ref=src, dst_ref=dst, send_sem=ssem.at[i, m], recv_sem=rsem.at[i, m],
+                                            device_id=to, device_id_type=MESH)
+
+    def send(w, k, m, src, dst, to):
+        c = msg(w, k, m, src, dst, to)
+        c.start()
+        started.append(c)
+
+    def arrived(w, k, m, dst):
+        msg(w, k, m, dst, dst, sibling).wait_recv()
+
+    w1s, in1s = (g.w1_0, g.w1_1, g.w1_2), (g.in1_0, g.in1_1, g.in1_2)
+    w2s, in2s = (g.w2_0, g.w2_1, g.w2_2), (g.in2_0, g.in2_1, g.in2_2)
+    w3s, in3s = (g.w3_0, g.w3_1, g.w3_2), (g.in3_0, g.in3_1, g.in3_2)
+    cas, cgs = (g.ca_0, g.ca_1), (g.cg_0, g.cg_1)
+    outs = (w_d, w_u, w_qo)
+    memo = {}
+
+    def near(axis, by):
+        if (axis, by) not in memo:
+            there = along(pos, axis, by)
+            memo[axis, by] = (device(there, core), there[axis])
+        return memo[axis, by]
+
+    def ds(i, n, m):
+        return pl.ds(i if isinstance(i, int) else pl.multiple_of(i, m), n)
+
+    def window(ref, r0, l0, shape):
+        return ref.at[ds(r0, shape[0], 16), ds(l0, shape[1], 128)]
+
+    def block(w, c1):
+        return ((384 * c1, 0), (0, 128 * c1), (192 * c1, 0))[w]
+
+    def piece(w, c1, c2):
+        r, l = block(w, c1)
+        return r + PIECES[w][0] * c2, l
+
+    def inner(w, c3):
+        return ((48 * lax.div(c3, 2), 128 * lax.rem(c3, 2)), (48 * c3, 0), (0, 128 * c3))[w]
+
+    HALVES = ((384, 128), (384, 128), (192, 256))
+
+    def half_of(w, cols):
+        return ((0, 128 * cols), (384 * cols, 0), (0, 256 * cols))[w]
+
+    def send_first(w, k):
+        axis = ORDERS[k][0]
+        for d in (1, 2, 3):
+            to, c = near(axis, d)
+            send(w, k, d - 1, window(w1s[w].at[k], *block(w, c), BLOCKS[w]), in1s[w].at[k, d - 1], to)
+
+    def send_left(k):
+        axis = ORDERS[k][0]
+        mine = near(axis, 0)[1]
+        g.ca_0[k, 0] = g.c_act[:, ds(384 * mine, 384, 128)]
+        g.ca_1[k, 0] = g.c_n2[...]
+        for d in (1, 2, 3):
+            to, c = near(axis, d)
+            send(0, k, 2 + d, window(g.c_act, 0, 384 * c, (32, 384)), g.ca_0.at[k, d], to)
+            send(1, k, 2 + d, g.c_n2, g.ca_1.at[k, d], to)
+
+    def send_right(k):
+        axis = ORDERS[k][0]
+        mine = near(axis, 0)[1]
+        g.cg_0[k, 0] = g.c_e[:, 256 * k : 256 * k + 256]
+        g.cg_1[k, 0] = g.c_du[:, ds(512 * k + 128 * mine, 128, 128)]
+        for d in (1, 2, 3):
+            to, c = near(axis, d)
+            send(0, k, 28 + d, window(g.c_e, 0, 256 * k, (32, 256)), g.cg_0.at[k, d], to)
+            send(1, k, 28 + d, window(g.c_du, 0, 512 * k + 128 * c, (32, 128)), g.cg_1.at[k, d], to)
+
+    def sum_first(w, k):
+        mine = near(ORDERS[k][0], 0)[1]
+        for d in (1, 2, 3):
+            arrived(w, k, 2 + d, cas[w].at[k, d])
+            arrived(w, k, 28 + d, cgs[w].at[k, d])
+            arrived(w, k, d - 1, in1s[w].at[k, d - 1])
+        n = BLOCKS[w][0]
+        total = mm_tn(cas[w][k].reshape(128, n), cgs[w][k].reshape(128, BLOCKS[w][1]))
+        total = total + window(w1s[w].at[k], *block(w, mine), BLOCKS[w])[...].astype(F32)
+        for d in range(3):
+            total = total + in1s[w][k, d].astype(F32)
+        w2s[w][k] = total.astype(BF)
+
+    A, B = pl.ds(0, 256), pl.ds(256, 256)
+
+    def ring_a(k):
+        axis = ORDERS[k][0]
+        w1, inn = g.w1_2.at[k], g.in1_2.at[k]
+        (up, c_up), (dn, c_dn), (_, far) = near(axis, 1), near(axis, 3), near(axis, 2)
+
+        def blk(c):
+            return ds(c * 192, 192, 16)
+
+        send(2, k, 0, w1.at[blk(far), A], g.relay.at[k, 0], up)
+        send(2, k, 1, w1.at[blk(far), B], g.relay.at[k, 1], dn)
+        send(2, k, 2, w1.at[blk(c_up), B], inn.at[0, :, B], up)
+        send(2, k, 3, w1.at[blk(c_dn), A], inn.at[1, :, A], dn)
+
+    def ring_b(k):
+        axis = ORDERS[k][0]
+        for side, by, cols in ((0, 1, A), (1, 3, B)):
+            to, c = near(axis, by)
+            arrived(2, k, side, g.relay.at[k, side])
+            g.relay[k, side] = (g.relay[k, side].astype(F32) + g.w1_2[k, ds(c * 192, 192, 16), cols].astype(F32)).astype(BF)
+            send(2, k, 4 + side, g.relay.at[k, side], g.in1_2.at[k, side, :, cols], to)
+
+    def ring_c(k):
+        inn = g.in1_2
+        arrived(2, k, 2, inn.at[k, 0, :, B])
+        arrived(2, k, 3, inn.at[k, 1, :, A])
+        arrived(2, k, 4, inn.at[k, 0, :, A])
+        arrived(2, k, 5, inn.at[k, 1, :, B])
+        mine = near(ORDERS[k][0], 0)[1]
+        total = g.w1_2[k, ds(mine * 192, 192, 16), :].astype(F32) + inn[k, 0].astype(F32) + inn[k, 1].astype(F32)
+        g.w2_2[k] = total.astype(BF)
+
+    def rs2a(w, k):
+        axis = ORDERS[k][1]
+        for d in (1, 2, 3):
+            to, c = near(axis, d)
+            send(w, k, 5 + d, window(w2s[w].at[k], PIECES[w][0] * c, 0, PIECES[w]), in2s[w].at[k, d - 1], to)
+
+    def rs2b(w, k):
+        mine = near(ORDERS[k][1], 0)[1]
+        for d in (1, 2, 3):
+            arrived(w, k, 5 + d, in2s[w].at[k, d - 1])
+        total = window(w2s[w].at[k], PIECES[w][0] * mine, 0, PIECES[w])[...].astype(F32)
+        for d in range(3):
+            total = total + in2s[w][k, d].astype(F32)
+        w3s[w][k] = total.astype(BF)
+
+    def rs3a(w, k):
+        axis = ORDERS[k][2]
+        for d in (1, 2, 3):
+            to, c = near(axis, d)
+            send(w, k, 8 + d, window(w3s[w].at[k], *inner(w, c), SUB), in3s[w].at[k, d - 1], to)
+
+    def out_window(w, k, r, l, shape, c=None):
+        c = core if c is None else c
+        r0, l0 = (c * 1536, 256 * k) if w == 0 else (0, c * 1536 + 512 * k)
+        return window(outs[w], r0 + r, l0 + l, shape)
+
+    def out_block(w, k, c1, cols=None, c=None):
+        r, l = block(w, c1)
+        if cols is None:
+            return out_window(w, k, r, l, BLOCKS[w], c)
+        r1, l1 = half_of(w, cols)
+        return out_window(w, k, r + r1, l + l1, HALVES[w], c)
+
+    def out_piece(w, k, c1, c2):
+        return out_window(w, k, *piece(w, c1, c2), PIECES[w])
+
+    def out_sub(w, k, c1, c2, c3):
+        (r, l), (r1, l1) = piece(w, c1, c2), inner(w, c3)
+        return out_window(w, k, r + r1, l + l1, SUB)
+
+    def at(k):
+        return tuple(near(a, 0)[1] for a in ORDERS[k])
+
+    def rs3b(w, k):
+        axis = ORDERS[k][2]
+        for d in (1, 2, 3):
+            arrived(w, k, 8 + d, in3s[w].at[k, d - 1])
+        total = window(w3s[w].at[k], *inner(w, near(axis, 0)[1]), SUB)[...].astype(F32)
+        for d in range(3):
+            total = total + in3s[w][k, d].astype(F32)
+        mine = out_sub(w, k, *at(k))
+        mine[...] = total.astype(BF)
+        for d in (1, 2, 3):
+            send(w, k, 11 + d, mine, mine, near(axis, d)[0])
+
+    def ag3b(w, k):
+        c1, c2, _ = at(k)
+        for d in (1, 2, 3):
+            arrived(w, k, 11 + d, out_sub(w, k, c1, c2, near(ORDERS[k][2], 4 - d)[1]))
+
+    def ag2a(w, k):
+        c1, c2, _ = at(k)
+        mine = out_piece(w, k, c1, c2)
+        for d in (1, 2, 3):
+            send(w, k, 14 + d, mine, mine, near(ORDERS[k][1], d)[0])
+
+    def ag2b(w, k):
+        c1 = at(k)[0]
+        for d in (1, 2, 3):
+            arrived(w, k, 14 + d, out_piece(w, k, c1, near(ORDERS[k][1], 4 - d)[1]))
+
+    def ag1a(w, k):
+        axis = ORDERS[k][0]
+        c1 = at(k)[0]
+        for cols, m in ((0, 18), (1, 20)):
+            up = out_block(w, k, c1, cols)
+            send(w, k, m, up, up, near(axis, 1)[0])
+            dn = out_block(w, k, c1, 1 - cols)
+            send(w, k, m + 1, dn, dn, near(axis, 3)[0])
+        mine = out_block(w, k, c1)
+        send(w, k, 24, mine, mine, sibling)
+
+    def ag1b(w, k):
+        axis = ORDERS[k][0]
+        left, right = near(axis, 3)[1], near(axis, 1)[1]
+        a = out_block(w, k, left, 0)
+        arrived(w, k, 18, a)
+        send(w, k, 22, a, a, near(axis, 1)[0])
+        b = out_block(w, k, right, 1)
+        arrived(w, k, 19, b)
+        send(w, k, 23, b, b, near(axis, 3)[0])
+        arrived(w, k, 20, out_block(w, k, left, 1))
+        send(w, k, 25, out_block(w, k, left), out_block(w, k, left), sibling)
+        arrived(w, k, 21, out_block(w, k, right, 0))
+        send(w, k, 26, out_block(w, k, right), out_block(w, k, right), sibling)
+
+    def ag1c(w, k):
+        far = near(ORDERS[k][0], 2)[1]
+        for cols in range(2):
+            v = out_block(w, k, far, cols)
+            arrived(w, k, 22 + cols, v)
+            send(w, k, 27 + cols, v, v, sibling)
+
+    def sib(w, k):
+        axis = ORDERS[k][0]
+        for by, m in ((0, 24), (3, 25), (1, 26)):
+            arrived(w, k, m, out_block(w, k, near(axis, by)[1], c=1 - core))
+        for cols in range(2):
+            arrived(w, k, 27 + cols, out_block(w, k, near(axis, 2)[1], cols, c=1 - core))
+
+    def step(w, *fs):
+        for f in fs:
+            for k in range(3):
+                f(w, k)
+
+    def each(f):
+        for k in range(3):
+            f(k)
+
+    def own_msg(i, src, dst, to):
+        return pltpu.make_async_remote_copy(src_ref=src, dst_ref=dst, send_sem=xs_send.at[i], recv_sem=xs_recv.at[i],
+                                            device_id=to, device_id_type=MESH)
+
+    def own_rows(part, b):
+        return ds(128 * lax.div(b, 2) + 64 * (1 - part) + 32 * lax.rem(b, 2), 32, 16)
+
+    def own_a(part):
+        for b in range(4):
+            first = 128 * (b // 2) + 64 * (1 - part) + 32 * (b % 2)
+            g.own[part, b] = g.dx[first : first + 32, :].astype(BF)
+        for by in (1, 2, 3):
+            to, c = near(1, by)
+            m = own_msg(3 + 6 * part + by - 1, g.own.at[part, c], g.own_in.at[part, by - 1], to)
+            m.start()
+            started.append(m)
+
+    def own_b(part):
+        total = g.own[part, me].astype(F32)
+        for by in (1, 2, 3):
+            ref = g.own_in.at[part, by - 1]
+            own_msg(3 + 6 * part + by - 1, ref, ref, sibling).wait_recv()
+            total = total + g.own_in[part, by - 1].astype(F32)
+        mine = own_out.at[own_rows(part, me)]
+        mine[...] = total.astype(BF)
+        for by in (1, 2, 3):
+            m = own_msg(6 + 6 * part + by - 1, mine, mine, near(1, by)[0])
+            m.start()
+            started.append(m)
+
+    def own_c(part):
+        for by in (1, 2, 3):
+            ref = own_out.at[own_rows(part, near(1, 4 - by)[1])]
+            own_msg(6 + 6 * part + by - 1, ref, ref, sibling).wait_recv()
+
+    def small_send(stage):
+        n = 1 if stage == 0 else 3
+        first = 0 if stage == 0 else 3 * stage - 2
+        for k in range(n):
+            to = sibling if stage == 0 else near(stage - 1, k + 1)[0]
+            c = pltpu.make_async_remote_copy(
+                src_ref=g.small_out_v.at[stage], dst_ref=g.small_in.at[first + k], send_sem=xs_send.at[15 + first + k],
+                recv_sem=xs_recv.at[15 + first + k], device_id=to, device_id_type=MESH)
+            c.start()
+            started.append(c)
+
+    def small_take(stage):
+        n = 1 if stage == 0 else 3
+        first = 0 if stage == 0 else 3 * stage - 2
+        total = g.small_out_v[stage]
+        for k in range(n):
+            ref = g.small_in.at[first + k]
+            pltpu.make_async_remote_copy(
+                src_ref=ref, dst_ref=ref, send_sem=xs_send.at[15 + first + k],
+                recv_sem=xs_recv.at[15 + first + k], device_id=sibling, device_id_type=MESH).wait_recv()
+            total = total + g.small_in[first + k]
+        g.small_out_v[stage + 1] = total
+
     g.slot_out[...] = mm(pick, g.dx[...].astype(BF)).astype(BF)
     for by in (1, 2, 3):
         c = pltpu.make_async_remote_copy(
@@ -427,8 +733,26 @@
     g.dqkv_own[...] = jnp.zeros((80, 3 * D), BF)
     g.dxm_own[...] = jnp.zeros((16, D), BF)
     g.dxb_own[...] = jnp.zeros((64, D), F32)
+    dh_go.wait_recv()
+    act_go.wait_recv()
+    act_local.wait()
+    for k in range(2):
+        v = mm_tn(g.f_act[:, 768 * k : 768 * k + 768], g.f_dh[...]).astype(BF)
+        for j in range(3):
+            g.w1_0[j, 768 * k : 768 * k + 768, :] = v[:, 256 * j : 256 * j + 256]
+    each(lambda k: send_first(0, k))
+    own_a(0)
+    du_go.wait_recv()
+    du_local.wait()
+    n2_go.wait_recv()
+    for k in range(3):
+        g.w1_1[k] = mm_tn(g.f_n2[...], g.f_du[:, 512 * k : 512 * k + 512]).astype(BF)
+    each(lambda k: send_first(1, k))
+    c_act_go.wait_recv()
+    c_n2_go.wait_recv()
+    each(send_left)
     for by in (1, 2, 3):
-        src = (me + 4 - by) % 4
+        src = near(1, 4 - by)[1]
         pltpu.make_async_remote_copy(
             src_ref=g.slot_out, dst_ref=g.slots.at[src], send_sem=xs_send.at[by - 1], recv_sem=xs_recv.at[by - 1],
             device_id=device(along(pos, 1, by), core), device_id_type=MESH).wait_recv()
@@ -496,312 +820,35 @@
 
     lax.fori_loop(0, 3, thought_back, 0)
 
+    g.c_e[0:16, :] = g.e_own[...]
+    g.c_du[0:16, :] = g.du_own[:, pl.ds(pl.multiple_of(core * 1536, 128), 1536)]
+    c_e_go = to_sibling(9, g.c_e.at[mini_lo], g.c_e.at[mini_hi])
+    c_du_go = to_sibling(10, half(g.du_own, 1 - core, 1536), g.c_du.at[mini_hi])
     top = [slice(128 * q, 128 * q + TOP) for q in range(2)]
-
-    def merge(into, own, q):
-        into[top[q], :] = (into[top[q], :].astype(F32) + mm(place[q], own[...])).astype(BF)
-
     for q in range(2):
-        merge(g.cot_v, g.e_own, q)
-    dh_go = to_sibling(4, g.cot_v, g.f_dh.at[hi])
-    for q in range(2):
-        merge(g.du, g.du_own, q)
-    du_go = to_sibling(5, half(g.du, 1 - core, 1536), g.f_du.at[hi])
-    du_local = local(3, half(g.du, core, 1536), g.f_du.at[lo])
-    for q in range(2):
-        merge(g.da, g.da_own, q)
+        g.da[top[q], :] = (g.da[top[q], :].astype(F32) + mm(place[q], g.da_own[...])).astype(BF)
         base = jnp.concatenate([g.dqkv_own[32 * q : 32 * q + 32, :].astype(F32), jnp.zeros((16, 3 * D), F32)], 0)
         g.dqkv[top[q], :] = (g.dqkv[top[q], :].astype(F32) + mm(place[q], g.dqkv_own[64:80, :]) + base).astype(BF)
     dq_go = to_sibling(6, half(g.dqo, 1 - core, 1536), g.f_qo.at[hi])
     dq_local = local(4, half(g.dqo, core, 1536), g.f_qo.at[lo])
+    c_e_go.wait_recv()
+    c_du_go.wait_recv()
+    each(send_right)
+    g.small_out_v[0] = g.sums[...]
+    small_send(0)
+    own_b(0)
     later = (me > 0).astype(F32)
     for q, s in ((0, s0), (1, s1)):
         dx = g.dx[top[q], :] + mm(place[q], g.dxm_own[...])
         dx = dx + jnp.concatenate([g.dxb_own[32 * q : 32 * q + 32, :], jnp.zeros((16, D), F32)], 0)
         dx = dx * (1.0 - later * is_slot(s, TOP).astype(F32))
         g.dx[top[q], :] = dx
-    for k in range(4):
-        g.own[k] = g.dx[64 * k : 64 * k + 64, :].astype(BF)
-
-    def msg(w, k, m, src, dst, to):
-        i = 3 * w + k
-        return pltpu.make_async_remote_copy(src_ref=src, dst_ref=dst, send_sem=ssem.at[i, m], recv_sem=rsem.at[i, m],
-                                            device_id=to, device_id_type=MESH)
-
-    def send(w, k, m, src, dst, to):
-        c = msg(w, k, m, src, dst, to)
-        c.start()
-        started.append(c)
-
-    def arrived(w, k, m, dst):
-        msg(w, k, m, dst, dst, sibling).wait_recv()
-
-    w1s, relays, in1s = (g.w1_0, g.w1_1, g.w1_2), (g.relay_0, g.relay_1, g.relay_2), (g.in1_0, g.in1_1, g.in1_2)
-    w2s, in2s = (g.w2_0, g.w2_1, g.w2_2), (g.in2_0, g.in2_1, g.in2_2)
-    w3s, in3s = (g.w3_0, g.w3_1, g.w3_2), (g.in3_0, g.in3_1, g.in3_2)
-    outs = (w_d, w_u, w_qo)
-
-    def ds(i, n, m):
-        return pl.ds(pl.multiple_of(i, m), n)
-
-    def place_of(k, phase):
-        axis = ORDERS[k][phase]
-        return pos[axis], lambda by: device(along(pos, axis, by), core)
-
-    def dims(w):
-        n, c = SHAPES[w]
-        return n // 4, n // 16, c, ds(0, c // 2, 128), ds(c // 2, c // 2, 128)
-
-    def rs1a(w, k):
-        i, to = place_of(k, 0)
-        n, _, _, A, B = dims(w)
-        w1, relay, inn = w1s[w].at[k], relays[w].at[k], in1s[w].at[k]
-
-        def blk(by):
-            return ds(((i + by) % 4) * n, n, 16)
-
-        send(w, k, 0, w1.at[blk(2), A], relay.at[0], to(1))
-        send(w, k, 1, w1.at[blk(2), B], relay.at[1], to(3))
-        send(w, k, 2, w1.at[blk(1), B], inn.at[0, :, B], to(1))
-        send(w, k, 3, w1.at[blk(3), A], inn.at[1, :, A], to(3))
-
-    def rs1b(w, k):
-        i, to = place_of(k, 0)
-        n, _, _, A, B = dims(w)
-        w1, relay, inn = w1s[w], relays[w], in1s[w]
-        for side, by, cols in ((0, 1, A), (1, 3, B)):
-            first = ((i + by) % 4) * n
-            arrived(w, k, side, relay.at[k, side])
-
-            def add(j, _):
-                s = ds(j * 16, 16, 16)
-                t = ds(first + j * 16, 16, 16)
-                relay[k, side, s, :] = (relay[k, side, s, :].astype(F32) + w1[k, t, cols].astype(F32)).astype(BF)
-                return 0
-
-            lax.fori_loop(0, n // 16, add, 0)
-            send(w, k, 4 + side, relay.at[k, side], inn.at[k, side, :, cols], to(by))
-
-    def rs1c(w, k):
-        i, _ = place_of(k, 0)
-        n, _, _, A, B = dims(w)
-        w1, inn, w2 = w1s[w], in1s[w], w2s[w]
-        arrived(w, k, 2, inn.at[k, 0, :, B])
-        arrived(w, k, 3, inn.at[k, 1, :, A])
-        arrived(w, k, 4, inn.at[k, 0, :, A])
-        arrived(w, k, 5, inn.at[k, 1, :, B])
-
-        def add(j, _):
-            s = ds(j * 16, 16, 16)
-            t = ds(i * n + j * 16, 16, 16)
-            w2[k, s, :] = (w1[k, t, :].astype(F32) + inn[k, 0, s, :].astype(F32) + inn[k, 1, s, :].astype(F32)).astype(BF)
-            return 0
-
-        lax.fori_loop(0, n // 16, add, 0)
-
-    def rs2a(w, k):
-        i, to = place_of(k, 1)
-        _, n, _, _, _ = dims(w)
-        for d in (1, 2, 3):
-            send(w, k, 5 + d, w2s[w].at[k, ds(((i + d) % 4) * n, n, 16)], in2s[w].at[k, d - 1], to(d))
-
-    def rs2b(w, k):
-        i, _ = place_of(k, 1)
-        _, n, _, _, _ = dims(w)
-        for d in (1, 2, 3):
-            arrived(w, k, 5 + d, in2s[w].at[k, d - 1])
-        total = w2s[w][k, ds(i * n, n, 16), :].astype(F32)
-        for d in range(3):
-            total = total + in2s[w][k, d].astype(F32)
-        w3s[w][k] = total.astype(BF)
-
-    def sub(w, j):
-        n, c = SUBS[w]
-        if w == 0:
-            return ds((j // 2) * n, n, 16), ds((j % 2) * c, c, 128)
-        return slice(None), ds(j * c, c, 128)
-
-    def rs3a(w, k):
-        i, to = place_of(k, 2)
-        for d in (1, 2, 3):
-            rows, cols = sub(w, (i + d) % 4)
-            send(w, k, 8 + d, w3s[w].at[k, rows, cols], in3s[w].at[k, d - 1], to(d))
-
-    def spot(w, k, c1, c2=None, c3=None, cols=None, c=None):
-        c = core if c is None else c
-        n1, n2, width, _, _ = dims(w)
-        r0, l0 = (c * 1536 + 512 * k, 0) if w == 0 else (0, c * 1536 + 512 * k)
-        r0 = r0 + n1 * c1
-        n = n1
-        if c2 is not None:
-            r0 = r0 + n2 * c2
-            n = n2
-        if c3 is not None:
-            n, width = SUBS[w]
-            if w == 0:
-                r0, l0 = r0 + n * (c3 // 2), l0 + width * (c3 % 2)
-            else:
-                l0 = l0 + width * c3
-        elif cols is not None:
-            width = width // 2
-            l0 = l0 + width * cols
-        return outs[w].at[ds(r0, n, 16), ds(l0, width, 128)]
-
-    def at(k):
-        return tuple(pos[a] for a in ORDERS[k])
-
-    def rs3b(w, k):
-        i, to = place_of(k, 2)
-        for d in (1, 2, 3):
-            arrived(w, k, 8 + d, in3s[w].at[k, d - 1])
-        rows, cols = sub(w, i)
-        total = w3s[w][k, rows, cols].astype(F32)
-        for d in range(3):
-            total = total + in3s[w][k, d].astype(F32)
-        mine = spot(w, k, *at(k))
-        mine[...] = total.astype(BF)
-        for d in (1, 2, 3):
-            send(w, k, 11 + d, mine, mine, to(d))
-
-    def ag3b(w, k):
-        c1, c2, c3 = at(k)
-        for d in (1, 2, 3):
-            arrived(w, k, 11 + d, spot(w, k, c1, c2, (c3 + 4 - d) % 4))
-
-    def ag2a(w, k):
-        c1, c2, _ = at(k)
-        _, to = place_of(k, 1)
-        mine = spot(w, k, c1, c2)
-        for d in (1, 2, 3):
-            send(w, k, 14 + d, mine, mine, to(d))
-
-    def ag2b(w, k):
-        c1, c2, _ = at(k)
-        for d in (1, 2, 3):
-            arrived(w, k, 14 + d, spot(w, k, c1, (c2 + 4 - d) % 4))
-
-    def ag1a(w, k):
-        c1, _, _ = at(k)
-        _, to = place_of(k, 0)
-        for cols, m in ((0, 18), (1, 20)):
-            up = spot(w, k, c1, cols=cols)
-            send(w, k, m, up, up, to(1))
-            dn = spot(w, k, c1, cols=1 - cols)
-            send(w, k, m + 1, dn, dn, to(3))
-        mine = spot(w, k, c1)
-        send(w, k, 24, mine, mine, sibling)
-
-    def ag1b(w, k):
-        c1, _, _ = at(k)
-        _, to = place_of(k, 0)
-        left, right = (c1 + 3) % 4, (c1 + 1) % 4
-        a = spot(w, k, left, cols=0)
-        arrived(w, k, 18, a)
-        send(w, k, 22, a, a, to(1))
-        b = spot(w, k, right, cols=1)
-        arrived(w, k, 19, b)
-        send(w, k, 23, b, b, to(3))
-        arrived(w, k, 20, spot(w, k, left, cols=1))
-        send(w, k, 25, spot(w, k, left), spot(w, k, left), sibling)
-        arrived(w, k, 21, spot(w, k, right, cols=0))
-        send(w, k, 26, spot(w, k, right), spot(w, k, right), sibling)
-
-    def ag1c(w, k):
-        c1, _, _ = at(k)
-        for cols in range(2):
-            far = spot(w, k, (c1 + 2) % 4, cols=cols)
-            arrived(w, k, 22 + cols, far)
-            send(w, k, 27 + cols, far, far, sibling)
-
-    def sib(w, k):
-        c1, _, _ = at(k)
-        for by, m in ((0, 24), (3, 25), (1, 26)):
-            arrived(w, k, m, spot(w, k, (c1 + by) % 4, c=1 - core))
-        for cols in range(2):
-            arrived(w, k, 27 + cols, spot(w, k, (c1 + 2) % 4, cols=cols, c=1 - core))
-
-    STEPS = ((rs1a,), (rs1b,), (rs1c, rs2a), (rs2b, rs3a), (rs3b,), (ag3b, ag2a), (ag2b, ag1a), (ag1b,), (ag1c,), (sib,))
-
-    def step(w, n):
-        for k in range(3):
-            for f in STEPS[n]:
-                f(w, k)
-
-    def own_a():
-        for by in (1, 2, 3):
-            c = pltpu.make_async_remote_copy(
-                src_ref=g.own.at[(me + by) % 4], dst_ref=g.own_in.at[by - 1], send_sem=xs_send.at[2 + by],
-                recv_sem=xs_recv.at[2 + by], device_id=device(along(pos, 1, by), core), device_id_type=MESH)
-            c.start()
-            started.append(c)
-
-    def own_b():
-        total = g.own[me].astype(F32)
-        for by in (1, 2, 3):
-            pltpu.make_async_remote_copy(
-                src_ref=g.own_in.at[by - 1], dst_ref=g.own_in.at[by - 1], send_sem=xs_send.at[2 + by],
-                recv_sem=xs_recv.at[2 + by], device_id=sibling, device_id_type=MESH).wait_recv()
-            total = total + g.own_in[by - 1].astype(F32)
-        mine = own_out.at[pl.ds(pl.multiple_of(64 * me, 16), 64)]
-        mine[...] = total.astype(BF)
-        for by in (1, 2, 3):
-            c = pltpu.make_async_remote_copy(
-                src_ref=mine, dst_ref=mine, send_sem=xs_send.at[5 + by],
-                recv_sem=xs_recv.at[5 + by], device_id=device(along(pos, 1, by), core), device_id_type=MESH)
-            c.start()
-            started.append(c)
-
-    def own_c():
-        for by in (1, 2, 3):
-            src = own_out.at[pl.ds(pl.multiple_of(64 * ((me + 4 - by) % 4), 16), 64)]
-            pltpu.make_async_remote_copy(
-                src_ref=src, dst_ref=src, send_sem=xs_send.at[5 + by],
-                recv_sem=xs_recv.at[5 + by], device_id=sibling, device_id_type=MESH).wait_recv()
-
-    def small_send(stage):
-        n = 1 if stage == 0 else 3
-        first = 0 if stage == 0 else 3 * stage - 2
-        for k in range(n):
-            to = sibling if stage == 0 else device(along(pos, stage - 1, k + 1), core)
-            c = pltpu.make_async_remote_copy(
-                src_ref=g.small_out_v.at[stage], dst_ref=g.small_in.at[first + k], send_sem=xs_send.at[9 + first + k],
-                recv_sem=xs_recv.at[9 + first + k], device_id=to, device_id_type=MESH)
-            c.start()
-            started.append(c)
-
-    def small_take(stage):
-        n = 1 if stage == 0 else 3
-        first = 0 if stage == 0 else 3 * stage - 2
-        total = g.small_out_v[stage]
-        for k in range(n):
-            ref = g.small_in.at[first + k]
-            pltpu.make_async_remote_copy(
-                src_ref=ref, dst_ref=ref, send_sem=xs_send.at[9 + first + k],
-                recv_sem=xs_recv.at[9 + first + k], device_id=sibling, device_id_type=MESH).wait_recv()
-            total = total + g.small_in[first + k]
-        g.small_out_v[stage + 1] = total
-
-    g.small_out_v[0] = g.sums[...]
-    small_send(0)
-    act_local.wait()
-    act_go.wait_recv()
-    dh_go.wait_recv()
-    for k in range(3):
-        g.w1_0[k] = mm_tn(g.f_act[:, 512 * k : 512 * k + 512], g.f_dh[...]).astype(BF)
-    step(0, 0)
-    du_local.wait()
-    du_go.wait_recv()
-    n2_go.wait_recv()
-    for k in range(3):
-        g.w1_1[k] = mm_tn(g.f_n2[...], g.f_du[:, 512 * k : 512 * k + 512]).astype(BF)
     dq_local.wait()
     for c in (dq_go, n1_go, o_go):
         c.wait_recv()
     left = mm_tn(g.f_n1[...], g.f_qo[:, 0:768]).astype(BF)
     g.w1_2[0] = left[:, 0:512]
     g.w1_2[1, :, 0:256] = left[:, 512:768]
-    step(0, 1)
-    step(1, 0)
 
     def right(factor):
         v = mm_tn(factor[...], g.f_qo[:, 768:1536]).astype(BF)
@@ -816,43 +863,44 @@
     def _():
         right(g.f_o)
 
-    step(0, 2)
-    step(1, 1)
-    step(2, 0)
-    own_a()
+    each(ring_a)
     small_take(0)
     small_send(1)
-    step(0, 3)
-    step(1, 2)
-    step(2, 1)
+    step(0, sum_first, rs2a)
+    step(1, sum_first, rs2a)
+    own_a(1)
+    each(ring_b)
+    step(0, rs2b, rs3a)
+    step(1, rs2b, rs3a)
     small_take(1)
     small_send(2)
-    step(0, 4)
-    step(1, 3)
-    step(2, 2)
-    own_b()
+    each(ring_c)
+    step(2, rs2a)
+    step(0, rs3b)
+    step(1, rs3b)
+    own_b(1)
+    step(0, ag3b, ag2a)
+    step(2, rs2b, rs3a)
+    step(1, ag3b, ag2a)
     small_take(2)
     small_send(3)
-    step(0, 5)
-    step(1, 4)
-    step(2, 3)
+    step(2, rs3b)
+    step(0, ag2b, ag1a)
+    step(2, ag3b, ag2a)
+    step(1, ag2b, ag1a)
     small_take(3)
     small_out[...] = g.small_out_v[4]
-    step(0, 6)
-    step(1, 5)
-    step(2, 4)
-    own_c()
-    step(0, 7)
-    step(1, 6)
-    step(2, 5)
-    step(0, 8)
-    step(1, 7)
-    step(2, 6)
-    step(1, 8)
-    step(2, 7)
-    step(2, 8)
+    own_c(0)
+    own_c(1)
+    step(0, ag1b)
+    step(2, ag2b, ag1a)
+    step(1, ag1b)
+    step(0, ag1c)
+    step(1, ag1c)
+    step(2, ag1b)
+    step(2, ag1c)
     for w in range(3):
-        step(w, 9)
+        step(w, sib)
     for c in started:
         c.wait_send()
 
@@ -879,7 +927,7 @@
         in_specs=[smem, smem] + [hbm] * (len(args) - 2),
         out_specs=[vmem] * 6,
         scratch_shapes=[pltpu.VMEM(s, t) for s, t in SCRATCH.values()]
-        + [dma((21,)), dma((8,)), dma((8,)), dma((9, NMSG)), dma((9, NMSG)), dma((19,)), dma((19,))],
+        + [dma((21,)), dma((11,)), dma((11,)), dma((9, NMSG)), dma((9, NMSG)), dma((25,)), dma((25,))],
         compiler_params=pltpu.CompilerParams(
             collective_id=0, has_side_effects=True, vmem_limit_bytes=VMEM_LIMIT
         ),
@@ -887,7 +935,7 @@
     )(*args)
 
 
-VMEM_LIMIT = 46 * 2**20
+VMEM_LIMIT = 48 * 2**20
 SMALL = ((LN1G, 1), (LN1S, 1), (BQV, 2), (BOUT, 1), (LN2G, 1), (LN2S, 1), (BUP, 4), (BDOWN, 1))
 
 

time: 157 us -> 144 us (0.917)
  Pallas kernels: 156 us -> 143 us
    pallas_call x1, Pallas kernels: 146 us -> 133 us  [passes(): pl.pallas_call(kernel, out_shape=[pltpu.VMEM((ROWS, D), BF), pltpu.VMEM((...]
where the time goes in v4:
time: 144 us
  Pallas kernels  143 us (99%)
    pallas_call x1, Pallas kernels, passes(): pl.pallas_call(kernel, out_shape=[pltpu.VMEM((ROWS, D), BF), pltpu.VMEM((...  133 us
    pallas_call x1, Pallas kernels, widen(): pl.pallas_call(widen_kernel, in_specs=[vmem] * 6, out_specs=[hbm] * 14, o...  9.85 us

profile of v4, /device:TPU:1, one launch (start us, length us, event | category | flops | bytes accessed | tf_op | source)
XLA Modules:
  0.0 143.8 jit_solution(11396407547077717713)
XLA Ops:
  0.7 133.1 %passes.1 = (bf16[256,768]{1,0:T(8,128)(2,1)S(1)}, bf16[256,768]{1,0:T(8,128)(2,1)S(1)}, f32[16,768]{1,0:T(8,128)S(1)}, bf16[768,3072]{1,0:T(8,128)(2,1)S(1)}, b...) custom-call(s32[2]{0:T(128)} %start_ref.1, s32[2]{0:T(128)} %length_ref.1, bf16[256,768]{1,0:T(8,128)(2,1)} %bitcast.4, ...), custom_call_target="tpu_custom_call" | custom-call | tf_op jit(solution)/shard_map/passes/pallas_call | solution.py:917
  133.8 9.9 %widen.1 = (bf16[256,768]{1,0:T(8,128)(2,1)}, bf16[256,768]{1,0:T(8,128)(2,1)}, f32[768,2304]{1,0:T(8,128)}, f32[768,768]{1,0:T(8,128)}, f32[768,3072]{1,0:T(8,1...) custom-call(bf16[256,768]{1,0:T(8,128)(2,1)S(1)} %get-tuple-element., ...), custom_call_target="tpu_custom_call" | custom-call | tf_op jit(solution)/shard_map/widen/pallas_call | solution.py:983

commit v5 on v4

--- a/solution.py
+++ b/solution.py
@@ -126,7 +126,7 @@
     kall=((3, 128, D), BF), vall=((3, 128, D), BF), pm=((3, 192, 128), F32),
     xh2m=((3, 16, D), F32), rs2m=((3, 16, 1), F32), gpm=((3, 16, FF), F32),
     slots=((4, 16, D), BF), slot_out=((16, D), BF),
-    e_own=((16, D), BF), du_own=((16, FF), BF), da_own=((16, D), BF), dqkv_own=((80, 3 * D), BF),
+    e_own=((16, D), BF), du_own=((16, FF), BF), dqo_own=((80, FF), BF), c_qo=((80, 1536), BF),
     dx_mini=((16, D), F32), dxm_own=((16, D), BF), dxb_own=((64, D), F32),
     f_n1=((512, D), BF), f_o=((512, D), BF), f_n2=((512, D), BF), f_dh=((512, D), BF),
     f_qo=((512, 1536), BF), f_du=((512, 1536), BF), f_act=((512, 1536), BF),
@@ -137,7 +137,7 @@
     in2_0=((3, 3, 96, 256), BF), in2_1=((3, 3, 192, 128), BF), in2_2=((3, 3, 48, 512), BF),
     w3_0=((3, 96, 256), BF), w3_1=((3, 192, 128), BF), w3_2=((3, 48, 512), BF),
     in3_0=((3, 3, 48, 128), BF), in3_1=((3, 3, 48, 128), BF), in3_2=((3, 3, 48, 128), BF),
-    act_mini=((16, FF), BF), c_act=((32, 1536), BF), c_n2=((32, D), BF), c_e=((32, D), BF), c_du=((32, 1536), BF),
+    spread=((2, 2, TOP, 16), BF), act_mini=((16, FF), BF), c_act=((32, 1536), BF), c_n2=((32, D), BF), c_e=((32, D), BF), c_du=((32, 1536), BF),
     ca_0=((3, 4, 32, 384), BF), cg_0=((3, 4, 32, 256), BF), ca_1=((3, 4, 32, D), BF), cg_1=((3, 4, 32, 128), BF),
     own=((2, 4, 32, D), BF), own_in=((2, 3, 32, D), BF),
     small_in=((10, 16, D), F32),
@@ -178,6 +178,8 @@
         for k in range(src.shape[0] // D):
             par_loads.append(load(9 + first + k, src.at[pl.ds(k * D, D)], g.par.at[first + k]))
     wq_load = load(2, wq_hbm, g.wq)
+    w_loads = [load(3, wo_hbm, g.wo), load(4, wu_hbm, g.wu), load(5, wd_hbm, g.wd)]
+    cot_load = load(6, cot_hbm, g.cot_v)
 
     def row(i, n=1):
         if n == 1:
@@ -215,8 +217,6 @@
         g.f_n1[rows, :] = (xhat * row(LN1G) + row(LN1S)).astype(BF)
         return 0
 
-    w_loads = [load(3, wo_hbm, g.wo), load(4, wu_hbm, g.wu), load(5, wd_hbm, g.wd)]
-    cot_load = load(6, cot_hbm, g.cot_v)
     lax.fori_loop(0, 8, norm_one, 0)
     wq_load.wait()
     qkv_bias = (row(BQV), jnp.zeros((1, D), F32), row(BQV + 1))
@@ -352,6 +352,15 @@
     def half(ref, which, width):
         return ref.at[:, pl.ds(pl.multiple_of(which * width, 128), width)]
 
+    mini_lo, mini_hi = pl.ds(0, 16), pl.ds(16, 16)
+    g.act_mini[...] = mm(pick, g.act[...]).astype(BF)
+    g.c_act[0:16, :] = g.act_mini[:, pl.ds(pl.multiple_of(core * 1536, 128), 1536)]
+    g.c_n2[0:16, :] = mm(pick, g.f_n2[0:256, :]).astype(BF)
+    for q in range(2):
+        g.spread[0, q] = place[q]
+    spread_go = to_sibling(11, g.spread.at[0], g.spread.at[1])
+    c_act_go = to_sibling(7, half(g.act_mini, 1 - core, 1536), g.c_act.at[mini_hi])
+    c_n2_go = to_sibling(12, g.c_n2.at[mini_lo], g.c_n2.at[mini_hi])
     cot_load.wait()
     dh_go = to_sibling(4, g.f_dh.at[lo], g.f_dh.at[hi])
     act_go = to_sibling(3, half(g.act, 1 - core, 1536), g.f_act.at[hi])
@@ -359,12 +368,302 @@
     n2_go = to_sibling(2, g.f_n2.at[lo], g.f_n2.at[hi])
     n1_go = to_sibling(0, g.f_n1.at[lo], g.f_n1.at[hi])
     o_go = to_sibling(1, g.f_o.at[lo], g.f_o.at[hi])
-    mini_lo, mini_hi = pl.ds(0, 16), pl.ds(16, 16)
-    g.act_mini[...] = mm(pick, g.act[...]).astype(BF)
-    g.c_act[0:16, :] = g.act_mini[:, pl.ds(pl.multiple_of(core * 1536, 128), 1536)]
-    g.c_n2[0:16, :] = mm(pick, g.f_n2[0:256, :]).astype(BF)
-    c_act_go = to_sibling(7, half(g.act_mini, 1 - core, 1536), g.c_act.at[mini_hi])
-    c_n2_go = to_sibling(8, g.c_n2.at[mini_lo], g.c_n2.at[mini_hi])
+
+    def msg(w, k, m, src, dst, to):
+        i = 3 * w + k
+        return pltpu.make_async_remote_copy(src_ref=src, dst_ref=dst, send_sem=ssem.at[i, m], recv_sem=rsem.at[i, m],
+                                            device_id=to, device_id_type=MESH)
+
+    def send(w, k, m, src, dst, to):
+        c = msg(w, k, m, src, dst, to)
+        c.start()
+        started.append(c)
+
+    def arrived(w, k, m, dst):
+        msg(w, k, m, dst, dst, sibling).wait_recv()
+
+    w1s, in1s = (g.w1_0, g.w1_1, g.w1_2), (g.in1_0, g.in1_1, g.in1_2)
+    w2s, in2s = (g.w2_0, g.w2_1, g.w2_2), (g.in2_0, g.in2_1, g.in2_2)
+    w3s, in3s = (g.w3_0, g.w3_1, g.w3_2), (g.in3_0, g.in3_1, g.in3_2)
+    cas, cgs = (g.ca_0, g.ca_1), (g.cg_0, g.cg_1)
+    outs = (w_d, w_u, w_qo)
+    memo = {}
+
+    def near(axis, by):
+        if (axis, by) not in memo:
+            there = along(pos, axis, by)
+            memo[axis, by] = (device(there, core), there[axis])
+        return memo[axis, by]
+
+    def ds(i, n, m):
+        return pl.ds(i if isinstance(i, int) else pl.multiple_of(i, m), n)
+
+    def window(ref, r0, l0, shape):
+        return ref.at[ds(r0, shape[0], 16), ds(l0, shape[1], 128)]
+
+    def block(w, c1):
+        return ((384 * c1, 0), (0, 128 * c1), (192 * c1, 0))[w]
+
+    def piece(w, c1, c2):
+        r, l = block(w, c1)
+        return r + PIECES[w][0] * c2, l
+
+    def inner(w, c3):
+        return ((48 * lax.div(c3, 2), 128 * lax.rem(c3, 2)), (48 * c3, 0), (0, 128 * c3))[w]
+
+    HALVES = ((384, 128), (384, 128), (192, 256))
+
+    def half_of(w, cols):
+        return ((0, 128 * cols), (384 * cols, 0), (0, 256 * cols))[w]
+
+    def send_first(w, k):
+        axis = ORDERS[k][0]
+        for d in (1, 2, 3):
+            to, c = near(axis, d)
+            send(w, k, d - 1, window(w1s[w].at[k], *block(w, c), BLOCKS[w]), in1s[w].at[k, d - 1], to)
+
+    def send_left(k):
+        axis = ORDERS[k][0]
+        mine = near(axis, 0)[1]
+        g.ca_0[k, 0] = g.c_act[:, ds(384 * mine, 384, 128)]
+        g.ca_1[k, 0] = g.c_n2[...]
+        for d in (1, 2, 3):
+            to, c = near(axis, d)
+            send(0, k, 2 + d, window(g.c_act, 0, 384 * c, (32, 384)), g.ca_0.at[k, d], to)
+            send(1, k, 2 + d, g.c_n2, g.ca_1.at[k, d], to)
+
+    def send_right(k):
+        axis = ORDERS[k][0]
+        mine = near(axis, 0)[1]
+        g.cg_0[k, 0] = g.c_e[:, 256 * k : 256 * k + 256]
+        g.cg_1[k, 0] = g.c_du[:, ds(512 * k + 128 * mine, 128, 128)]
+        for d in (1, 2, 3):
+            to, c = near(axis, d)
+            send(0, k, 28 + d, window(g.c_e, 0, 256 * k, (32, 256)), g.cg_0.at[k, d], to)
+            send(1, k, 28 + d, window(g.c_du, 0, 512 * k + 128 * c, (32, 128)), g.cg_1.at[k, d], to)
+
+    def sum_first(w, k):
+        mine = near(ORDERS[k][0], 0)[1]
+        for d in (1, 2, 3):
+            arrived(w, k, 2 + d, cas[w].at[k, d])
+            arrived(w, k, 28 + d, cgs[w].at[k, d])
+            arrived(w, k, d - 1, in1s[w].at[k, d - 1])
+        n = BLOCKS[w][0]
+        total = mm_tn(cas[w][k].reshape(128, n), cgs[w][k].reshape(128, BLOCKS[w][1]))
+        total = total + window(w1s[w].at[k], *block(w, mine), BLOCKS[w])[...].astype(F32)
+        for d in range(3):
+            total = total + in1s[w][k, d].astype(F32)
+        w2s[w][k] = total.astype(BF)
+
+    A, B = pl.ds(0, 256), pl.ds(256, 256)
+
+    def ring_a(k):
+        axis = ORDERS[k][0]
+        w1, inn = g.w1_2.at[k], g.in1_2.at[k]
+        (up, c_up), (dn, c_dn), (_, far) = near(axis, 1), near(axis, 3), near(axis, 2)
+
+        def blk(c):
+            return ds(c * 192, 192, 16)
+
+        send(2, k, 0, w1.at[blk(far), A], g.relay.at[k, 0], up)
+        send(2, k, 1, w1.at[blk(far), B], g.relay.at[k, 1], dn)
+        send(2, k, 2, w1.at[blk(c_up), B], inn.at[0, :, B], up)
+        send(2, k, 3, w1.at[blk(c_dn), A], inn.at[1, :, A], dn)
+
+    def ring_b(k):
+        axis = ORDERS[k][0]
+        for side, by, cols in ((0, 1, A), (1, 3, B)):
+            to, c = near(axis, by)
+            arrived(2, k, side, g.relay.at[k, side])
+            g.relay[k, side] = (g.relay[k, side].astype(F32) + g.w1_2[k, ds(c * 192, 192, 16), cols].astype(F32)).astype(BF)
+            send(2, k, 4 + side, g.relay.at[k, side], g.in1_2.at[k, side, :, cols], to)
+
+    def ring_c(k):
+        inn = g.in1_2
+        arrived(2, k, 2, inn.at[k, 0, :, B])
+        arrived(2, k, 3, inn.at[k, 1, :, A])
+        arrived(2, k, 4, inn.at[k, 0, :, A])
+        arrived(2, k, 5, inn.at[k, 1, :, B])
+        mine = near(ORDERS[k][0], 0)[1]
+        total = g.w1_2[k, ds(mine * 192, 192, 16), :].astype(F32) + inn[k, 0].astype(F32) + inn[k, 1].astype(F32)
+        g.w2_2[k] = total.astype(BF)
+
+    def rs2a(w, k):
+        axis = ORDERS[k][1]
+        for d in (1, 2, 3):
+            to, c = near(axis, d)
+            send(w, k, 5 + d, window(w2s[w].at[k], PIECES[w][0] * c, 0, PIECES[w]), in2s[w].at[k, d - 1], to)
+
+    def rs2b(w, k):
+        mine = near(ORDERS[k][1], 0)[1]
+        for d in (1, 2, 3):
+            arrived(w, k, 5 + d, in2s[w].at[k, d - 1])
+        total = window(w2s[w].at[k], PIECES[w][0] * mine, 0, PIECES[w])[...].astype(F32)
+        for d in range(3):
+            total = total + in2s[w][k, d].astype(F32)
+        w3s[w][k] = total.astype(BF)
+
+    def rs3a(w, k):
+        axis = ORDERS[k][2]
+        for d in (1, 2, 3):
+            to, c = near(axis, d)
+            send(w, k, 8 + d, window(w3s[w].at[k], *inner(w, c), SUB), in3s[w].at[k, d - 1], to)
+
+    def out_window(w, k, r, l, shape, c=None):
+        c = core if c is None else c
+        r0, l0 = (c * 1536, 256 * k) if w == 0 else (0, c * 1536 + 512 * k)
+        return window(outs[w], r0 + r, l0 + l, shape)
+
+    def out_block(w, k, c1, cols=None, c=None):
+        r, l = block(w, c1)
+        if cols is None:
+            return out_window(w, k, r, l, BLOCKS[w], c)
+        r1, l1 = half_of(w, cols)
+        return out_window(w, k, r + r1, l + l1, HALVES[w], c)
+
+    def out_piece(w, k, c1, c2):
+        return out_window(w, k, *piece(w, c1, c2), PIECES[w])
+
+    def out_sub(w, k, c1, c2, c3):
+        (r, l), (r1, l1) = piece(w, c1, c2), inner(w, c3)
+        return out_window(w, k, r + r1, l + l1, SUB)
+
+    def at(k):
+        return tuple(near(a, 0)[1] for a in ORDERS[k])
+
+    def rs3b(w, k):
+        axis = ORDERS[k][2]
+        for d in (1, 2, 3):
+            arrived(w, k, 8 + d, in3s[w].at[k, d - 1])
+        total = window(w3s[w].at[k], *inner(w, near(axis, 0)[1]), SUB)[...].astype(F32)
+        for d in range(3):
+            total = total + in3s[w][k, d].astype(F32)
+        mine = out_sub(w, k, *at(k))
+        mine[...] = total.astype(BF)
+        for d in (1, 2, 3):
+            send(w, k, 11 + d, mine, mine, near(axis, d)[0])
+
+    def ag3b(w, k):
+        c1, c2, _ = at(k)
+        for d in (1, 2, 3):
+            arrived(w, k, 11 + d, out_sub(w, k, c1, c2, near(ORDERS[k][2], 4 - d)[1]))
+
+    def ag2a(w, k):
+        c1, c2, _ = at(k)
+        mine = out_piece(w, k, c1, c2)
+        for d in (1, 2, 3):
+            send(w, k, 14 + d, mine, mine, near(ORDERS[k][1], d)[0])
+
+    def ag2b(w, k):
+        c1 = at(k)[0]
+        for d in (1, 2, 3):
+            arrived(w, k, 14 + d, out_piece(w, k, c1, near(ORDERS[k][1], 4 - d)[1]))
+
+    def ag1a(w, k):
+        axis = ORDERS[k][0]
+        c1 = at(k)[0]
+        for cols, m in ((0, 18), (1, 20)):
+            up = out_block(w, k, c1, cols)
+            send(w, k, m, up, up, near(axis, 1)[0])
+            dn = out_block(w, k, c1, 1 - cols)
+            send(w, k, m + 1, dn, dn, near(axis, 3)[0])
+        mine = out_block(w, k, c1)
+        send(w, k, 24, mine, mine, sibling)
+
+    def ag1b(w, k):
+        axis = ORDERS[k][0]
+        left, right = near(axis, 3)[1], near(axis, 1)[1]
+        a = out_block(w, k, left, 0)
+        arrived(w, k, 18, a)
+        send(w, k, 22, a, a, near(axis, 1)[0])
+        b = out_block(w, k, right, 1)
+        arrived(w, k, 19, b)
+        send(w, k, 23, b, b, near(axis, 3)[0])
+        arrived(w, k, 20, out_block(w, k, left, 1))
+        send(w, k, 25, out_block(w, k, left), out_block(w, k, left), sibling)
+        arrived(w, k, 21, out_block(w, k, right, 0))
+        send(w, k, 26, out_block(w, k, right), out_block(w, k, right), sibling)
+
+    def ag1c(w, k):
+        far = near(ORDERS[k][0], 2)[1]
+        for cols in range(2):
+            v = out_block(w, k, far, cols)
+            arrived(w, k, 22 + cols, v)
+            send(w, k, 27 + cols, v, v, sibling)
+
+    def sib(w, k):
+        axis = ORDERS[k][0]
+        for by, m in ((0, 24), (3, 25), (1, 26)):
+            arrived(w, k, m, out_block(w, k, near(axis, by)[1], c=1 - core))
+        for cols in range(2):
+            arrived(w, k, 27 + cols, out_block(w, k, near(axis, 2)[1], cols, c=1 - core))
+
+    def step(w, *fs):
+        for f in fs:
+            for k in range(3):
+                f(w, k)
+
+    def each(f):
+        for k in range(3):
+            f(k)
+
+    def own_msg(i, src, dst, to):
+        return pltpu.make_async_remote_copy(src_ref=src, dst_ref=dst, send_sem=xs_send.at[i], recv_sem=xs_recv.at[i],
+                                            device_id=to, device_id_type=MESH)
+
+    def own_rows(part, b):
+        return ds(128 * lax.div(b, 2) + 64 * (1 - part) + 32 * lax.rem(b, 2), 32, 16)
+
+    def own_a(part):
+        for b in range(4):
+            first = 128 * (b // 2) + 64 * (1 - part) + 32 * (b % 2)
+            g.own[part, b] = g.dx[first : first + 32, :].astype(BF)
+        for by in (1, 2, 3):
+            to, c = near(1, by)
+            m = own_msg(3 + 6 * part + by - 1, g.own.at[part, c], g.own_in.at[part, by - 1], to)
+            m.start()
+            started.append(m)
+
+    def own_b(part):
+        total = g.own[part, me].astype(F32)
+        for by in (1, 2, 3):
+            ref = g.own_in.at[part, by - 1]
+            own_msg(3 + 6 * part + by - 1, ref, ref, sibling).wait_recv()
+            total = total + g.own_in[part, by - 1].astype(F32)
+        mine = own_out.at[own_rows(part, me)]
+        mine[...] = total.astype(BF)
+        for by in (1, 2, 3):
+            m = own_msg(6 + 6 * part + by - 1, mine, mine, near(1, by)[0])
+            m.start()
+            started.append(m)
+
+    def own_c(part):
+        for by in (1, 2, 3):
+            ref = own_out.at[own_rows(part, near(1, 4 - by)[1])]
+            own_msg(6 + 6 * part + by - 1, ref, ref, sibling).wait_recv()
+
+    def small_send(stage):
+        n = 1 if stage == 0 else 3
+        first = 0 if stage == 0 else 3 * stage - 2
+        for k in range(n):
+            to = sibling if stage == 0 else near(stage - 1, k + 1)[0]
+            c = pltpu.make_async_remote_copy(
+                src_ref=g.small_out_v.at[stage], dst_ref=g.small_in.at[first + k], send_sem=xs_send.at[15 + first + k],
+                recv_sem=xs_recv.at[15 + first + k], device_id=to, device_id_type=MESH)
+            c.start()
+            started.append(c)
+
+    def small_take(stage):
+        n = 1 if stage == 0 else 3
+        first = 0 if stage == 0 else 3 * stage - 2
+        total = g.small_out_v[stage]
+        for k in range(n):
+            ref = g.small_in.at[first + k]
+            pltpu.make_async_remote_copy(
+                src_ref=ref, dst_ref=ref, send_sem=xs_send.at[15 + first + k],
+                recv_sem=xs_recv.at[15 + first + k], device_id=sibling, device_id_type=MESH).wait_recv()
+            total = total + g.small_in[first + k]
+        g.small_out_v[stage + 1] = total
 
     for k in range(4):
         c = slice(k * D, (k + 1) * D)
@@ -374,6 +673,9 @@
     du_go = to_sibling(5, half(g.du, 1 - core, 1536), g.f_du.at[hi])
     du_local = local(3, half(g.du, core, 1536), g.f_du.at[lo])
     g.sums[BDOWN : BDOWN + 1, :] = column_sum(g.cot_v[...].astype(F32))
+    c_act_go.wait_recv()
+    c_n2_go.wait_recv()
+    each(send_left)
     g.tmp[...] = mm_nt(g.du[...], g.wu[...])
     zero8 = jnp.zeros((8, D), F32)
 
@@ -423,302 +725,6 @@
     for i, a in zip((LN1G, LN1S, BQV, BQV + 1), acc):
         g.sums[i : i + 1, :] = jnp.sum(a, 0, keepdims=True)
 
-    def msg(w, k, m, src, dst, to):
-        i = 3 * w + k
-        return pltpu.make_async_remote_copy(src_ref=src, dst_ref=dst, send_sem=ssem.at[i, m], recv_sem=rsem.at[i, m],
-                                            device_id=to, device_id_type=MESH)
-
-    def send(w, k, m, src, dst, to):
-        c = msg(w, k, m, src, dst, to)
-        c.start()
-        started.append(c)
-
-    def arrived(w, k, m, dst):
-        msg(w, k, m, dst, dst, sibling).wait_recv()
-
-    w1s, in1s = (g.w1_0, g.w1_1, g.w1_2), (g.in1_0, g.in1_1, g.in1_2)
-    w2s, in2s = (g.w2_0, g.w2_1, g.w2_2), (g.in2_0, g.in2_1, g.in2_2)
-    w3s, in3s = (g.w3_0, g.w3_1, g.w3_2), (g.in3_0, g.in3_1, g.in3_2)
-    cas, cgs = (g.ca_0, g.ca_1), (g.cg_0, g.cg_1)
-    outs = (w_d, w_u, w_qo)
-    memo = {}
-
-    def near(axis, by):
-        if (axis, by) not in memo:
-            there = along(pos, axis, by)
-            memo[axis, by] = (device(there, core), there[axis])
-        return memo[axis, by]
-
-    def ds(i, n, m):
-        return pl.ds(i if isinstance(i, int) else pl.multiple_of(i, m), n)
-
-    def window(ref, r0, l0, shape):
-        return ref.at[ds(r0, shape[0], 16), ds(l0, shape[1], 128)]
-
-    def block(w, c1):
-        return ((384 * c1, 0), (0, 128 * c1), (192 * c1, 0))[w]
-
-    def piece(w, c1, c2):
-        r, l = block(w, c1)
-        return r + PIECES[w][0] * c2, l
-
-    def inner(w, c3):
-        return ((48 * lax.div(c3, 2), 128 * lax.rem(c3, 2)), (48 * c3, 0), (0, 128 * c3))[w]
-
-    HALVES = ((384, 128), (384, 128), (192, 256))
-
-    def half_of(w, cols):
-        return ((0, 128 * cols), (384 * cols, 0), (0, 256 * cols))[w]
-
-    def send_first(w, k):
-        axis = ORDERS[k][0]
-        for d in (1, 2, 3):
-            to, c = near(axis, d)
-            send(w, k, d - 1, window(w1s[w].at[k], *block(w, c), BLOCKS[w]), in1s[w].at[k, d - 1], to)
-
-    def send_left(k):
-        axis = ORDERS[k][0]
-        mine = near(axis, 0)[1]
-        g.ca_0[k, 0] = g.c_act[:, ds(384 * mine, 384, 128)]
-        g.ca_1[k, 0] = g.c_n2[...]
-        for d in (1, 2, 3):
-            to, c = near(axis, d)
-            send(0, k, 2 + d, window(g.c_act, 0, 384 * c, (32, 384)), g.ca_0.at[k, d], to)
-            send(1, k, 2 + d, g.c_n2, g.ca_1.at[k, d], to)
-
-    def send_right(k):
-        axis = ORDERS[k][0]
-        mine = near(axis, 0)[1]
-        g.cg_0[k, 0] = g.c_e[:, 256 * k : 256 * k + 256]
-        g.cg_1[k, 0] = g.c_du[:, ds(512 * k + 128 * mine, 128, 128)]
-        for d in (1, 2, 3):
-            to, c = near(axis, d)
-            send(0, k, 28 + d, window(g.c_e, 0, 256 * k, (32, 256)), g.cg_0.at[k, d], to)
-            send(1, k, 28 + d, window(g.c_du, 0, 512 * k + 128 * c, (32, 128)), g.cg_1.at[k, d], to)
-
-    def sum_first(w, k):
-        mine = near(ORDERS[k][0], 0)[1]
-        for d in (1, 2, 3):
-            arrived(w, k, 2 + d, cas[w].at[k, d])
-            arrived(w, k, 28 + d, cgs[w].at[k, d])
-            arrived(w, k, d - 1, in1s[w].at[k, d - 1])
-        n = BLOCKS[w][0]
-        total = mm_tn(cas[w][k].reshape(128, n), cgs[w][k].reshape(128, BLOCKS[w][1]))
-        total = total + window(w1s[w].at[k], *block(w, mine), BLOCKS[w])[...].astype(F32)
-        for d in range(3):
-            total = total + in1s[w][k, d].astype(F32)
-        w2s[w][k] = total.astype(BF)
-
-    A, B = pl.ds(0, 256), pl.ds(256, 256)
-
-    def ring_a(k):
-        axis = ORDERS[k][0]
-        w1, inn = g.w1_2.at[k], g.in1_2.at[k]
-        (up, c_up), (dn, c_dn), (_, far) = near(axis, 1), near(axis, 3), near(axis, 2)
-
-        def blk(c):
-            return ds(c * 192, 192, 16)
-
-        send(2, k, 0, w1.at[blk(far), A], g.relay.at[k, 0], up)
-        send(2, k, 1, w1.at[blk(far), B], g.relay.at[k, 1], dn)
-        send(2, k, 2, w1.at[blk(c_up), B], inn.at[0, :, B], up)
-        send(2, k, 3, w1.at[blk(c_dn), A], inn.at[1, :, A], dn)
-
-    def ring_b(k):
-        axis = ORDERS[k][0]
-        for side, by, cols in ((0, 1, A), (1, 3, B)):
-            to, c = near(axis, by)
-            arrived(2, k, side, g.relay.at[k, side])
-            g.relay[k, side] = (g.relay[k, side].astype(F32) + g.w1_2[k, ds(c * 192, 192, 16), cols].astype(F32)).astype(BF)
-            send(2, k, 4 + side, g.relay.at[k, side], g.in1_2.at[k, side, :, cols], to)
-
-    def ring_c(k):
-        inn = g.in1_2
-        arrived(2, k, 2, inn.at[k, 0, :, B])
-        arrived(2, k, 3, inn.at[k, 1, :, A])
-        arrived(2, k, 4, inn.at[k, 0, :, A])
-        arrived(2, k, 5, inn.at[k, 1, :, B])
-        mine = near(ORDERS[k][0], 0)[1]
-        total = g.w1_2[k, ds(mine * 192, 192, 16), :].astype(F32) + inn[k, 0].astype(F32) + inn[k, 1].astype(F32)
-        g.w2_2[k] = total.astype(BF)
-
-    def rs2a(w, k):
-        axis = ORDERS[k][1]
-        for d in (1, 2, 3):
-            to, c = near(axis, d)
-            send(w, k, 5 + d, window(w2s[w].at[k], PIECES[w][0] * c, 0, PIECES[w]), in2s[w].at[k, d - 1], to)
-
-    def rs2b(w, k):
-        mine = near(ORDERS[k][1], 0)[1]
-        for d in (1, 2, 3):
-            arrived(w, k, 5 + d, in2s[w].at[k, d - 1])
-        total = window(w2s[w].at[k], PIECES[w][0] * mine, 0, PIECES[w])[...].astype(F32)
-        for d in range(3):
-            total = total + in2s[w][k, d].astype(F32)
-        w3s[w][k] = total.astype(BF)
-
-    def rs3a(w, k):
-        axis = ORDERS[k][2]
-        for d in (1, 2, 3):
-            to, c = near(axis, d)
-            send(w, k, 8 + d, window(w3s[w].at[k], *inner(w, c), SUB), in3s[w].at[k, d - 1], to)
-
-    def out_window(w, k, r, l, shape, c=None):
-        c = core if c is None else c
-        r0, l0 = (c * 1536, 256 * k) if w == 0 else (0, c * 1536 + 512 * k)
-        return window(outs[w], r0 + r, l0 + l, shape)
-
-    def out_block(w, k, c1, cols=None, c=None):
-        r, l = block(w, c1)
-        if cols is None:
-            return out_window(w, k, r, l, BLOCKS[w], c)
-        r1, l1 = half_of(w, cols)
-        return out_window(w, k, r + r1, l + l1, HALVES[w], c)
-
-    def out_piece(w, k, c1, c2):
-        return out_window(w, k, *piece(w, c1, c2), PIECES[w])
-
-    def out_sub(w, k, c1, c2, c3):
-        (r, l), (r1, l1) = piece(w, c1, c2), inner(w, c3)
-        return out_window(w, k, r + r1, l + l1, SUB)
-
-    def at(k):
-        return tuple(near(a, 0)[1] for a in ORDERS[k])
-
-    def rs3b(w, k):
-        axis = ORDERS[k][2]
-        for d in (1, 2, 3):
-            arrived(w, k, 8 + d, in3s[w].at[k, d - 1])
-        total = window(w3s[w].at[k], *inner(w, near(axis, 0)[1]), SUB)[...].astype(F32)
-        for d in range(3):
-            total = total + in3s[w][k, d].astype(F32)
-        mine = out_sub(w, k, *at(k))
-        mine[...] = total.astype(BF)
-        for d in (1, 2, 3):
-            send(w, k, 11 + d, mine, mine, near(axis, d)[0])
-
-    def ag3b(w, k):
-        c1, c2, _ = at(k)
-        for d in (1, 2, 3):
-            arrived(w, k, 11 + d, out_sub(w, k, c1, c2, near(ORDERS[k][2], 4 - d)[1]))
-
-    def ag2a(w, k):
-        c1, c2, _ = at(k)
-        mine = out_piece(w, k, c1, c2)
-        for d in (1, 2, 3):
-            send(w, k, 14 + d, mine, mine, near(ORDERS[k][1], d)[0])
-
-    def ag2b(w, k):
-        c1 = at(k)[0]
-        for d in (1, 2, 3):
-            arrived(w, k, 14 + d, out_piece(w, k, c1, near(ORDERS[k][1], 4 - d)[1]))
-
-    def ag1a(w, k):
-        axis = ORDERS[k][0]
-        c1 = at(k)[0]
-        for cols, m in ((0, 18), (1, 20)):
-            up = out_block(w, k, c1, cols)
-            send(w, k, m, up, up, near(axis, 1)[0])
-            dn = out_block(w, k, c1, 1 - cols)
-            send(w, k, m + 1, dn, dn, near(axis, 3)[0])
-        mine = out_block(w, k, c1)
-        send(w, k, 24, mine, mine, sibling)
-
-    def ag1b(w, k):
-        axis = ORDERS[k][0]
-        left, right = near(axis, 3)[1], near(axis, 1)[1]
-        a = out_block(w, k, left, 0)
-        arrived(w, k, 18, a)
-        send(w, k, 22, a, a, near(axis, 1)[0])
-        b = out_block(w, k, right, 1)
-        arrived(w, k, 19, b)
-        send(w, k, 23, b, b, near(axis, 3)[0])
-        arrived(w, k, 20, out_block(w, k, left, 1))
-        send(w, k, 25, out_block(w, k, left), out_block(w, k, left), sibling)
-        arrived(w, k, 21, out_block(w, k, right, 0))
-        send(w, k, 26, out_block(w, k, right), out_block(w, k, right), sibling)
-
-    def ag1c(w, k):
-        far = near(ORDERS[k][0], 2)[1]
-        for cols in range(2):
-            v = out_block(w, k, far, cols)
-            arrived(w, k, 22 + cols, v)
-            send(w, k, 27 + cols, v, v, sibling)
-
-    def sib(w, k):
-        axis = ORDERS[k][0]
-        for by, m in ((0, 24), (3, 25), (1, 26)):
-            arrived(w, k, m, out_block(w, k, near(axis, by)[1], c=1 - core))
-        for cols in range(2):
-            arrived(w, k, 27 + cols, out_block(w, k, near(axis, 2)[1], cols, c=1 - core))
-
-    def step(w, *fs):
-        for f in fs:
-            for k in range(3):
-                f(w, k)
-
-    def each(f):
-        for k in range(3):
-            f(k)
-
-    def own_msg(i, src, dst, to):
-        return pltpu.make_async_remote_copy(src_ref=src, dst_ref=dst, send_sem=xs_send.at[i], recv_sem=xs_recv.at[i],
-                                            device_id=to, device_id_type=MESH)
-
-    def own_rows(part, b):
-        return ds(128 * lax.div(b, 2) + 64 * (1 - part) + 32 * lax.rem(b, 2), 32, 16)
-
-    def own_a(part):
-        for b in range(4):
-            first = 128 * (b // 2) + 64 * (1 - part) + 32 * (b % 2)
-            g.own[part, b] = g.dx[first : first + 32, :].astype(BF)
-        for by in (1, 2, 3):
-            to, c = near(1, by)
-            m = own_msg(3 + 6 * part + by - 1, g.own.at[part, c], g.own_in.at[part, by - 1], to)
-            m.start()
-            started.append(m)
-
-    def own_b(part):
-        total = g.own[part, me].astype(F32)
-        for by in (1, 2, 3):
-            ref = g.own_in.at[part, by - 1]
-            own_msg(3 + 6 * part + by - 1, ref, ref, sibling).wait_recv()
-            total = total + g.own_in[part, by - 1].astype(F32)
-        mine = own_out.at[own_rows(part, me)]
-        mine[...] = total.astype(BF)
-        for by in (1, 2, 3):
-            m = own_msg(6 + 6 * part + by - 1, mine, mine, near(1, by)[0])
-            m.start()
-            started.append(m)
-
-    def own_c(part):
-        for by in (1, 2, 3):
-            ref = own_out.at[own_rows(part, near(1, 4 - by)[1])]
-            own_msg(6 + 6 * part + by - 1, ref, ref, sibling).wait_recv()
-
-    def small_send(stage):
-        n = 1 if stage == 0 else 3
-        first = 0 if stage == 0 else 3 * stage - 2
-        for k in range(n):
-            to = sibling if stage == 0 else near(stage - 1, k + 1)[0]
-            c = pltpu.make_async_remote_copy(
-                src_ref=g.small_out_v.at[stage], dst_ref=g.small_in.at[first + k], send_sem=xs_send.at[15 + first + k],
-                recv_sem=xs_recv.at[15 + first + k], device_id=to, device_id_type=MESH)
-            c.start()
-            started.append(c)
-
-    def small_take(stage):
-        n = 1 if stage == 0 else 3
-        first = 0 if stage == 0 else 3 * stage - 2
-        total = g.small_out_v[stage]
-        for k in range(n):
-            ref = g.small_in.at[first + k]
-            pltpu.make_async_remote_copy(
-                src_ref=ref, dst_ref=ref, send_sem=xs_send.at[15 + first + k],
-                recv_sem=xs_recv.at[15 + first + k], device_id=sibling, device_id_type=MESH).wait_recv()
-            total = total + g.small_in[first + k]
-        g.small_out_v[stage + 1] = total
-
     g.slot_out[...] = mm(pick, g.dx[...].astype(BF)).astype(BF)
     for by in (1, 2, 3):
         c = pltpu.make_async_remote_copy(
@@ -729,8 +735,7 @@
     g.dx_mini[...] = jnp.zeros((16, D), F32)
     g.e_own[...] = jnp.zeros((16, D), BF)
     g.du_own[...] = jnp.zeros((16, FF), BF)
-    g.da_own[...] = jnp.zeros((16, D), BF)
-    g.dqkv_own[...] = jnp.zeros((80, 3 * D), BF)
+    g.dqo_own[...] = jnp.zeros((80, FF), BF)
     g.dxm_own[...] = jnp.zeros((16, D), BF)
     g.dxb_own[...] = jnp.zeros((64, D), F32)
     dh_go.wait_recv()
@@ -748,9 +753,8 @@
     for k in range(3):
         g.w1_1[k] = mm_tn(g.f_n2[...], g.f_du[:, 512 * k : 512 * k + 512]).astype(BF)
     each(lambda k: send_first(1, k))
-    c_act_go.wait_recv()
-    c_n2_go.wait_recv()
-    each(send_left)
+    dq_go = to_sibling(6, half(g.dqo, 1 - core, 1536), g.f_qo.at[hi])
+    dq_local = local(4, half(g.dqo, core, 1536), g.f_qo.at[lo])
     for by in (1, 2, 3):
         src = near(1, 4 - by)[1]
         pltpu.make_async_remote_copy(
@@ -796,8 +800,8 @@
             def _():
                 g.e_own[...] = eb
                 g.du_own[...] = du
-                g.da_own[...] = da
-                g.dqkv_own[...] = dqkv
+                g.dqo_own[:, 0 : 3 * D] = dqkv
+                g.dqo_own[64:80, 3 * D : FF] = da
                 g.dxm_own[...] = dxm.astype(BF)
                 total = {}
                 b0, b1 = g.xh1[0:32, :], g.xh1[128:160, :]
@@ -824,78 +828,83 @@
     g.c_du[0:16, :] = g.du_own[:, pl.ds(pl.multiple_of(core * 1536, 128), 1536)]
     c_e_go = to_sibling(9, g.c_e.at[mini_lo], g.c_e.at[mini_hi])
     c_du_go = to_sibling(10, half(g.du_own, 1 - core, 1536), g.c_du.at[mini_hi])
+    c_qo_go = to_sibling(8, half(g.dqo_own, 1 - core, 1536), g.c_qo)
     top = [slice(128 * q, 128 * q + TOP) for q in range(2)]
+
+    def merge(first, own, cols, q, spread):
+        rows = slice(first + 128 * q, first + 128 * q + TOP)
+        base = jnp.concatenate([own[32 * q : 32 * q + 32, cols].astype(F32), jnp.zeros((16, 1536), F32)], 0)
+        g.f_qo[rows, :] = (g.f_qo[rows, :].astype(F32) + mm(spread, own[64:80, cols]) + base).astype(BF)
+
+    dq_local.wait()
     for q in range(2):
-        g.da[top[q], :] = (g.da[top[q], :].astype(F32) + mm(place[q], g.da_own[...])).astype(BF)
-        base = jnp.concatenate([g.dqkv_own[32 * q : 32 * q + 32, :].astype(F32), jnp.zeros((16, 3 * D), F32)], 0)
-        g.dqkv[top[q], :] = (g.dqkv[top[q], :].astype(F32) + mm(place[q], g.dqkv_own[64:80, :]) + base).astype(BF)
-    dq_go = to_sibling(6, half(g.dqo, 1 - core, 1536), g.f_qo.at[hi])
-    dq_local = local(4, half(g.dqo, core, 1536), g.f_qo.at[lo])
+        merge(0, g.dqo_own, pl.ds(pl.multiple_of(core * 1536, 128), 1536), q, place[q])
     c_e_go.wait_recv()
     c_du_go.wait_recv()
     each(send_right)
+    for c in (dq_go, c_qo_go, n1_go, o_go, spread_go):
+        c.wait_recv()
+    for q in range(2):
+        merge(256, g.c_qo, slice(None), q, g.spread[1, q])
+    left = mm_tn(g.f_n1[...], g.f_qo[:, 0:768]).astype(BF)
+    g.w1_2[0] = left[:, 0:512]
+    g.w1_2[1, :, 0:256] = left[:, 512:768]
+
+    def right(factor):
+        v = mm_tn(factor[...], g.f_qo[:, 768:1536]).astype(BF)
+        g.w1_2[1, :, 256:512] = v[:, 0:256]
+        g.w1_2[2] = v[:, 256:768]
+
+    @pl.when(core == 0)
+    def _():
+        right(g.f_n1)
+
+    @pl.when(core == 1)
+    def _():
+        right(g.f_o)
+
+    each(ring_a)
+    step(0, sum_first, rs2a)
+    step(1, sum_first, rs2a)
     g.small_out_v[0] = g.sums[...]
     small_send(0)
-    own_b(0)
+    each(ring_b)
     later = (me > 0).astype(F32)
     for q, s in ((0, s0), (1, s1)):
         dx = g.dx[top[q], :] + mm(place[q], g.dxm_own[...])
         dx = dx + jnp.concatenate([g.dxb_own[32 * q : 32 * q + 32, :], jnp.zeros((16, D), F32)], 0)
         dx = dx * (1.0 - later * is_slot(s, TOP).astype(F32))
         g.dx[top[q], :] = dx
-    dq_local.wait()
-    for c in (dq_go, n1_go, o_go):
-        c.wait_recv()
-    left = mm_tn(g.f_n1[...], g.f_qo[:, 0:768]).astype(BF)
-    g.w1_2[0] = left[:, 0:512]
-    g.w1_2[1, :, 0:256] = left[:, 512:768]
-
-    def right(factor):
-        v = mm_tn(factor[...], g.f_qo[:, 768:1536]).astype(BF)
-        g.w1_2[1, :, 256:512] = v[:, 0:256]
-        g.w1_2[2] = v[:, 256:768]
-
-    @pl.when(core == 0)
-    def _():
-        right(g.f_n1)
-
-    @pl.when(core == 1)
-    def _():
-        right(g.f_o)
-
-    each(ring_a)
+    own_a(1)
+    own_b(0)
+    step(0, rs2b, rs3a)
+    step(1, rs2b, rs3a)
     small_take(0)
     small_send(1)
-    step(0, sum_first, rs2a)
-    step(1, sum_first, rs2a)
-    own_a(1)
-    each(ring_b)
-    step(0, rs2b, rs3a)
-    step(1, rs2b, rs3a)
-    small_take(1)
-    small_send(2)
     each(ring_c)
     step(2, rs2a)
     step(0, rs3b)
     step(1, rs3b)
+    small_take(1)
+    small_send(2)
+    step(2, rs2b, rs3a)
+    step(0, ag3b, ag2a)
+    step(1, ag3b, ag2a)
     own_b(1)
-    step(0, ag3b, ag2a)
-    step(2, rs2b, rs3a)
-    step(1, ag3b, ag2a)
+    step(2, rs3b)
+    step(0, ag2b, ag1a)
     small_take(2)
     small_send(3)
-    step(2, rs3b)
-    step(0, ag2b, ag1a)
     step(2, ag3b, ag2a)
     step(1, ag2b, ag1a)
+    step(0, ag1b)
+    step(2, ag2b, ag1a)
+    step(1, ag1b)
+    step(0, ag1c)
     small_take(3)
     small_out[...] = g.small_out_v[4]
     own_c(0)
     own_c(1)
-    step(0, ag1b)
-    step(2, ag2b, ag1a)
-    step(1, ag1b)
-    step(0, ag1c)
     step(1, ag1c)
     step(2, ag1b)
     step(2, ag1c)
@@ -927,7 +936,7 @@
         in_specs=[smem, smem] + [hbm] * (len(args) - 2),
         out_specs=[vmem] * 6,
         scratch_shapes=[pltpu.VMEM(s, t) for s, t in SCRATCH.values()]
-        + [dma((21,)), dma((11,)), dma((11,)), dma((9, NMSG)), dma((9, NMSG)), dma((25,)), dma((25,))],
+        + [dma((21,)), dma((13,)), dma((13,)), dma((9, NMSG)), dma((9, NMSG)), dma((25,)), dma((25,))],
         compiler_params=pltpu.CompilerParams(
             collective_id=0, has_side_effects=True, vmem_limit_bytes=VMEM_LIMIT
         ),

time: 144 us -> 143 us (level)
  no operation moved by 1% of the time
where the time goes in v5:
time: 143 us
  Pallas kernels  142 us (99%)
    pallas_call x1, Pallas kernels, passes(): pl.pallas_call(kernel, out_shape=[pltpu.VMEM((ROWS, D), BF), pltpu.VMEM((...  132 us
    pallas_call x1, Pallas kernels, widen(): pl.pallas_call(widen_kernel, in_specs=[vmem] * 6, out_specs=[hbm] * 14, o...  9.85 us

profile of v5, /device:TPU:1, one launch (start us, length us, event | category | flops | bytes accessed | tf_op | source)
XLA Modules:
  0.0 142.6 jit_solution(13703604127302295841)
XLA Ops:
  0.7 131.9 %passes.1 = (bf16[256,768]{1,0:T(8,128)(2,1)S(1)}, bf16[256,768]{1,0:T(8,128)(2,1)S(1)}, f32[16,768]{1,0:T(8,128)S(1)}, bf16[768,3072]{1,0:T(8,128)(2,1)S(1)}, b...) custom-call(s32[2]{0:T(128)} %start_ref.1, s32[2]{0:T(128)} %length_ref.1, bf16[256,768]{1,0:T(8,128)(2,1)} %bitcast.4, ...), custom_call_target="tpu_custom_call" | custom-call | tf_op jit(solution)/shard_map/passes/pallas_call | solution.py:926
  132.5 9.9 %widen.1 = (bf16[256,768]{1,0:T(8,128)(2,1)}, bf16[256,768]{1,0:T(8,128)(2,1)}, f32[768,2304]{1,0:T(8,128)}, f32[768,768]{1,0:T(8,128)}, f32[768,3072]{1,0:T(8,1...) custom-call(bf16[256,768]{1,0:T(8,128)(2,1)S(1)} %get-tuple-element., ...), custom_call_target="tpu_custom_call" | custom-call | tf_op jit(solution)/shard_map/widen/pallas_call | solution.py:992

commit v6 on v5

--- a/solution.py
+++ b/solution.py
@@ -210,14 +210,14 @@
         c.wait()
 
     def norm_one(i, _):
-        rows = pl.ds(pl.multiple_of(i * 32, 32), 32)
+        rows = pl.ds(pl.multiple_of(i * 64, 64), 64)
         xhat, rs = normalise(g.x_v[rows, :].astype(F32))
         g.xh1[rows, :] = xhat
         g.rs1[rows, :] = rs
         g.f_n1[rows, :] = (xhat * row(LN1G) + row(LN1S)).astype(BF)
         return 0
 
-    lax.fori_loop(0, 8, norm_one, 0)
+    lax.fori_loop(0, 4, norm_one, 0)
     wq_load.wait()
     qkv_bias = (row(BQV), jnp.zeros((1, D), F32), row(BQV + 1))
     for k in range(3):
@@ -316,7 +316,7 @@
     g.tmp[...] = mm(g.f_o[0:256, :], g.wo[...])
 
     def norm_two(i, _):
-        rows = pl.ds(pl.multiple_of(i * 32, 32), 32)
+        rows = pl.ds(pl.multiple_of(i * 64, 64), 64)
         res = g.x_v[rows, :].astype(F32) + g.tmp[rows, :] + row(BOUT)
         g.res[rows, :] = res
         xhat, rs = normalise(res)
@@ -325,7 +325,7 @@
         g.f_n2[rows, :] = (xhat * row(LN2G) + row(LN2S)).astype(BF)
         return 0
 
-    lax.fori_loop(0, 8, norm_two, 0)
+    lax.fori_loop(0, 4, norm_two, 0)
     for k in range(4):
         c = slice(k * D, (k + 1) * D)
         m, slope = gelu_both(mm(g.f_n2[0:256, :], g.wu[:, c]) + row(BUP + k))
@@ -680,7 +680,7 @@
     zero8 = jnp.zeros((8, D), F32)
 
     def back_two(i, acc):
-        rows = pl.ds(pl.multiple_of(i * 32, 32), 32)
+        rows = pl.ds(pl.multiple_of(i * 64, 64), 64)
         dn = g.tmp[rows, :]
         xhat = g.xh2[rows, :]
         dres = g.cot_v[rows, :].astype(F32) + normalise_back(dn, row(LN2G), xhat, g.rs2[rows, :])
@@ -689,7 +689,7 @@
         g.da[rows, :] = da
         return acc[0] + eights(dn * xhat), acc[1] + eights(dn), acc[2] + eights(da.astype(F32))
 
-    acc = lax.fori_loop(0, 8, back_two, (zero8, zero8, zero8))
+    acc = lax.fori_loop(0, 4, back_two, (zero8, zero8, zero8))
     for i, a in zip((LN2G, LN2S, BOUT), acc):
         g.sums[i : i + 1, :] = jnp.sum(a, 0, keepdims=True)
     g.dmix[...] = mm_nt(g.da[...], g.wo[...]).astype(BF)
@@ -713,7 +713,7 @@
     g.dn1[...] = mm_nt(g.dqkv[...], g.wq[...])
 
     def back_one(i, acc):
-        rows = pl.ds(pl.multiple_of(i * 32, 32), 32)
+        rows = pl.ds(pl.multiple_of(i * 64, 64), 64)
         dn = g.dn1[rows, :]
         xhat = g.xh1[rows, :]
         g.dx[rows, :] = g.dres[rows, :] + normalise_back(dn, row(LN1G), xhat, g.rs1[rows, :])
@@ -721,7 +721,7 @@
         dv = eights(g.dqkv[rows, 2 * D : 3 * D].astype(F32))
         return acc[0] + eights(dn * xhat), acc[1] + eights(dn), acc[2] + dq, acc[3] + dv
 
-    acc = lax.fori_loop(0, 8, back_one, (zero8, zero8, zero8, zero8))
+    acc = lax.fori_loop(0, 4, back_one, (zero8, zero8, zero8, zero8))
     for i, a in zip((LN1G, LN1S, BQV, BQV + 1), acc):
         g.sums[i : i + 1, :] = jnp.sum(a, 0, keepdims=True)
 

time: 143 us -> 141 us (0.986)
  Pallas kernels: 142 us -> 140 us
    pallas_call x1, Pallas kernels: 132 us -> 130 us  [passes(): pl.pallas_call(kernel, out_shape=[pltpu.VMEM((ROWS, D), BF), pltpu.VMEM((...]
where the time goes in v6:
time: 141 us
  Pallas kernels  140 us (99%)
    pallas_call x1, Pallas kernels, passes(): pl.pallas_call(kernel, out_shape=[pltpu.VMEM((ROWS, D), BF), pltpu.VMEM((...  130 us
    pallas_call x1, Pallas kernels, widen(): pl.pallas_call(widen_kernel, in_specs=[vmem] * 6, out_specs=[hbm] * 14, o...  9.85 us

profile of v6, /device:TPU:1, one launch (start us, length us, event | category | flops | bytes accessed | tf_op | source)
XLA Modules:
  0.0 141.1 jit_solution(10024381018951534123)
XLA Ops:
  0.7 130.4 %passes.1 = (bf16[256,768]{1,0:T(8,128)(2,1)S(1)}, bf16[256,768]{1,0:T(8,128)(2,1)S(1)}, f32[16,768]{1,0:T(8,128)S(1)}, bf16[768,3072]{1,0:T(8,128)(2,1)S(1)}, b...) custom-call(s32[2]{0:T(128)} %start_ref.1, s32[2]{0:T(128)} %length_ref.1, bf16[256,768]{1,0:T(8,128)(2,1)} %bitcast.4, ...), custom_call_target="tpu_custom_call" | custom-call | tf_op jit(solution)/shard_map/passes/pallas_call | solution.py:926
  131.1 9.9 %widen.1 = (bf16[256,768]{1,0:T(8,128)(2,1)}, bf16[256,768]{1,0:T(8,128)(2,1)}, f32[768,2304]{1,0:T(8,128)}, f32[768,768]{1,0:T(8,128)}, f32[768,3072]{1,0:T(8,1...) custom-call(bf16[256,768]{1,0:T(8,128)(2,1)S(1)} %get-tuple-element., ...), custom_call_target="tpu_custom_call" | custom-call | tf_op jit(solution)/shard_map/widen/pallas_call | solution.py:992
